TPU v7x, 256 devices: a whole 4x4x8 slice. The times are simulated.
256 devices in a mesh: grp: 4 (over z_hi), seq: 16 (over z_lo, y, core), dp: 4 (over x).
Axes of the slice: x: 4, y: 4, z: 8 (z_hi: 4, z_lo: 2; z = z_hi * 2 + z_lo), core: 2. Of those that a mesh axis runs over, the one named last changes fastest.
Arguments:
- image_hidden: bfloat16 [8, 4, 512, 3072], P('grp', 'dp', 'seq'), may hold values from -6 to 6
- control_hidden: bfloat16 [8, 4, 512, 3072], P(None, 'dp', 'seq', 'grp'), may hold values from -6 to 6
- text_qkv: bfloat16 [3, 8, 4, 512, 2048], P(None, 'grp', 'dp', 'seq')
- text_lengths: int32 [8, 4], P('grp', 'dp'), may hold values from 64 to 512, as said below
- timesteps: int32 [8, 4], P('grp', 'dp'), may hold values from 0 to 999
- mod_weight: bfloat16 [256, 6144], replicated, may hold values from -0.375 to 0.375
- qkv_weight: bfloat16 [3072, 3, 2048], P('dp', None, 'seq'), may hold values from -0.078125 to 0.078125
- zero_weight: bfloat16 [3072, 3072], P('grp'), may hold values from -0.109375 to 0.109375
- image_cotangent: bfloat16 [8, 4, 512, 2048], P('grp', 'dp', 'seq'), may hold values from -6 to 6
- text_cotangent: bfloat16 [8, 4, 512, 2048], P('grp', 'dp', 'seq'), may hold values from -6 to 6
Outputs:
- image_attn: bfloat16 [8, 4, 512, 2048], P('grp', 'dp', 'seq')
- text_attn: bfloat16 [8, 4, 512, 2048], P('grp', 'dp', 'seq')
- control_grad: bfloat16 [8, 4, 512, 3072], P(None, 'dp', 'seq', 'grp')
- zero_grad: float32 [3072, 3072], P('grp', 'seq')
Inputs may be any that keep to these rules, and one draw needn't show every extreme that they name: `text_lengths`: text positions at or beyond a sample's length are padding.
All inputs are finite; a program needn't handle non-finite values.
Results may differ from a plain program's by a relative error of at most 0.029.
Values may be sent and summed in bfloat16 or wider, within the bound.
A program may use at most 128 MiB of HBM per device.

v0:
```python
import math

import jax
import jax.numpy as jnp
from jax import lax
from jax.sharding import PartitionSpec as P

D = 3072
HEADS = 16
HD = 128
IMG = 512
TXT = 512
FREQ = 256


def timestep_modulation(timesteps, mod_weight):
    half_freq = FREQ // 2
    frequency = jnp.exp(-math.log(10000.0) * jnp.arange(half_freq, dtype=jnp.float32) / half_freq)
    angles = timesteps.astype(jnp.float32)[..., None] * frequency
    embedding = jnp.concatenate([jnp.cos(angles), jnp.sin(angles)], axis=-1)
    activated = jax.nn.silu(embedding).astype(jnp.bfloat16)
    return jnp.dot(activated.reshape(-1, FREQ), mod_weight, preferred_element_type=jnp.float32)


def normalize(rows):
    values = rows.astype(jnp.float32)
    average = jnp.mean(values, axis=-1, keepdims=True)
    centred = values - average
    reciprocal = lax.rsqrt(jnp.mean(centred * centred, axis=-1, keepdims=True) + 1e-06)
    return (centred * reciprocal, reciprocal)


def head_pass(query, key_rows, value_rows, cotangent, live_keys, first_row):
    scaling = query.shape[-1] ** (-0.5)
    dims = (((0,), (0,)), ((), ()))
    scores = jnp.dot(query, key_rows.T, preferred_element_type=jnp.float32) * scaling
    scores = jnp.where(live_keys[None, :], scores, -jnp.inf)
    row_max = jnp.max(scores, axis=1, keepdims=True)
    exp_terms = jnp.exp(scores - row_max)
    prob_rows = exp_terms / jnp.sum(exp_terms, axis=1, keepdims=True)
    prob_low = prob_rows.astype(jnp.bfloat16)
    attended = jnp.dot(prob_low, value_rows, preferred_element_type=jnp.float32).astype(
        jnp.bfloat16
    )
    row_dots = jnp.sum(
        cotangent.astype(jnp.float32) * attended.astype(jnp.float32), axis=1, keepdims=True
    )
    prob_grad = jnp.dot(cotangent, value_rows.T, preferred_element_type=jnp.float32)
    score_grad = (prob_rows * (prob_grad - row_dots)).astype(jnp.bfloat16)
    query_grad = (
        jnp.dot(score_grad[first_row:], key_rows, preferred_element_type=jnp.float32) * scaling
    ).astype(jnp.bfloat16)
    key_grad = (
        lax.dot_general(score_grad[:, first_row:], query, dims, preferred_element_type=jnp.float32)
        * scaling
    ).astype(jnp.bfloat16)
    value_grad = lax.dot_general(
        prob_low[:, first_row:], cotangent, dims, preferred_element_type=jnp.float32
    ).astype(jnp.bfloat16)
    return (attended, query_grad, key_grad, value_grad)


def body(
    image_hidden,
    control_hidden,
    text_qkv,
    text_lengths,
    timesteps,
    mod_weight,
    qkv_weight,
    zero_weight,
    image_cotangent,
    text_cotangent,
):
    sample_count = image_hidden.shape[0]
    local_tokens = image_hidden.shape[2]
    text_local = text_qkv.shape[3]
    head_local = HEADS // lax.axis_size("seq")
    joint_len = TXT + IMG
    modulation = timestep_modulation(timesteps, mod_weight).reshape(sample_count, 1, 1, 2 * D)
    offset = modulation[..., :D]
    stretch = 1.0 + modulation[..., D:]
    selected = control_hidden
    residual = lax.psum_scatter(
        jnp.einsum("abtf,fe->abte", selected, zero_weight, preferred_element_type=jnp.float32),
        "grp",
        scatter_dimension=0,
        tiled=True,
    )
    hidden = (image_hidden.astype(jnp.float32) + residual).astype(jnp.bfloat16)
    gathered = lax.all_gather(hidden, "seq", axis=2, tiled=True)
    standard_all, _ = normalize(gathered)
    normed = (standard_all * stretch + offset).astype(jnp.bfloat16)
    weight_full = lax.all_gather(qkv_weight, "dp", axis=0, tiled=True)
    image_qkv = jnp.einsum(
        "abtd,dcq->abtcq", normed, weight_full, preferred_element_type=jnp.float32
    ).astype(jnp.bfloat16)
    text_send = text_qkv.reshape(3, sample_count, 1, text_local, HEADS, HD)
    text_grad_send = text_cotangent.reshape(1, sample_count, 1, text_local, HEADS, HD)
    image_grad_send = image_cotangent.reshape(1, sample_count, 1, local_tokens, HEADS, HD)
    text_heads, text_grad_heads, image_grad_heads = (
        lax.all_to_all(text_send, "seq", split_axis=4, concat_axis=3, tiled=True),
        lax.all_to_all(text_grad_send, "seq", split_axis=4, concat_axis=3, tiled=True),
        lax.all_to_all(image_grad_send, "seq", split_axis=4, concat_axis=3, tiled=True),
    )
    image_heads = jnp.transpose(
        image_qkv.reshape(sample_count, IMG, 3, head_local, HD), (2, 0, 3, 1, 4)
    )
    text_part = jnp.transpose(
        text_heads.reshape(3, sample_count, TXT, head_local, HD), (0, 1, 3, 2, 4)
    )
    joint = jnp.concatenate([text_part, image_heads], axis=3).reshape(
        3, sample_count * head_local, joint_len, HD
    )
    cotangent = jnp.concatenate(
        [
            text_grad_heads.reshape(sample_count, TXT, head_local, HD),
            image_grad_heads.reshape(sample_count, IMG, head_local, HD),
        ],
        axis=1,
    )
    cotangent = jnp.transpose(cotangent, (0, 2, 1, 3)).reshape(
        sample_count * head_local, joint_len, HD
    )
    position = jnp.arange(joint_len)
    live_keys = (position[None, :] >= TXT) | (position[None, :] < text_lengths)
    live_keys = jnp.repeat(live_keys, head_local, axis=0)
    attended, query_grad, key_grad, value_grad = lax.map(
        lambda item_args: head_pass(*item_args, TXT),
        (joint[0], joint[1], joint[2], cotangent, live_keys),
    )
    attended = jnp.transpose(
        attended.reshape(sample_count, head_local, joint_len, HD), (0, 2, 1, 3)
    )
    text_out = attended[:, :TXT].reshape(1, sample_count, 1, TXT, head_local, HD)
    image_out = attended[:, TXT:].reshape(1, sample_count, 1, IMG, head_local, HD)
    text_back, image_back = (
        lax.all_to_all(text_out, "seq", split_axis=3, concat_axis=4, tiled=True),
        lax.all_to_all(image_out, "seq", split_axis=3, concat_axis=4, tiled=True),
    )
    text_attn = text_back.reshape(sample_count, 1, text_local, HEADS * HD)
    image_attn = image_back.reshape(sample_count, 1, local_tokens, HEADS * HD)
    image_grads = jnp.stack([query_grad, key_grad, value_grad]).reshape(
        3, sample_count, head_local, IMG, HD
    )
    image_grads = jnp.transpose(image_grads, (3, 1, 0, 2, 4)).reshape(
        IMG, sample_count, 3, head_local * HD
    )
    selected = image_grads
    normed_grad = lax.psum_scatter(
        jnp.einsum(
            "tscq,dcq->tsd", selected, weight_full, preferred_element_type=jnp.float32
        ).astype(jnp.bfloat16),
        "seq",
        scatter_dimension=0,
        tiled=True,
    ).astype(jnp.float32)
    normed_grad = jnp.transpose(normed_grad, (1, 0, 2))[:, None]
    standard, reciprocal = normalize(hidden)
    scaled_grad = normed_grad * stretch
    residual_grad = (
        reciprocal
        * (
            scaled_grad
            - jnp.mean(scaled_grad, axis=-1, keepdims=True)
            - standard * jnp.mean(scaled_grad * standard, axis=-1, keepdims=True)
        )
    ).astype(jnp.bfloat16)
    grad_rows = lax.all_gather(residual_grad, "grp", axis=0, tiled=True)
    control_grad = jnp.einsum(
        "abte,fe->abtf", grad_rows, zero_weight, preferred_element_type=jnp.float32
    ).astype(jnp.bfloat16)
    norm_factor = (control_hidden.shape[0] * lax.axis_size("dp") * IMG) ** (-0.5)
    full_terms = jnp.einsum(
        "abtf,abte->fe", control_hidden, grad_rows, preferred_element_type=jnp.float32
    )
    zero_part = lax.psum_scatter(full_terms, "seq", scatter_dimension=1, tiled=True)
    zero_grad = lax.psum(zero_part, "dp") * norm_factor
    return (image_attn, text_attn, control_grad, zero_grad)


def solution(mesh):
    placed = (
        P("grp", "dp", "seq", None),
        P(None, "dp", "seq", "grp"),
        P(None, "grp", "dp", "seq", None),
        P("grp", "dp"),
        P("grp", "dp"),
        P(),
        P("dp", None, "seq"),
        P("grp", None),
        P("grp", "dp", "seq", None),
        P("grp", "dp", "seq", None),
    )
    return jax.shard_map(
        body,
        mesh=mesh,
        in_specs=placed,
        out_specs=(
            P("grp", "dp", "seq", None),
            P("grp", "dp", "seq", None),
            P(None, "dp", "seq", "grp"),
            P("grp", "seq"),
        ),
        check_vma=False,
    )
```

profile of v0, /device:TPU:32, one launch (start us, length us, event | category | flops | bytes accessed | tf_op | source)
XLA Modules:
  0.0 483.4 jit_solution(425698475610706914)
XLA Ops:
  7.2 5.7 %fusion.48 = f32[8,1,32,3072]{3,2,0,1:T(8,128)} fusion(bf16[768,3072]{1,0:T(8,128)(2,1)} %param.19, bf16[8,1,32,768]{3,2,1,0:T(8,128)(2,1)} %param.13), kind=kOutput, calls=%fused_computation.63 | convolution fusion | flops 1207959552 | bytes 8257536 | tf_op jit(solution)/shard_map/abtf,fe->abte/dot_general | solution.py:85
  13.0 68.9 %reduce-scatter.4.cloned.1.call-done = f32[2,1,32,3072]{3,2,0,1:T(8,128)} async-done(((f32[8,1,32,3072]{3,2,0,1:T(8,128)}), f32[2,1,32,3072]{3,2,0,1:T(8,128)}) %reduce-scatter.4.cloned.1.call-update) | async-done | bytes 786448 | tf_op jit(solution)/shard_map/reduce_scatter | solution.py:84
  82.0 2.0 convert_reduce_fusion.1
  84.0 1.0 copy.83
  85.0 0.8 copy.64
  85.8 6.2 %all-to-all-start.2 = ((bf16[1,2,1,32,16,128]{5,3,1,2,0,4:T(8,128)(2,1)}), bf16[1,2,1,32,16,128]{5,3,1,2,0,4:T(8,128)(2,1)S(1)}, u32[]{:S(2)}, u32[]{:S(2)}) async-start(bf16[1,2,1,32,16,128]{5,3,1,2,0,4:T(8,128)(2,1)} %copy.64), calls=%async_computation.3 | async-start | bytes 524288 | tf_op jit(solution)/shard_map/all_to_all | solution.py:104
  92.0 0.7 all-gather.6.cloned.1.call-update
  92.7 1.0 copy.82
  93.7 0.8 copy.62
  94.5 4.3 all-to-all-done.2
  98.8 5.3 %all-to-all-start.1 = ((bf16[1,2,1,32,16,128]{5,3,1,2,0,4:T(8,128)(2,1)}), bf16[1,2,1,32,16,128]{5,3,1,2,0,4:T(8,128)(2,1)}, u32[]{:S(2)}, u32[]{:S(2)}) async-start(bf16[1,2,1,32,16,128]{5,3,1,2,0,4:T(8,128)(2,1)} %copy.62), calls=%async_computation.2 | async-start | bytes 524288 | tf_op jit(solution)/shard_map/all_to_all | solution.py:103
  104.1 1.3 copy.81
  105.4 1.1 copy.59
  106.6 7.4 %all-to-all-done.1 = bf16[1,2,1,32,16,128]{5,3,1,2,0,4:T(8,128)(2,1)} async-done(((bf16[1,2,1,32,16,128]{5,3,1,2,0,4:T(8,128)(2,1)}), bf16[1,2,1,32,16,128]{5,3,1,2,0,4:T(8,128)(2,1)}, u32[]{:S(2)}, u32[]{:S(2)}) %all-to-all-start.1) | async-done | bytes 262176 | tf_op jit(solution)/shard_map/all_to_all | solution.py:103
  114.0 5.6 %all-to-all-start = ((bf16[3,2,1,32,16,128]{5,3,0,1,2,4:T(8,128)(2,1)}), bf16[3,2,1,32,16,128]{5,3,0,1,2,4:T(8,128)(2,1)}, u32[]{:S(2)}, u32[]{:S(2)}) async-start(bf16[3,2,1,32,16,128]{5,3,0,1,2,4:T(8,128)(2,1)} %copy.59), calls=%async_computation | async-start | bytes 1572864 | tf_op jit(solution)/shard_map/all_to_all | solution.py:102
  119.8 0.5 convolution_bitcast_fusion
  120.4 1.0 copy.63
  121.4 0.9 maximum_bitcast_fusion.2
  122.2 17.2 %all-to-all-done = bf16[3,2,1,32,16,128]{5,3,0,1,2,4:T(8,128)(2,1)} async-done(((bf16[3,2,1,32,16,128]{5,3,0,1,2,4:T(8,128)(2,1)}), bf16[3,2,1,32,16,128]{5,3,0,1,2,4:T(8,128)(2,1)}, u32[]{:S(2)}, u32[]{:S(2)}) %all-to-all-start) | async-done | bytes 786464 | tf_op jit(solution)/shard_map/all_to_all | solution.py:102
  139.5 2.1 copy.60
  141.6 3.8 convert_reduce_fusion
  145.4 0.8 copy-done.1
  146.2 1.8 fusion.37
  148.0 30.4 %all-gather.6.cloned.1.call-done = bf16[3072,3,128]{2,0,1:T(8,128)(2,1)} async-done(((bf16[768,3,128]{2,0,1:T(8,128)(2,1)}), bf16[3072,3,128]{2,0,1:T(8,128)(2,1)}) %all-gather.6.cloned.1.call-update) | async-done | bytes 2359312 | tf_op jit(solution)/shard_map/all_gather | solution.py:94
  178.4 7.0 %fusion.60 = bf16[3,2,1,512,128]{4,3,0,1,2:T(8,128)(2,1)S(1)} fusion(bf16[3072,3,128]{2,0,1:T(8,128)(2,1)} %all-gather.6.cloned.1.call-done, bf16[2,1,512,3072]{3,2,0,1:T(8,128)(2,1)} %all-gather.4.cloned.1.call-done, f32[2,3072]{1,0:T(2,128)S(1)} %get-tuple-element.155, f32[2,3072]{1,0:T(2,128)S(1)} %get-tuple-element.154, ...), kind=kOutput, calls=%fused_computation.73 | convolution fusion | flops 2435186688 | bytes 9494528 | tf_op jit(solution)/shard_map/abtd,dcq->abtcq/dot_general | solution.py:95
  185.4 1.2 fusion.92
  186.6 23.8 %while.16 = (s32[]{:T(128)}, bf16[2,1024,128]{1,2,0:T(8,128)(2,1)}, bf16[2,512,128]{2,1,0:T(8,128)(2,1)}, bf16[2,512,128]{2,1,0:T(8,128)(2,1)}, bf16[2,512,128]{...) while((s32[]{:T(128)}, bf16[2,1024,128]{1,2,0:T(8,128)(2,1)}, ...), condition=%wide.region_7.8_spmd, body=%wide.region_3.7_spmd.sunk | while | flops 1228862464 | bytes 49725900 | solution.py:128
  186.7 1.7 constant_dynamic-slice_fusion.4
  188.3 1.1 copy.85
  189.4 1.8 fusion.129
  191.2 0.9 fusion.130
  192.1 1.4 fusion.131
  194.8 1.7 multiply_convert_fusion.2
  197.1 0.6 fusion.132
  197.8 0.7 copy-done.19
  198.6 1.7 constant_dynamic-slice_fusion.4
  200.2 1.1 copy.85
  201.3 1.8 fusion.129
  203.1 0.9 fusion.130
  204.0 1.4 fusion.131
  205.5 0.5 fusion.134
  206.7 1.7 multiply_convert_fusion.2
  209.0 0.6 fusion.132
  209.7 0.7 copy-done.19
  210.4 8.0 %bitcast_convert_fusion = bf16[512,2,3072]{2,0,1:T(8,128)(2,1)} fusion(bf16[3072,3,128]{2,0,1:T(8,128)(2,1)} %all-gather.6.cloned.1.call-done, bf16[1,2,512,128]{3,2,0,1:T(8,128)(2,1)} %bitcast.250, bf16[1,2,512,128]{3,2,0,1:T(8,128)(2,1)} %bitcast.251, bf16[1,2,512,128]{3,2,0,1:T(8,128)(2,1)} %bitcast.252), kind=kOutput, calls=%fused_computation.54 | convolution fusion | flops 2419851264 | bytes 9437184 | tf_op jit(solution)/shard_map/tscq,dcq->tsd/dot_general | solution.py:151
  218.6 0.9 copy-done.2
  219.7 71.3 %reduce-scatter.6.cloned.1.call-done = bf16[32,2,3072]{2,0,1:T(8,128)(2,1)} async-done(((bf16[512,2,3072]{2,0,1:T(8,128)(2,1)}), bf16[32,2,3072]{2,0,1:T(8,128)(2,1)}) %reduce-scatter.6.cloned.1.call-update) | async-done | bytes 393232 | tf_op jit(solution)/shard_map/reduce_scatter | solution.py:150
  291.0 1.2 bitcast_reduce_fusion
  292.2 1.3 fusion.79
  293.5 2.0 fusion.93
  295.6 39.1 %all-gather.8.cloned.1.call-done = bf16[8,1,32,3072]{3,2,1,0:T(8,128)(2,1)} async-done(((bf16[2,1,32,3072]{3,2,1,0:T(8,128)(2,1)}), bf16[8,1,32,3072]{3,2,1,0:T(8,128)(2,1)}) %all-gather.8.cloned.1.call-update) | async-done | bytes 1572880 | tf_op jit(solution)/shard_map/all_gather | solution.py:169
  334.7 6.6 %convolution_bitcast_fusion.1 = f32[768,3072]{0,1:T(8,128)} fusion(bf16[8,1,32,3072]{3,2,1,0:T(8,128)(2,1)} %all-gather.8.cloned.1.call-done, bf16[8,1,32,768]{3,2,1,0:T(8,128)(2,1)} %param.13), kind=kOutput, calls=%fused_computation.58 | convolution fusion | flops 1207959552 | bytes 11403264 | tf_op jit(solution)/shard_map/abtf,abte->fe/dot_general | solution.py:174
  341.3 2.0 copy.67
  343.3 2.1 slice_bitcast_fusion
  345.4 16.0 %all_to_all.75 = bf16[1,2,1,512,1,128]{5,1,4,2,0,3:T(2,128)(2,1)} all-to-all(bf16[1,2,1,512,1,128]{5,1,4,2,0,3:T(2,128)(2,1)S(1)} %get-tuple-element.152), channel_id=1, replica_groups=mesh['grp'=4,'seq'=16,'dp'=4] {'seq'}, dimensions={3} | all-to-all | bytes 524288 | tf_op jit(solution)/shard_map/all_to_all | solution.py:138
  361.4 4.8 all-to-all-start.3
  366.2 59.9 %reduce-scatter.8.cloned.1.call-done = f32[768,192]{0,1:T(8,128)} async-done(((f32[768,3072]{0,1:T(8,128)}), f32[768,192]{0,1:T(8,128)}) %reduce-scatter.8.cloned.1.call-update) | async-done | bytes 589840 | tf_op jit(solution)/shard_map/reduce_scatter | solution.py:177
  426.1 1.0 copy.71
  427.1 0.8 copy.72
  427.9 1.8 reshape.236
  429.8 0.8 reshape.234
  430.7 5.0 %fusion.70 = bf16[8,1,32,768]{3,2,1,0:T(8,128)(2,1)} fusion(bf16[768,3072]{1,0:T(8,128)(2,1)} %param.19, bf16[8,1,32,3072]{3,2,1,0:T(8,128)(2,1)} %all-gather.8.cloned.1.call-done), kind=kOutput, calls=%fused_computation.75 | convolution fusion | flops 1208156160 | bytes 6684672 | tf_op jit(solution)/shard_map/abte,fe->abtf/dot_general | solution.py:170
  435.6 39.0 %all-reduce.2.cloned.1.call-done = f32[768,192]{0,1:T(8,128)} async-done(((f32[768,192]{0,1:T(8,128)}), f32[768,192]{0,1:T(8,128)}) %all-reduce.2.cloned.1.call-update) | async-done | bytes 589840 | tf_op jit(solution)/shard_map/psum | solution.py:178
  474.7 1.9 broadcast_multiply_fusion
  (103 shorter events, 4.2 us)
Async XLA Ops:
  7.2 112.7 %copy-start = (bf16[256,6144]{1,0:T(8,128)(2,1)S(1)}, bf16[256,6144]{1,0:T(8,128)(2,1)}, u32[]{:S(2)}) copy-start(bf16[256,6144]{1,0:T(8,128)(2,1)} %param.17) | copy-start | bytes 9437188
  7.2 74.8 %copy-start.11 = (bf16[2,1,32,3072]{3,2,1,0:T(8,128)(2,1)S(1)}, bf16[2,1,32,3072]{3,2,1,0:T(8,128)(2,1)}, u32[]{:S(2)}) copy-start(bf16[2,1,32,3072]{3,2,1,0:T(8,128)(2,1)} %param.12) | copy-start | bytes 1179652
  7.2 74.8 %reduce-scatter.4.cloned.1.call-start = ((), (), s32[]{:S(2)}) async-start(), calls=%async_computation.8 | async-start | bytes 3932160 | tf_op jit(solution)/shard_map/reduce_scatter | solution.py:84
  12.9 93.6 %copy-start.13 = (s32[2,1]{0,1:T(1,128)S(1)}, s32[2,1]{0,1:T(1,128)}, u32[]{:S(2)}) copy-start(s32[2,1]{0,1:T(1,128)} %param.16) | copy-start | bytes 28
  13.0 128.6 %all-gather.4.cloned.1.call-start = ((), (), s32[]{:S(2)}) async-start(), calls=%async_computation.9 | async-start | bytes 6684672 | tf_op jit(solution)/shard_map/all_gather | solution.py:91
  84.0 35.8 %copy-start.12 = (s32[2,1]{0,1:T(1,128)S(1)}, s32[2,1]{0,1:T(1,128)}, u32[]{:S(2)}) copy-start(s32[2,1]{0,1:T(1,128)} %param.15) | copy-start | bytes 28
  85.8 13.0 %all-to-all-start.2 = ((bf16[1,2,1,32,16,128]{5,3,1,2,0,4:T(8,128)(2,1)}), bf16[1,2,1,32,16,128]{5,3,1,2,0,4:T(8,128)(2,1)S(1)}, u32[]{:S(2)}, u32[]{:S(2)}) async-start(bf16[1,2,1,32,16,128]{5,3,1,2,0,4:T(8,128)(2,1)} %copy.64), calls=%async_computation.3 | async-start | bytes 524288 | tf_op jit(solution)/shard_map/all_to_all | solution.py:104
  92.0 86.4 %all-gather.6.cloned.1.call-start = ((), (), s32[]{:S(2)}) async-start(), calls=%async_computation.10 | async-start | bytes 2949120 | tf_op jit(solution)/shard_map/all_gather | solution.py:94
  98.8 15.2 %all-to-all-start.1 = ((bf16[1,2,1,32,16,128]{5,3,1,2,0,4:T(8,128)(2,1)}), bf16[1,2,1,32,16,128]{5,3,1,2,0,4:T(8,128)(2,1)}, u32[]{:S(2)}, u32[]{:S(2)}) async-start(bf16[1,2,1,32,16,128]{5,3,1,2,0,4:T(8,128)(2,1)} %copy.62), calls=%async_computation.2 | async-start | bytes 524288 | tf_op jit(solution)/shard_map/all_to_all | solution.py:103
  114.0 25.5 %all-to-all-start = ((bf16[3,2,1,32,16,128]{5,3,0,1,2,4:T(8,128)(2,1)}), bf16[3,2,1,32,16,128]{5,3,0,1,2,4:T(8,128)(2,1)}, u32[]{:S(2)}, u32[]{:S(2)}) async-start(bf16[3,2,1,32,16,128]{5,3,0,1,2,4:T(8,128)(2,1)} %copy.59), calls=%async_computation | async-start | bytes 1572864 | tf_op jit(solution)/shard_map/all_to_all | solution.py:102
  119.6 171.5 %reduce-scatter.6.cloned.1.call-start = ((), (), s32[]{:S(2)}) async-start(), calls=%async_computation.11 | async-start | bytes 6684672 | tf_op jit(solution)/shard_map/reduce_scatter | solution.py:150
  120.4 58.0 %copy-start.10 = (f32[2,3072]{1,0:T(2,128)}, f32[2,3072]{1,0:T(2,128)S(1)}, u32[]{:S(2)}) copy-start(f32[2,3072]{1,0:T(2,128)S(1)} %get-tuple-element.154) | copy-start | bytes 73732
  141.6 4.6 copy-start.1
  178.4 7.0 %copy-start.7 = (bf16[3,2,1,16,32,1,128]{6,4,3,0,1,5,2:T(8,128)(2,1)S(1)}, bf16[3,2,1,16,32,1,128]{6,4,3,0,1,5,2:T(8,128)(2,1)}, u32[]{:S(2)}) copy-start(bf16[3,2,1,16,32,1,128]{6,4,3,0,1,5,2:T(8,128)(2,1)} %copy.60) | copy-start | bytes 2359300
  192.1 1.5 copy-start.3
  192.1 1.5 copy-start.14
  192.1 2.0 copy-start.4
  192.1 2.0 copy-start.8
  194.1 2.4 copy-start.15
  194.7 1.9 copy-start.9
  194.8 1.8 copy-start.5
  194.8 1.8 copy-start.16
  194.8 2.3 copy-start.6
  194.8 2.3 copy-start.18
  197.1 0.7 copy-start.17
  197.8 0.7 copy-start.19
  204.0 1.5 copy-start.3
  204.0 1.5 copy-start.14
  204.0 2.0 copy-start.4
  204.0 2.0 copy-start.8
  206.0 2.4 copy-start.15
  206.6 1.9 copy-start.9
  206.7 1.8 copy-start.5
  206.7 1.8 copy-start.16
  206.7 2.3 copy-start.6
  206.7 2.3 copy-start.18
  209.0 0.7 copy-start.17
  209.7 0.7 copy-start.19
  218.5 1.0 copy-start.2
  218.5 116.2 %all-gather.8.cloned.1.call-start = ((), (), s32[]{:S(2)}) async-start(), calls=%async_computation.12 | async-start | bytes 1966080 | tf_op jit(solution)/shard_map/all_gather | solution.py:169
  295.6 130.5 %reduce-scatter.8.cloned.1.call-start = ((), (), s32[]{:S(2)}) async-start(), calls=%async_computation.13 | async-start | bytes 10027008 | tf_op jit(solution)/shard_map/reduce_scatter | solution.py:177
  361.4 68.3 %all-to-all-start.3 = ((bf16[1,2,1,512,1,128]{5,1,4,2,0,3:T(2,128)(2,1)}), bf16[1,2,1,512,1,128]{5,1,4,2,0,3:T(2,128)(2,1)S(1)}, u32[]{:S(2)}, u32[]{:S(2)}) async-start(bf16[1,2,1,512,1,128]{5,1,4,2,0,3:T(2,128)(2,1)} %get-tuple-element.153), calls=%async_computation.4 | async-start | bytes 524288 | tf_op jit(solution)/shard_map/all_to_all | solution.py:139
  366.2 108.5 %all-reduce.2.cloned.1.call-start = ((), (), s32[]{:S(2)}) async-start(), calls=%async_computation.14 | async-start | bytes 1179648 | tf_op jit(solution)/shard_map/psum | solution.py:178
Sparse Core Ops, SparseCore 0:
  13.1 68.8 reduce-scatter.3
  84.3 55.6 all-gather.3
  141.8 36.4 all-gather.5
  218.6 72.3 reduce-scatter.5
  295.7 38.9 all-gather.7
  341.4 84.6 reduce-scatter.7
  428.4 46.1 all-reduce.1
where the time goes:
time: 485 us; the launch traced here: 483 us
  waiting for transfers between devices  338 us (70%)
  matrix products  44 us (9%)
  local copies, waits for them, and re-layouts  26.7 us (6%)
  starting transfers between devices  22.2 us (5%)
  other arithmetic  21.5 us (4%)
  blocking collectives  16 us (3%)
  between operations  14.3 us (3%)
    reduce_scatter x1, waiting for transfers between devices, body(): lax.psum_scatter(jnp.einsum('tscq,dcq->tsd', selected, weight_full, prefe...  71.3 us
    reduce_scatter x1, waiting for transfers between devices, body(): lax.psum_scatter(jnp.einsum('abtf,fe->abte', selected, zero_weight, prefe...  68.9 us
    reduce_scatter x1, waiting for transfers between devices, body(): lax.psum_scatter(full_terms, 'seq', scatter_dimension=1, tiled=True)  59.9 us
    all_gather x1, waiting for transfers between devices, body(): grad_rows = lax.all_gather(residual_grad, 'grp', axis=0, tiled=True)  39.1 us
    psum x1, waiting for transfers between devices, body(): zero_grad = lax.psum(zero_part, 'dp') * norm_factor  39 us
    all_gather x1, waiting for transfers between devices, body(): weight_full = lax.all_gather(qkv_weight, 'dp', axis=0, tiled=True)  30.4 us
    all_to_all x1, waiting for transfers between devices, body(): lax.all_to_all(text_send, 'seq', split_axis=4, concat_axis=3, tiled=True)  17.2 us
    all_to_all x1, blocking collectives, body(): lax.all_to_all(text_out, 'seq', split_axis=3, concat_axis=4, tiled=True)  16 us
  transfers between devices with their start and end apart: 11, of which 9 were waited for; matrix products, arithmetic and copies ran while one was open for 6% of the time, Pallas kernels for 0%

commit v1 on v0

v1 whole, which is shorter than its diff:
```python
import math

import jax
import jax.numpy as jnp
from jax import lax
from jax.experimental import pallas as pl
from jax.experimental.pallas import tpu as pltpu
from jax.sharding import PartitionSpec as P

D = 3072
HEADS = 16
HD = 128
IMG = 512
TXT = 512
FREQ = 256
ROWS = 32
HALF = D // 2
MESH = pl.DeviceIdType.MESH
BF = jnp.bfloat16
F32 = jnp.float32
VMEM_LIMIT = 60 * 1024 * 1024
ANY = pl.BlockSpec(memory_space=pl.ANY)
VMEM = pl.BlockSpec(memory_space=pltpu.VMEM)


class Sends:
    def __init__(self, sems):
        self.sems = sems
        self.copies = []

    def __call__(self, src, dst, recv, **to):
        copy = pltpu.make_async_remote_copy(
            src_ref=src,
            dst_ref=dst,
            send_sem=self.sems.at[len(self.copies)],
            recv_sem=recv,
            device_id=to,
            device_id_type=MESH,
        )
        copy.start()
        self.copies.append(copy)

    def drain(self):
        for copy in self.copies:
            copy.wait_send()


def arrived(dst, recv):
    pltpu.make_async_copy(dst, dst, recv).wait()


def greet(groups):
    barrier = pltpu.get_barrier_semaphore()
    for to in groups:
        pl.semaphore_signal(barrier, inc=1, device_id=to, device_id_type=MESH)
    pl.semaphore_wait(barrier, len(groups))


class Place:
    def __init__(self):
        self.s = lax.axis_index("seq")
        self.g = lax.axis_index("grp")
        self.d = lax.axis_index("dp")
        self.z = self.s // 8
        self.y = (self.s // 2) % 4
        self.c = self.s % 2
        self.zo = 1 - self.z
        self.co = 1 - self.c
        self.yl = (self.y + 3) % 4
        self.yr = (self.y + 1) % 4
        self.yo = (self.y + 2) % 4
        self.gl = (self.g + 3) % 4
        self.gr = (self.g + 1) % 4
        self.go = (self.g + 2) % 4
        self.dl = (self.d + 3) % 4
        self.dr = (self.d + 1) % 4
        self.do = (self.d + 2) % 4

    def seq(self, z, y, c):
        return z * 8 + y * 2 + c


def add_into(dst, *others):
    total = dst[...].astype(F32)
    for other in others:
        total = total + other[...].astype(F32)
    dst[...] = total.astype(dst.dtype)


class Scatter4:
    def __init__(self, send, src, relay, from_left, from_right, sems, me, left, right, far, to):
        self.send, self.src, self.relay = send, src, relay
        self.from_left, self.from_right, self.sems = from_left, from_right, sems
        self.me, self.left, self.right, self.far, self.to = me, left, right, far, to

    def start(self):
        self.send(self.src(self.far, 0), self.relay(0), self.sems.at[0], **self.to(self.left))
        self.send(self.src(self.far, 1), self.relay(1), self.sems.at[1], **self.to(self.right))

    def direct(self):
        self.send(
            self.src(self.left, 1), self.from_right(1), self.sems.at[2], **self.to(self.left)
        )
        self.send(
            self.src(self.right, 0), self.from_left(0), self.sems.at[3], **self.to(self.right)
        )

    def pass_on(self):
        arrived(self.relay(0), self.sems.at[0])
        add_into(self.src(self.left, 0), self.relay(0))
        self.send(
            self.src(self.left, 0), self.from_right(0), self.sems.at[4], **self.to(self.left)
        )
        arrived(self.relay(1), self.sems.at[1])
        add_into(self.src(self.right, 1), self.relay(1))
        self.send(
            self.src(self.right, 1), self.from_left(1), self.sems.at[5], **self.to(self.right)
        )

    def finish(self):
        arrived(self.from_right(1), self.sems.at[2])
        arrived(self.from_left(0), self.sems.at[3])
        arrived(self.from_right(0), self.sems.at[4])
        arrived(self.from_left(1), self.sems.at[5])


class Gather4:
    def __init__(self, send, slot, half, sems, me, left, right, far, to):
        self.send, self.slot, self.half, self.sems = send, slot, half, sems
        self.me, self.left, self.right, self.far, self.to = me, left, right, far, to

    def start(self, own=None):
        own = self.slot(self.me) if own is None else own
        self.send(own, self.slot(self.me), self.sems.at[0], **self.to(self.right))
        self.send(own, self.slot(self.me), self.sems.at[1], **self.to(self.left))

    def pass_left(self):
        arrived(self.slot(self.left), self.sems.at[0])
        part = self.half(self.left, 0)
        self.send(part, part, self.sems.at[2], **self.to(self.right))

    def pass_right(self):
        arrived(self.slot(self.right), self.sems.at[1])
        part = self.half(self.right, 1)
        self.send(part, part, self.sems.at[3], **self.to(self.left))

    def finish(self):
        arrived(self.half(self.far, 0), self.sems.at[2])
        arrived(self.half(self.far, 1), self.sems.at[3])


NT = (((1,), (1,)), ((), ()))
TN = (((0,), (0,)), ((), ()))
BLOCK = 256


def block_kernel(
    lengths,
    activated,
    mod_weight,
    control,
    zero_weight,
    image_hidden,
    weight,
    text,
    text_cot,
    image_cot,
    attn_out,
    control_grad,
    zero_out,
    ctl,
    zw,
    base,
    wall,
    offset,
    stretch,
    partial,
    rg_relay,
    rg_left,
    rg_right,
    hidden,
    normed,
    joint,
    cots,
    tstage,
    cstage,
    attn,
    ostage,
    grads,
    key_acc,
    value_acc,
    dn,
    pair_in,
    pair_sum,
    ry_relay,
    ry_left,
    ry_right,
    cross_out,
    cross_in,
    rows_all,
    zpart,
    zpair_in,
    zsum,
    zx_relay,
    zx_left,
    zx_right,
    zy_relay,
    zy_left,
    zy_right,
    za_out,
    zb_out,
    za_in,
    zb_in,
    zown,
    zall,
    load_sem,
    send_sem,
    w_sem,
    rg_sem,
    ag_sem,
    text_send,
    text_recv,
    stage_recv,
    cross_recv,
    pair_sem,
    ry_sem,
    cross_sem,
    gg_sem,
    attn_send,
    attn_recv,
    zpair_sem,
    zx_sem,
    zy_sem,
    za_sem,
    zb_sem,
    zg_sem,
):
    p = Place()
    send = Sends(send_sem)
    q = p.y * 2 + p.c
    partner = {"seq": p.seq(p.z, p.y, p.co)}
    across = {"seq": p.seq(p.zo, p.y, p.c)}
    to_y = lambda y: {"seq": p.seq(p.z, y, p.c)}
    to_g = lambda g: {"grp": g}
    to_d = lambda d: {"dp": d}

    loads = []

    def load(src, dst):
        copy = pltpu.make_async_copy(src, dst, load_sem.at[len(loads)])
        copy.start()
        loads.append(copy)
        return copy

    load_weight = [
        load(weight.at[n], wall.at[p.d, :, pl.ds(n * HD, HD)]) for n in range(3)
    ]
    load_control = load(control, ctl)
    load_zero = [
        load(zero_weight.at[:, pl.ds(n * 512, 512)], zw.at[:, pl.ds(n * 512, 512)])
        for n in range(6)
    ]
    load_base = load(image_hidden, base)
    load_mod = [
        load(
            mod_weight.at[pl.ds(n % 8 * ROWS, ROWS), pl.ds(n // 8 * D, D)],
            dn.at[n],
        )
        for n in range(16)
    ]

    greet(
        [{"seq": (p.s + k) % 16} for k in range(1, 16)]
        + [{"grp": p.gl}, {"grp": p.gr}]
        + [{"dp": (p.d + k) % 4} for k in range(1, 4)]
        + [{"dp": (p.d + k) % 4, "seq": p.seq(p.zo, p.y, p.c)} for k in range(1, 4)]
    )

    row = pl.multiple_of(p.s * ROWS, ROWS)
    stage_row = pl.multiple_of(q * ROWS, ROWS)
    plane = pl.ds(pl.multiple_of(p.z * 256, 256), 256)
    other_plane = pl.ds(pl.multiple_of(p.zo * 256, 256), 256)

    def text_pairs(to):
        near = pl.ds(pl.multiple_of((p.z * 8 + to) * HD, HD), HD)
        far = pl.ds(pl.multiple_of((p.zo * 8 + to) * HD, HD), HD)
        rows = pl.ds(row, ROWS)
        image_rows = pl.ds(TXT + row, ROWS)
        staged = pl.ds(stage_row, ROWS)
        return (
            (text.at[:, :, :, near], joint.at[:, :, rows], text_recv.at[0]),
            (text_cot.at[:, :, near], cots.at[:, rows], text_recv.at[1]),
            (image_cot.at[:, :, near], cots.at[:, image_rows], text_recv.at[2]),
            (text.at[:, :, :, far], tstage.at[:, :, staged], stage_recv.at[0]),
            (text_cot.at[:, :, far], cstage.at[0, :, staged], stage_recv.at[1]),
            (image_cot.at[:, :, far], cstage.at[1, :, staged], stage_recv.at[2]),
        )

    def text_copies(k):
        to = (q + k) % 8
        return [
            pltpu.make_async_remote_copy(
                src_ref=src,
                dst_ref=dst,
                send_sem=text_send.at[n, k],
                recv_sem=recv,
                device_id={"seq": p.z * 8 + to},
                device_id_type=MESH,
            )
            for n, (src, dst, recv) in enumerate(text_pairs(to))
        ]

    @pl.loop(1, 8)
    def _(k):
        for copy in text_copies(k):
            copy.start()

    for src, dst, recv in text_pairs(q):
        pltpu.make_async_copy(src, dst, recv).start()

    def text_second_hop(i):
        send(tstage.at[:, i], joint.at[:, i, plane], cross_recv.at[i, 0], **across)
        send(cstage.at[0, i], cots.at[i, plane], cross_recv.at[i, 1], **across)
        image_rows = pl.ds(pl.multiple_of(TXT + p.z * 256, 256), 256)
        send(cstage.at[1, i], cots.at[i, image_rows], cross_recv.at[i, 2], **across)

    def text_wait(i):
        arrived(joint.at[:, i, other_plane], cross_recv.at[i, 0])
        arrived(cots.at[i, other_plane], cross_recv.at[i, 1])
        image_rows = pl.ds(pl.multiple_of(TXT + p.zo * 256, 256), 256)
        arrived(cots.at[i, image_rows], cross_recv.at[i, 2])

    for copy in load_weight:
        copy.wait()
    weights = Gather4(
        send,
        lambda d: wall.at[d],
        lambda d, h: wall.at[d, pl.ds(h * 384, 384)],
        w_sem,
        p.d,
        p.dl,
        p.dr,
        p.do,
        to_d,
    )
    weights.start()

    load_control.wait()
    for block in range(6):
        cols = pl.ds(block * 512, 512)
        load_zero[block].wait()
        product = jnp.dot(ctl[...], zw[:, cols], preferred_element_type=F32)
        partial[:, :, :, cols] = product.astype(BF).reshape(4, 2, ROWS, 512)
    to_group = [
        Scatter4(
            send,
            lambda g, h, i=i: partial.at[g, i, :, pl.ds(h * HALF, HALF)],
            lambda h, i=i: rg_relay.at[i, h],
            lambda h, i=i: rg_left.at[i, h],
            lambda h, i=i: rg_right.at[i, h],
            rg_sem.at[i],
            p.g,
            p.gl,
            p.gr,
            p.go,
            to_g,
        )
        for i in range(2)
    ]
    to_group[0].start()
    to_group[0].direct()

    for copy in load_mod:
        copy.wait()
    offset[...] = jnp.dot(
        activated[...], dn[:8].reshape(FREQ, D), preferred_element_type=F32
    )
    stretch[...] = 1.0 + jnp.dot(
        activated[...], dn[8:].reshape(FREQ, D), preferred_element_type=F32
    )
    load_base.wait()

    to_group[0].pass_on()
    to_group[1].start()
    weights.pass_left()
    weights.pass_right()

    gathers = [
        [
            Gather4(
                send,
                lambda y, i=i, z=z: normed.at[i, z, y, p.c],
                lambda y, h, i=i, z=z: normed.at[i, z, y, p.c, pl.ds(h * 16, 16)],
                ag_sem.at[i, pl.ds(which * 4, 4)],
                p.y,
                p.yl,
                p.yr,
                p.yo,
                to_y,
            )
            for which, z in enumerate((p.z, p.zo))
        ]
        for i in range(2)
    ]

    def share(i, z, y, sem):
        slot = normed.at[i, z, y, p.c]
        send(slot, slot, ag_sem.at[i, sem], **partner)

    def standardise(i):
        values = hidden[i].astype(F32)
        average = jnp.mean(values, axis=-1, keepdims=True)
        centred = values - average
        reciprocal = lax.rsqrt(jnp.mean(centred * centred, axis=-1, keepdims=True) + 1e-06)
        return centred * reciprocal, reciprocal

    def gather_first(i):
        for h in range(2):
            cols = pl.ds(h * HALF, HALF)
            residual = (
                partial[p.g, i, :, cols].astype(F32)
                + rg_left[i, h].astype(F32)
                + rg_right[i, h].astype(F32)
            )
            hidden[i, :, cols] = (base[i, :, cols].astype(F32) + residual).astype(BF)
        standard, _ = standardise(i)
        normed[i, p.z, p.y, p.c] = (
            standard * stretch[i : i + 1] + offset[i : i + 1]
        ).astype(BF)
        mine = normed.at[i, p.z, p.y, p.c]
        send(mine, mine, ag_sem.at[i, 8], **across)
        gathers[i][0].start()
        send(mine, mine, ag_sem.at[i, 9], **partner)

    def gather_second(i):
        arrived(normed.at[i, p.zo, p.y, p.c], ag_sem.at[i, 8])
        gathers[i][1].start()
        share(i, p.zo, p.y, 10)

    def gather_third(i, which):
        z = (p.z, p.zo)[which]
        gathers[i][which].pass_left()
        gathers[i][which].pass_right()
        share(i, z, p.yl, 11 + 3 * which)
        share(i, z, p.yr, 12 + 3 * which)

    def gather_fourth(i, which):
        z = (p.z, p.zo)[which]
        gathers[i][which].finish()
        share(i, z, p.yo, 13 + 3 * which)

    def gather_wait(i):
        arrived(normed.at[i, p.z, p.y, p.co], ag_sem.at[i, 9])
        arrived(normed.at[i, p.zo, p.y, p.co], ag_sem.at[i, 10])
        for which, z in enumerate((p.z, p.zo)):
            for n, y in enumerate((p.yl, p.yr, p.yo)):
                arrived(normed.at[i, z, y, p.co], ag_sem.at[i, 11 + 3 * which + n])

    scaling = HD ** (-0.5)
    position = lax.broadcasted_iota(jnp.int32, (1, TXT + IMG), 1)

    def project(i):
        product = jnp.dot(
            normed[i].reshape(IMG, D), wall[...].reshape(D, 384), preferred_element_type=F32
        ).astype(BF)
        for n in range(3):
            joint[n, i, TXT:] = product[:, n * HD : (n + 1) * HD]

    def attend(i, block):
        rows = pl.ds(block * BLOCK, BLOCK)
        bias = jnp.where((position >= TXT) | (position < lengths[i]), 0.0, -jnp.inf)
        query, cot = joint[0, i, rows], cots[i, rows]
        keys, values = joint[1, i], joint[2, i]
        scores = lax.dot_general(query, keys, NT, preferred_element_type=F32) + bias
        row_max = jnp.max(scores, axis=1, keepdims=True)
        terms = jnp.exp2((scores - row_max) * (scaling * math.log2(math.e)))
        prob = terms * (1.0 / jnp.sum(terms, axis=1, keepdims=True))
        low = prob.astype(BF)
        attended = jnp.dot(low, values, preferred_element_type=F32).astype(BF)
        attn[block // 2, i, pl.ds(block % 2 * BLOCK, BLOCK)] = attended
        dots = jnp.sum(cot.astype(F32) * attended.astype(F32), axis=1, keepdims=True)
        prob_grad = lax.dot_general(cot, values, NT, preferred_element_type=F32)
        score_grad = (prob * (prob_grad - dots)).astype(BF)
        if block >= 2:
            grads[pl.ds((block - 2) * BLOCK, BLOCK), :HD] = (
                jnp.dot(score_grad, keys, preferred_element_type=F32) * scaling
            ).astype(BF)
        key_part = lax.dot_general(score_grad[:, TXT:], query, TN, preferred_element_type=F32)
        value_part = lax.dot_general(low[:, TXT:], cot, TN, preferred_element_type=F32)
        if block == 0:
            key_acc[...] = key_part
            value_acc[...] = value_part
        elif block < 3:
            key_acc[...] += key_part
            value_acc[...] += value_part
        else:
            grads[:, HD : 2 * HD] = ((key_acc[...] + key_part) * scaling).astype(BF)
            grads[:, 2 * HD :] = (value_acc[...] + value_part).astype(BF)

    pair_sends = [Sends(send_sem.at[pl.ds(160 + 8 * i, 8)]) for i in range(2)]

    def back_project(i):
        if i:
            pair_sends[0].drain()
        for n in range(2):
            rows = pl.ds(n * 256, 256)
            for block in range(4):
                cols = pl.ds(block * 768, 768)
                product = lax.dot_general(
                    grads[rows], wall[block], NT, preferred_element_type=F32
                ).astype(BF)
                dn[pl.ds(n * 8, 8), :, cols] = product.reshape(8, ROWS, 768)
            for y in range(4):
                pair_sends[i](
                    dn.at[n * 8 + y * 2 + p.co], pair_in.at[i, n, y], pair_sem.at[i, n * 4 + y],
                    **partner
                )

    def join(i, y):
        for z in range(2):
            arrived(pair_in.at[i, z, y], pair_sem.at[i, z * 4 + y])
            pair_sum[i, z, y] = (
                dn[z * 8 + y * 2 + p.c].astype(F32) + pair_in[i, z, y].astype(F32)
            ).astype(BF)

    round_y = [
        Scatter4(
            send,
            lambda y, h, i=i: pair_sum.at[i, :, y, :, pl.ds(h * HALF, HALF)],
            lambda h, i=i: ry_relay.at[i, h],
            lambda h, i=i: ry_left.at[i, h],
            lambda h, i=i: ry_right.at[i, h],
            ry_sem.at[i],
            p.y,
            p.yl,
            p.yr,
            p.yo,
            to_y,
        )
        for i in range(2)
    ]
    rows_gather = [
        Gather4(
            send,
            lambda g, i=i: rows_all.at[g, i],
            lambda g, h, i=i: rows_all.at[g, i, pl.ds(h * 16, 16)],
            gg_sem.at[i],
            p.g,
            p.gl,
            p.gr,
            p.go,
            to_g,
        )
        for i in range(2)
    ]

    def back_first(i):
        join(i, p.yo)
        round_y[i].start()
        join(i, p.yl)
        join(i, p.yr)
        round_y[i].direct()
        join(i, p.y)

    def y_sum(i, z, h):
        cols = pl.ds(h * HALF, HALF)
        return (
            pair_sum[i, z, p.y, :, cols].astype(F32)
            + ry_left[i, h, z].astype(F32)
            + ry_right[i, h, z].astype(F32)
        )

    def back_second(i):
        round_y[i].finish()
        for h in range(2):
            cross_out[i, :, pl.ds(h * HALF, HALF)] = y_sum(i, p.zo, h).astype(BF)
        send(cross_out.at[i], cross_in.at[i], cross_sem.at[i], **across)

    def back_third(i):
        mine = jnp.concatenate([y_sum(i, p.z, h) for h in range(2)], axis=1)
        standard, reciprocal = standardise(i)
        arrived(cross_in.at[i], cross_sem.at[i])
        scaled = (mine + cross_in[i].astype(F32)) * stretch[i : i + 1]
        rows_all[p.g, i] = (
            reciprocal
            * (
                scaled
                - jnp.mean(scaled, axis=-1, keepdims=True)
                - standard * jnp.mean(scaled * standard, axis=-1, keepdims=True)
            )
        ).astype(BF)
        rows_gather[i].start()

    def attn_pairs(to):
        near = pl.ds(pl.multiple_of((p.z * 8 + to) * ROWS, ROWS), ROWS)
        far = pl.ds(pl.multiple_of((p.zo * 8 + to) * ROWS, ROWS), ROWS)
        cols = pl.ds(pl.multiple_of(p.s * HD, HD), HD)
        staged = pl.ds(pl.multiple_of(q * HD, HD), HD)
        return (
            (attn.at[:, :, near], attn_out.at[:, :, :, cols], attn_recv.at[0]),
            (attn.at[:, :, far], ostage.at[:, :, :, staged], attn_recv.at[1]),
        )

    def attn_copies(k):
        to = (q + k) % 8
        return [
            pltpu.make_async_remote_copy(
                src_ref=src,
                dst_ref=dst,
                send_sem=attn_send.at[n, k],
                recv_sem=recv,
                device_id={"seq": p.z * 8 + to},
                device_id_type=MESH,
            )
            for n, (src, dst, recv) in enumerate(attn_pairs(to))
        ]

    def attn_first_hop():
        @pl.loop(1, 8)
        def _(k):
            for copy in attn_copies(k):
                copy.start()

        for src, dst, recv in attn_pairs(q):
            pltpu.make_async_copy(src, dst, recv).start()

    half_cols = pl.ds(pl.multiple_of(p.z * 1024, 1024), 1024)
    other_cols = pl.ds(pl.multiple_of(p.zo * 1024, 1024), 1024)

    def attn_second_hop():
        arrived(ostage, attn_recv.at[1])
        send(ostage, attn_out.at[:, :, :, half_cols], attn_recv.at[2], **across)

    to_group[0].finish()
    to_group[1].direct()
    gather_first(0)
    to_group[1].pass_on()
    gather_third(0, 0)
    gather_second(0)
    to_group[1].finish()
    arrived(tstage, stage_recv.at[0])
    arrived(cstage.at[0], stage_recv.at[1])
    arrived(cstage.at[1], stage_recv.at[2])
    text_second_hop(0)
    gather_first(1)
    text_second_hop(1)
    gather_fourth(0, 0)
    gather_third(0, 1)
    gather_third(1, 0)
    gather_second(1)
    gather_fourth(0, 1)
    weights.finish()
    gather_wait(0)
    project(0)
    gather_fourth(1, 0)
    arrived(joint.at[:, :, plane], text_recv.at[0])
    arrived(cots.at[:, plane], text_recv.at[1])
    arrived(
        cots.at[:, pl.ds(pl.multiple_of(TXT + p.z * 256, 256), 256)], text_recv.at[2]
    )
    text_wait(0)
    attend(0, 0)
    gather_third(1, 1)
    attend(0, 1)
    attend(0, 2)
    gather_fourth(1, 1)
    attend(0, 3)
    back_project(0)
    gather_wait(1)
    project(1)
    back_first(0)
    text_wait(1)
    attend(1, 0)
    attend(1, 1)
    round_y[0].pass_on()
    attend(1, 2)
    attend(1, 3)
    back_second(0)
    back_project(1)
    back_third(0)
    back_first(1)
    rows_gather[0].pass_left()
    rows_gather[0].pass_right()
    round_y[1].pass_on()
    back_second(1)
    attn_first_hop()
    back_third(1)
    rows_gather[0].finish()

    def control_part(i):
        control_grad[:, i] = (
            lax.dot_general(
                rows_all[:, i].reshape(128, D), zw[...], NT, preferred_element_type=F32
            )
            .astype(BF)
            .reshape(4, ROWS, 768)
        )

    control_part(0)
    rows_gather[1].pass_left()
    rows_gather[1].pass_right()
    rows_gather[1].finish()

    for z in range(2):
        for y in range(4):
            cols = pl.ds((z * 4 + y) * 384, 384)
            grad_cols = rows_all[:, :, :, cols].reshape(256, 384)
            product = lax.dot_general(grad_cols, ctl[...], TN, preferred_element_type=F32)
            zpart[z, y] = product.astype(BF).reshape(2, 192, 768)
            send(
                zpart.at[z, y, p.co], zpair_in.at[z, y], zpair_sem.at[z * 4 + y], **partner
            )
    attn_second_hop()

    cols_a, cols_b = pl.ds(0, 384), pl.ds(384, 384)
    quarter = lambda d: pl.ds(pl.multiple_of(d * 48, 16), 48)
    round_x = Scatter4(
        send,
        lambda d, h: zsum.at[h, :, quarter(d), cols_a],
        lambda h: zx_relay.at[h],
        lambda h: zx_left.at[h],
        lambda h: zx_right.at[h],
        zx_sem,
        p.d,
        p.dl,
        p.dr,
        p.do,
        to_d,
    )
    zero_y = Scatter4(
        send,
        lambda y, h: zsum.at[h, y, :, cols_b],
        lambda h: zy_relay.at[h],
        lambda h: zy_left.at[h],
        lambda h: zy_right.at[h],
        zy_sem,
        p.y,
        p.yl,
        p.yr,
        p.yo,
        to_y,
    )
    for z in range(2):
        for y in range(4):
            arrived(zpair_in.at[z, y], zpair_sem.at[z * 4 + y])
            zsum[z, y] = (
                zpart[z, y, p.c].astype(F32) + zpair_in[z, y].astype(F32)
            ).astype(BF)
    round_x.start()
    zero_y.start()
    round_x.direct()
    zero_y.direct()
    control_part(1)
    round_x.pass_on()
    zero_y.pass_on()
    round_x.finish()
    for z in range(2):
        za_out[z] = (
            zsum[z, :, quarter(p.d), cols_a].astype(F32)
            + zx_left[z].astype(F32)
            + zx_right[z].astype(F32)
        ).astype(BF)
    others_a = [(dz, dy) for dz in range(2) for dy in range(4) if dz or dy]
    for n, (dz, dy) in enumerate(others_a):
        z, y = (p.z + dz) % 2, (p.y + dy) % 4
        send(za_out.at[z, y], za_in.at[n], za_sem.at[n], seq=p.seq(z, y, p.c))
    zero_y.finish()
    for z in range(2):
        zb_out[z] = (
            (
                zsum[z, p.y, :, cols_b].astype(F32)
                + zy_left[z].astype(F32)
                + zy_right[z].astype(F32)
            )
            .astype(BF)
            .reshape(4, 48, 384)
        )
    for n, (dz, dd) in enumerate(others_a):
        z, d = (p.z + dz) % 2, (p.d + dd) % 4
        send(zb_out.at[z, d], zb_in.at[n], zb_sem.at[n], seq=p.seq(z, p.y, p.c), dp=d)
    total = za_out[p.z, p.y].astype(F32)
    for n in range(7):
        arrived(za_in.at[n], za_sem.at[n])
        total = total + za_in[n].astype(F32)
    zown[:, cols_a] = total.astype(BF)
    total = zb_out[p.z, p.d].astype(F32)
    for n in range(7):
        arrived(zb_in.at[n], zb_sem.at[n])
        total = total + zb_in[n].astype(F32)
    zown[:, cols_b] = total.astype(BF)
    for k in range(1, 4):
        send(zown, zall.at[p.d], zg_sem.at[k - 1], dp=(p.d + k) % 4)
    zall[p.d] = zown[...]
    for k in range(1, 4):
        arrived(zall.at[(p.d + 4 - k) % 4], zg_sem.at[k - 1])
    zero_out[...] = zall[...].reshape(192, 768)

    arrived(attn_out.at[:, :, :, half_cols], attn_recv.at[0])
    arrived(attn_out.at[:, :, :, other_cols], attn_recv.at[2])
    send.drain()
    pair_sends[1].drain()

    @pl.loop(1, 8)
    def _(k):
        for copy in text_copies(k):
            copy.wait_send()
        for copy in attn_copies(k):
            copy.wait_send()


def whole_block(*operands):
    dma = pltpu.SemaphoreType.DMA
    bf = lambda *shape: pltpu.VMEM(shape, BF)
    return pl.pallas_call(
        block_kernel,
        out_shape=(
            jax.ShapeDtypeStruct((2, 2, ROWS, HEADS * HD), BF),
            jax.ShapeDtypeStruct((4, 2, ROWS, 768), BF),
            jax.ShapeDtypeStruct((192, 768), BF),
        ),
        in_specs=[pl.BlockSpec(memory_space=pltpu.SMEM), VMEM] + [ANY] * 8,
        out_specs=(ANY, VMEM, VMEM),
        scratch_shapes=[
            bf(256, 768),
            bf(768, D),
            bf(2, ROWS, D),
            bf(4, 768, 384),
            pltpu.VMEM((16, D), F32),
            pltpu.VMEM((16, D), F32),
            bf(4, 2, ROWS, D),
            bf(2, 2, ROWS, HALF),
            bf(2, 2, ROWS, HALF),
            bf(2, 2, ROWS, HALF),
            bf(2, ROWS, D),
            bf(2, 2, 4, 2, ROWS, D),
            bf(3, 2, TXT + IMG, HD),
            bf(2, TXT + IMG, HD),
            bf(3, 2, 256, HD),
            bf(2, 2, 256, HD),
            bf(2, 2, 512, HD),
            bf(2, 2, ROWS, 1024),
            bf(IMG, 384),
            pltpu.VMEM((IMG, HD), F32),
            pltpu.VMEM((IMG, HD), F32),
            bf(16, ROWS, D),
            bf(2, 2, 4, ROWS, D),
            bf(2, 2, 4, ROWS, D),
            bf(2, 2, 2, ROWS, HALF),
            bf(2, 2, 2, ROWS, HALF),
            bf(2, 2, 2, ROWS, HALF),
            bf(2, ROWS, D),
            bf(2, ROWS, D),
            bf(4, 2, ROWS, D),
            bf(2, 4, 2, 192, 768),
            bf(2, 4, 192, 768),
            bf(2, 4, 192, 768),
            bf(2, 4, 48, 384),
            bf(2, 4, 48, 384),
            bf(2, 4, 48, 384),
            bf(2, 192, 384),
            bf(2, 192, 384),
            bf(2, 192, 384),
            bf(2, 4, 48, 384),
            bf(2, 4, 48, 384),
            bf(7, 48, 384),
            bf(7, 48, 384),
            bf(48, 768),
            bf(4, 48, 768),
            dma((28,)),
            dma((176,)),
            dma((4,)),
            dma((2, 6)),
            dma((2, 17)),
            dma((6, 8)),
            dma((3,)),
            dma((3,)),
            dma((2, 3)),
            dma((2, 8)),
            dma((2, 6)),
            dma((2,)),
            dma((2, 4)),
            dma((2, 8)),
            dma((3,)),
            dma((8,)),
            dma((6,)),
            dma((6,)),
            dma((7,)),
            dma((7,)),
            dma((3,)),
        ],
        compiler_params=pltpu.CompilerParams(
            collective_id=1, has_side_effects=True, vmem_limit_bytes=VMEM_LIMIT
        ),
        name="whole_block",
    )(*operands)


def timestep_activation(timesteps):
    half_freq = FREQ // 2
    frequency = jnp.exp(-math.log(10000.0) * jnp.arange(half_freq, dtype=F32) / half_freq)
    angles = timesteps.astype(F32)[..., None] * frequency
    embedding = jnp.concatenate([jnp.cos(angles), jnp.sin(angles)], axis=-1)
    return jax.nn.silu(embedding).astype(BF)


def body(
    image_hidden,
    control_hidden,
    text_qkv,
    text_lengths,
    timesteps,
    mod_weight,
    qkv_weight,
    zero_weight,
    image_cotangent,
    text_cotangent,
):
    activated = timestep_activation(timesteps.reshape(2))
    activated = jnp.pad(activated, ((0, 14), (0, 0)))
    attn_out, control_grad, zero_t = whole_block(
        text_lengths.reshape(2),
        activated,
        mod_weight,
        control_hidden.reshape(256, 768),
        zero_weight,
        image_hidden.reshape(2, ROWS, D),
        jnp.transpose(qkv_weight, (1, 0, 2)),
        text_qkv.reshape(3, 2, ROWS, HEADS * HD),
        text_cotangent.reshape(2, ROWS, HEADS * HD),
        image_cotangent.reshape(2, ROWS, HEADS * HD),
    )
    norm_factor = 16384 ** (-0.5)
    zero_grad = jnp.transpose(zero_t).astype(F32) * norm_factor
    return (
        attn_out[1].reshape(2, 1, ROWS, HEADS * HD),
        attn_out[0].reshape(2, 1, ROWS, HEADS * HD),
        control_grad.reshape(8, 1, ROWS, 768),
        zero_grad,
    )


def solution(mesh):
    placed = (
        P("grp", "dp", "seq", None),
        P(None, "dp", "seq", "grp"),
        P(None, "grp", "dp", "seq", None),
        P("grp", "dp"),
        P("grp", "dp"),
        P(),
        P("dp", None, "seq"),
        P("grp", None),
        P("grp", "dp", "seq", None),
        P("grp", "dp", "seq", None),
    )
    return jax.shard_map(
        body,
        mesh=mesh,
        in_specs=placed,
        out_specs=(
            P("grp", "dp", "seq", None),
            P("grp", "dp", "seq", None),
            P(None, "dp", "seq", "grp"),
            P("grp", "seq"),
        ),
        check_vma=False,
    )
```

time: 485 us -> 179 us (0.37)
  waiting for transfers between devices: 338 us -> 0 us
  Pallas kernels: 0 us -> 172 us
  matrix products: 44 us -> 0 us
  local copies, waits for them, and re-layouts: 26.7 us -> 4.24 us
  starting transfers between devices: 22.2 us -> 0 us
  other arithmetic: 21.5 us -> 2.61 us
  blocking collectives: 16 us -> 0 us
  between operations: 14.3 us -> 0.65 us
    reduce_scatter x3 -> x0, waiting for transfers between devices: 200 us -> none  [the longest x1 71.3 us: body(): lax.psum_scatter(jnp.einsum('tscq,dcq->tsd', selected, weight_full, prefe...]
    pallas_call x0 -> x1, Pallas kernels: none -> 172 us  [whole_block(): pl.pallas_call(block_kernel, out_shape=(jax.ShapeDtypeStruct((2, 2, ROWS,...]
    all_gather x3 -> x0, waiting for transfers between devices: 69.4 us -> none  [the longest x1 39.1 us: body(): grad_rows = lax.all_gather(residual_grad, 'grp', axis=0, tiled=True)]
    dot_general x18 -> x0, matrix products: 44 us -> none  [the longest x1 8.05 us: body(): jnp.einsum('tscq,dcq->tsd', selected, weight_full, preferred_element_type...]
    psum x1 -> x0, waiting for transfers between devices: 39 us -> none  [body(): zero_grad = lax.psum(zero_part, 'dp') * norm_factor]
    all_to_all x4 -> x0, waiting for transfers between devices: 28.9 us -> none  [the longest x1 17.2 us: body(): lax.all_to_all(text_send, 'seq', split_axis=4, concat_axis=3, tiled=True)]
    all_to_all x4 -> x0, starting transfers between devices: 21.9 us -> none  [the longest x1 6.23 us: body(): lax.all_to_all(image_grad_send, 'seq', split_axis=4, concat_axis=3, tiled...]
    all_to_all x1 -> x0, blocking collectives: 16 us -> none  [body(): lax.all_to_all(text_out, 'seq', split_axis=3, concat_axis=4, tiled=True)]
  transfers between devices with their start and end apart: 11 -> 0, of which waited for: 9 -> 0; matrix products, arithmetic and copies ran while one was open for 6% -> 0% of each run, Pallas kernels for 0% -> 0%
where the time goes in v1:
time: 179 us
  Pallas kernels  172 us (96%)
  local copies, waits for them, and re-layouts  4.24 us (2%)
  other arithmetic  2.61 us (1%)
    pallas_call x1, Pallas kernels, whole_block(): pl.pallas_call(block_kernel, out_shape=(jax.ShapeDtypeStruct((2, 2, ROWS,...  172 us
    unnamed x2, local copies, waits for them, and re-layouts  3.63 us

profile of v1, /device:TPU:32, one launch (start us, length us, event | category | flops | bytes accessed | tf_op | source)
XLA Modules:
  0.0 179.3 jit_solution(15582552311314994799)
XLA Ops:
  0.6 0.7 convert_bitcast_fusion
  1.3 0.1 multiply_cosine_fusion
  1.4 0.6 pad.4.activated
  2.0 171.7 %whole_block.1 = (bf16[2,2,32,2048]{3,2,1,0:T(8,128)(2,1)}, bf16[4,2,32,768]{3,2,1,0:T(8,128)(2,1)}, bf16[192,768]{1,0:T(8,128)(2,1)}) custom-call(s32[2]{0:T(128)} %bitcast.29, bf16[16,256]{1,0:T(8,128)(2,1)} %pad.4.activated, bf16[256,6144]{1,0:T(8,128)(2,1)} %mod_weight.1, bf16[256,768]{1,0:T(8,128)(2,1)} %bitcast.24, bf16[768,3072]{1,0:T(8,128)(2,1)} %zero_weight.1, ...), custom_call_target="tpu_custom_call" | custom-call | tf_op jit(solution)/shard_map/whole_block/pallas_call | solution.py:814
  173.8 1.9 %slice_bitcast_fusion = (bf16[2,1,32,2048]{3,2,1,0:T(8,128)(2,1)}, bf16[2,1,32,2048]{3,2,1,0:T(8,128)(2,1)}) fusion(bf16[2,2,32,2048]{3,2,1,0:T(8,128)(2,1)} %get-tuple-element.7), kind=kLoop, calls=%fused_computation.1 | loop fusion | bytes 1048576
  175.7 1.8 %multiply_bitcast_fusion = f32[768,192]{0,1:T(8,128)} fusion(bf16[192,768]{1,0:T(8,128)(2,1)} %get-tuple-element.9), kind=kLoop, calls=%fused_computation | loop fusion | flops 294912 | bytes 884736 | tf_op jit(solution)/shard_map/mul | solution.py:933
  177.5 1.8 copy.18
  (2 shorter events, 0.0 us)

commit v2 on v1

--- a/solution.py
+++ b/solution.py
@@ -21,23 +21,26 @@
 VMEM_LIMIT = 60 * 1024 * 1024
 ANY = pl.BlockSpec(memory_space=pl.ANY)
 VMEM = pl.BlockSpec(memory_space=pltpu.VMEM)
+HBM = pl.BlockSpec(memory_space=pltpu.HBM)
 
 
 class Sends:
     def __init__(self, sems):
         self.sems = sems
         self.copies = []
+        self.started = 0
 
     def __call__(self, src, dst, recv, **to):
         copy = pltpu.make_async_remote_copy(
             src_ref=src,
             dst_ref=dst,
-            send_sem=self.sems.at[len(self.copies)],
+            send_sem=self.sems.at[self.started],
             recv_sem=recv,
             device_id=to,
             device_id_type=MESH,
         )
         copy.start()
+        self.started += 1
         self.copies.append(copy)
 
     def drain(self):
@@ -53,7 +56,7 @@
     barrier = pltpu.get_barrier_semaphore()
     for to in groups:
         pl.semaphore_signal(barrier, inc=1, device_id=to, device_id_type=MESH)
-    pl.semaphore_wait(barrier, len(groups))
+    return lambda: pl.semaphore_wait(barrier, len(groups))
 
 
 class Place:
@@ -93,9 +96,10 @@
         self.from_left, self.from_right, self.sems = from_left, from_right, sems
         self.me, self.left, self.right, self.far, self.to = me, left, right, far, to
 
-    def start(self):
-        self.send(self.src(self.far, 0), self.relay(0), self.sems.at[0], **self.to(self.left))
-        self.send(self.src(self.far, 1), self.relay(1), self.sems.at[1], **self.to(self.right))
+    def start(self, *halves):
+        for h in halves or (0, 1):
+            to = (self.left, self.right)[h]
+            self.send(self.src(self.far, h), self.relay(h), self.sems.at[h], **self.to(to))
 
     def direct(self):
         self.send(
@@ -116,6 +120,13 @@
         self.send(
             self.src(self.right, 1), self.from_left(1), self.sems.at[5], **self.to(self.right)
         )
+        self.passed = self.send.copies[-2:]
+
+    def sent(self):
+        for copy in self.passed:
+            copy.wait_send()
+        waited = [id(copy) for copy in self.passed]
+        self.send.copies = [copy for copy in self.send.copies if id(copy) not in waited]
 
     def finish(self):
         arrived(self.from_right(1), self.sems.at[2])
@@ -244,6 +255,13 @@
     to_g = lambda g: {"grp": g}
     to_d = lambda d: {"dp": d}
 
+    all_here = greet(
+        [{"seq": (p.s + k) % 16} for k in range(1, 16)]
+        + [{"grp": p.gl}, {"grp": p.gr}]
+        + [{"dp": (p.d + k) % 4} for k in range(1, 4)]
+        + [{"dp": (p.d + k) % 4, "seq": p.seq(p.zo, p.y, p.c)} for k in range(1, 4)]
+    )
+
     loads = []
 
     def load(src, dst):
@@ -252,13 +270,13 @@
         loads.append(copy)
         return copy
 
-    load_weight = [
-        load(weight.at[n], wall.at[p.d, :, pl.ds(n * HD, HD)]) for n in range(3)
-    ]
     load_control = load(control, ctl)
     load_zero = [
         load(zero_weight.at[:, pl.ds(n * 512, 512)], zw.at[:, pl.ds(n * 512, 512)])
         for n in range(6)
+    ]
+    load_weight = [
+        load(weight.at[n], wall.at[p.d, :, pl.ds(n * HD, HD)]) for n in range(3)
     ]
     load_base = load(image_hidden, base)
     load_mod = [
@@ -269,12 +287,36 @@
         for n in range(16)
     ]
 
-    greet(
-        [{"seq": (p.s + k) % 16} for k in range(1, 16)]
-        + [{"grp": p.gl}, {"grp": p.gr}]
-        + [{"dp": (p.d + k) % 4} for k in range(1, 4)]
-        + [{"dp": (p.d + k) % 4, "seq": p.seq(p.zo, p.y, p.c)} for k in range(1, 4)]
-    )
+    load_control.wait()
+
+    def residual_part(h):
+        for block in range(3 * h, 3 * h + 3):
+            cols = pl.ds(block * 512, 512)
+            load_zero[block].wait()
+            product = jnp.dot(ctl[...], zw[:, cols], preferred_element_type=F32)
+            partial[:, :, :, cols] = product.astype(BF).reshape(4, 2, ROWS, 512)
+
+    to_group = [
+        Scatter4(
+            send,
+            lambda g, h, i=i: partial.at[g, i, :, pl.ds(h * HALF, HALF)],
+            lambda h, i=i: rg_relay.at[i, h],
+            lambda h, i=i: rg_left.at[i, h],
+            lambda h, i=i: rg_right.at[i, h],
+            rg_sem.at[i],
+            p.g,
+            p.gl,
+            p.gr,
+            p.go,
+            to_g,
+        )
+        for i in range(2)
+    ]
+    residual_part(0)
+    residual_part(1)
+    all_here()
+    to_group[0].start()
+    to_group[0].direct()
 
     row = pl.multiple_of(p.s * ROWS, ROWS)
     stage_row = pl.multiple_of(q * ROWS, ROWS)
@@ -345,31 +387,6 @@
     )
     weights.start()
 
-    load_control.wait()
-    for block in range(6):
-        cols = pl.ds(block * 512, 512)
-        load_zero[block].wait()
-        product = jnp.dot(ctl[...], zw[:, cols], preferred_element_type=F32)
-        partial[:, :, :, cols] = product.astype(BF).reshape(4, 2, ROWS, 512)
-    to_group = [
-        Scatter4(
-            send,
-            lambda g, h, i=i: partial.at[g, i, :, pl.ds(h * HALF, HALF)],
-            lambda h, i=i: rg_relay.at[i, h],
-            lambda h, i=i: rg_left.at[i, h],
-            lambda h, i=i: rg_right.at[i, h],
-            rg_sem.at[i],
-            p.g,
-            p.gl,
-            p.gr,
-            p.go,
-            to_g,
-        )
-        for i in range(2)
-    ]
-    to_group[0].start()
-    to_group[0].direct()
-
     for copy in load_mod:
         copy.wait()
     offset[...] = jnp.dot(
@@ -381,9 +398,11 @@
     load_base.wait()
 
     to_group[0].pass_on()
-    to_group[1].start()
     weights.pass_left()
     weights.pass_right()
+    to_group[0].sent()
+    to_group[1].start()
+    to_group[1].direct()
 
     gathers = [
         [
@@ -407,8 +426,8 @@
         slot = normed.at[i, z, y, p.c]
         send(slot, slot, ag_sem.at[i, sem], **partner)
 
-    def standardise(i):
-        values = hidden[i].astype(F32)
+    def standardise(rows):
+        values = rows.astype(F32)
         average = jnp.mean(values, axis=-1, keepdims=True)
         centred = values - average
         reciprocal = lax.rsqrt(jnp.mean(centred * centred, axis=-1, keepdims=True) + 1e-06)
@@ -423,7 +442,7 @@
                 + rg_right[i, h].astype(F32)
             )
             hidden[i, :, cols] = (base[i, :, cols].astype(F32) + residual).astype(BF)
-        standard, _ = standardise(i)
+        standard, _ = standardise(hidden[i])
         normed[i, p.z, p.y, p.c] = (
             standard * stretch[i : i + 1] + offset[i : i + 1]
         ).astype(BF)
@@ -449,22 +468,22 @@
         gathers[i][which].finish()
         share(i, z, p.yo, 13 + 3 * which)
 
-    def gather_wait(i):
-        arrived(normed.at[i, p.z, p.y, p.co], ag_sem.at[i, 9])
-        arrived(normed.at[i, p.zo, p.y, p.co], ag_sem.at[i, 10])
-        for which, z in enumerate((p.z, p.zo)):
-            for n, y in enumerate((p.yl, p.yr, p.yo)):
-                arrived(normed.at[i, z, y, p.co], ag_sem.at[i, 11 + 3 * which + n])
+    def gather_wait(i, which):
+        z = (p.z, p.zo)[which]
+        arrived(normed.at[i, z, p.y, p.co], ag_sem.at[i, 9 + which])
+        for n, y in enumerate((p.yl, p.yr, p.yo)):
+            arrived(normed.at[i, z, y, p.co], ag_sem.at[i, 11 + 3 * which + n])
 
     scaling = HD ** (-0.5)
     position = lax.broadcasted_iota(jnp.int32, (1, TXT + IMG), 1)
 
-    def project(i):
+    def project(i, z):
         product = jnp.dot(
-            normed[i].reshape(IMG, D), wall[...].reshape(D, 384), preferred_element_type=F32
+            normed[i, z].reshape(256, D), wall[...].reshape(D, 384), preferred_element_type=F32
         ).astype(BF)
+        rows = pl.ds(pl.multiple_of(TXT + z * 256, 256), 256)
         for n in range(3):
-            joint[n, i, TXT:] = product[:, n * HD : (n + 1) * HD]
+            joint[n, i, rows] = product[:, n * HD : (n + 1) * HD]
 
     def attend(i, block):
         rows = pl.ds(block * BLOCK, BLOCK)
@@ -497,24 +516,23 @@
             grads[:, HD : 2 * HD] = ((key_acc[...] + key_part) * scaling).astype(BF)
             grads[:, 2 * HD :] = (value_acc[...] + value_part).astype(BF)
 
-    pair_sends = [Sends(send_sem.at[pl.ds(160 + 8 * i, 8)]) for i in range(2)]
-
-    def back_project(i):
-        if i:
+    pair_sends = [Sends(send_sem.at[pl.ds(176 + 8 * i, 8)]) for i in range(2)]
+
+    def back_project(i, n):
+        if i == 1 and n == 0:
             pair_sends[0].drain()
-        for n in range(2):
-            rows = pl.ds(n * 256, 256)
-            for block in range(4):
-                cols = pl.ds(block * 768, 768)
-                product = lax.dot_general(
-                    grads[rows], wall[block], NT, preferred_element_type=F32
-                ).astype(BF)
-                dn[pl.ds(n * 8, 8), :, cols] = product.reshape(8, ROWS, 768)
-            for y in range(4):
-                pair_sends[i](
-                    dn.at[n * 8 + y * 2 + p.co], pair_in.at[i, n, y], pair_sem.at[i, n * 4 + y],
-                    **partner
-                )
+        rows = pl.ds(n * 256, 256)
+        for block in range(4):
+            cols = pl.ds(block * 768, 768)
+            product = lax.dot_general(
+                grads[rows], wall[block], NT, preferred_element_type=F32
+            ).astype(BF)
+            dn[pl.ds(n * 8, 8), :, cols] = product.reshape(8, ROWS, 768)
+        for y in range(4):
+            pair_sends[i](
+                dn.at[n * 8 + y * 2 + p.co], pair_in.at[i, n, y], pair_sem.at[i, n * 4 + y],
+                **partner
+            )
 
     def join(i, y):
         for z in range(2):
@@ -523,65 +541,73 @@
                 dn[z * 8 + y * 2 + p.c].astype(F32) + pair_in[i, z, y].astype(F32)
             ).astype(BF)
 
-    round_y = [
-        Scatter4(
+    half = lambda h: pl.ds(h * HALF, HALF)
+    part = lambda r: pl.ds(r * 16, 16)
+    chunks = [(i, r) for i in range(2) for r in range(2)]
+    round_y = {
+        (i, r): Scatter4(
             send,
-            lambda y, h, i=i: pair_sum.at[i, :, y, :, pl.ds(h * HALF, HALF)],
-            lambda h, i=i: ry_relay.at[i, h],
-            lambda h, i=i: ry_left.at[i, h],
-            lambda h, i=i: ry_right.at[i, h],
-            ry_sem.at[i],
+            lambda y, h, i=i, r=r: pair_sum.at[i, :, y, part(r), half(h)],
+            lambda h, i=i, r=r: ry_relay.at[i, h, :, part(r)],
+            lambda h, i=i, r=r: ry_left.at[i, h, :, part(r)],
+            lambda h, i=i, r=r: ry_right.at[i, h, :, part(r)],
+            ry_sem.at[i * 2 + r],
             p.y,
             p.yl,
             p.yr,
             p.yo,
             to_y,
         )
-        for i in range(2)
-    ]
-    rows_gather = [
-        Gather4(
+        for i, r in chunks
+    }
+    rows_gather = {
+        (i, r): Gather4(
             send,
-            lambda g, i=i: rows_all.at[g, i],
-            lambda g, h, i=i: rows_all.at[g, i, pl.ds(h * 16, 16)],
-            gg_sem.at[i],
+            lambda g, i=i, r=r: rows_all.at[g, i, part(r)],
+            lambda g, h, i=i, r=r: rows_all.at[g, i, part(r), half(h)],
+            gg_sem.at[i * 2 + r],
             p.g,
             p.gl,
             p.gr,
             p.go,
             to_g,
         )
-        for i in range(2)
-    ]
+        for i, r in chunks
+    }
 
     def back_first(i):
         join(i, p.yo)
-        round_y[i].start()
+        round_y[i, 0].start()
         join(i, p.yl)
         join(i, p.yr)
-        round_y[i].direct()
+        round_y[i, 0].direct()
         join(i, p.y)
 
-    def y_sum(i, z, h):
-        cols = pl.ds(h * HALF, HALF)
+    def back_next(i):
+        round_y[i, 0].pass_on()
+        round_y[i, 1].start()
+
+    def y_sum(i, r, z, h):
         return (
-            pair_sum[i, z, p.y, :, cols].astype(F32)
-            + ry_left[i, h, z].astype(F32)
-            + ry_right[i, h, z].astype(F32)
-        )
-
-    def back_second(i):
-        round_y[i].finish()
+            pair_sum[i, z, p.y, part(r), half(h)].astype(F32)
+            + ry_left[i, h, z, part(r)].astype(F32)
+            + ry_right[i, h, z, part(r)].astype(F32)
+        )
+
+    def back_second(i, r):
+        round_y[i, r].finish()
         for h in range(2):
-            cross_out[i, :, pl.ds(h * HALF, HALF)] = y_sum(i, p.zo, h).astype(BF)
-        send(cross_out.at[i], cross_in.at[i], cross_sem.at[i], **across)
-
-    def back_third(i):
-        mine = jnp.concatenate([y_sum(i, p.z, h) for h in range(2)], axis=1)
-        standard, reciprocal = standardise(i)
-        arrived(cross_in.at[i], cross_sem.at[i])
-        scaled = (mine + cross_in[i].astype(F32)) * stretch[i : i + 1]
-        rows_all[p.g, i] = (
+            cross_out[i, part(r), half(h)] = y_sum(i, r, p.zo, h).astype(BF)
+        send(
+            cross_out.at[i, part(r)], cross_in.at[i, part(r)], cross_sem.at[i * 2 + r], **across
+        )
+
+    def back_third(i, r):
+        mine = jnp.concatenate([y_sum(i, r, p.z, h) for h in range(2)], axis=1)
+        standard, reciprocal = standardise(hidden[i, part(r)])
+        arrived(cross_in.at[i, part(r)], cross_sem.at[i * 2 + r])
+        scaled = (mine + cross_in[i, part(r)].astype(F32)) * stretch[i : i + 1]
+        rows_all[p.g, i, part(r)] = (
             reciprocal
             * (
                 scaled
@@ -589,7 +615,11 @@
                 - standard * jnp.mean(scaled * standard, axis=-1, keepdims=True)
             )
         ).astype(BF)
-        rows_gather[i].start()
+        rows_gather[i, r].start()
+
+    def rows_pass(i, r):
+        rows_gather[i, r].pass_left()
+        rows_gather[i, r].pass_right()
 
     def attn_pairs(to):
         near = pl.ds(pl.multiple_of((p.z * 8 + to) * ROWS, ROWS), ROWS)
@@ -631,8 +661,16 @@
         arrived(ostage, attn_recv.at[1])
         send(ostage, attn_out.at[:, :, :, half_cols], attn_recv.at[2], **across)
 
+    def control_part(i):
+        control_grad[:, i] = (
+            lax.dot_general(
+                rows_all[:, i].reshape(128, D), zw[...], NT, preferred_element_type=F32
+            )
+            .astype(BF)
+            .reshape(4, ROWS, 768)
+        )
+
     to_group[0].finish()
-    to_group[1].direct()
     gather_first(0)
     to_group[1].pass_on()
     gather_third(0, 0)
@@ -643,15 +681,17 @@
     arrived(cstage.at[1], stage_recv.at[2])
     text_second_hop(0)
     gather_first(1)
-    text_second_hop(1)
     gather_fourth(0, 0)
     gather_third(0, 1)
+    gather_wait(0, 0)
+    weights.finish()
+    project(0, p.z)
     gather_third(1, 0)
+    gather_fourth(0, 1)
     gather_second(1)
-    gather_fourth(0, 1)
-    weights.finish()
-    gather_wait(0)
-    project(0)
+    text_second_hop(1)
+    gather_wait(0, 1)
+    project(0, p.zo)
     gather_fourth(1, 0)
     arrived(joint.at[:, :, plane], text_recv.at[0])
     arrived(cots.at[:, plane], text_recv.at[1])
@@ -665,41 +705,45 @@
     attend(0, 2)
     gather_fourth(1, 1)
     attend(0, 3)
-    back_project(0)
-    gather_wait(1)
-    project(1)
+    back_project(0, 0)
+    back_project(0, 1)
+    gather_wait(1, 0)
+    project(1, p.z)
     back_first(0)
+    gather_wait(1, 1)
+    project(1, p.zo)
     text_wait(1)
     attend(1, 0)
     attend(1, 1)
-    round_y[0].pass_on()
+    back_next(0)
     attend(1, 2)
+    back_second(0, 0)
+    round_y[0, 1].direct()
     attend(1, 3)
-    back_second(0)
-    back_project(1)
-    back_third(0)
+    round_y[0, 1].pass_on()
+    back_third(0, 0)
+    back_project(1, 0)
+    back_second(0, 1)
+    back_project(1, 1)
+    back_third(0, 1)
     back_first(1)
-    rows_gather[0].pass_left()
-    rows_gather[0].pass_right()
-    round_y[1].pass_on()
-    back_second(1)
+    rows_pass(0, 0)
+    back_next(1)
+    rows_pass(0, 1)
+    back_second(1, 0)
+    round_y[1, 1].direct()
+    round_y[1, 1].pass_on()
+    back_third(1, 0)
+    back_second(1, 1)
     attn_first_hop()
-    back_third(1)
-    rows_gather[0].finish()
-
-    def control_part(i):
-        control_grad[:, i] = (
-            lax.dot_general(
-                rows_all[:, i].reshape(128, D), zw[...], NT, preferred_element_type=F32
-            )
-            .astype(BF)
-            .reshape(4, ROWS, 768)
-        )
-
+    back_third(1, 1)
+    rows_pass(1, 0)
+    rows_gather[0, 0].finish()
+    rows_gather[0, 1].finish()
     control_part(0)
-    rows_gather[1].pass_left()
-    rows_gather[1].pass_right()
-    rows_gather[1].finish()
+    rows_pass(1, 1)
+    rows_gather[1, 0].finish()
+    rows_gather[1, 1].finish()
 
     for z in range(2):
         for y in range(4):
@@ -746,8 +790,8 @@
             zsum[z, y] = (
                 zpart[z, y, p.c].astype(F32) + zpair_in[z, y].astype(F32)
             ).astype(BF)
-    round_x.start()
-    zero_y.start()
+        round_x.start(z)
+        zero_y.start(z)
     round_x.direct()
     zero_y.direct()
     control_part(1)
@@ -793,7 +837,7 @@
     zall[p.d] = zown[...]
     for k in range(1, 4):
         arrived(zall.at[(p.d + 4 - k) % 4], zg_sem.at[k - 1])
-    zero_out[...] = zall[...].reshape(192, 768)
+    zero_out[...] = zall[...].reshape(192, 768).astype(F32) * (16384 ** (-0.5))
 
     arrived(attn_out.at[:, :, :, half_cols], attn_recv.at[0])
     arrived(attn_out.at[:, :, :, other_cols], attn_recv.at[2])
@@ -816,7 +860,7 @@
         out_shape=(
             jax.ShapeDtypeStruct((2, 2, ROWS, HEADS * HD), BF),
             jax.ShapeDtypeStruct((4, 2, ROWS, 768), BF),
-            jax.ShapeDtypeStruct((192, 768), BF),
+            jax.ShapeDtypeStruct((192, 768), F32),
         ),
         in_specs=[pl.BlockSpec(memory_space=pltpu.SMEM), VMEM] + [ANY] * 8,
         out_specs=(ANY, VMEM, VMEM),
@@ -825,8 +869,8 @@
             bf(768, D),
             bf(2, ROWS, D),
             bf(4, 768, 384),
-            pltpu.VMEM((16, D), F32),
-            pltpu.VMEM((16, D), F32),
+            pltpu.VMEM((2, D), F32),
+            pltpu.VMEM((2, D), F32),
             bf(4, 2, ROWS, D),
             bf(2, 2, ROWS, HALF),
             bf(2, 2, ROWS, HALF),
@@ -867,7 +911,7 @@
             bf(48, 768),
             bf(4, 48, 768),
             dma((28,)),
-            dma((176,)),
+            dma((192,)),
             dma((4,)),
             dma((2, 6)),
             dma((2, 17)),
@@ -876,9 +920,9 @@
             dma((3,)),
             dma((2, 3)),
             dma((2, 8)),
-            dma((2, 6)),
-            dma((2,)),
-            dma((2, 4)),
+            dma((4, 6)),
+            dma((4,)),
+            dma((4, 4)),
             dma((2, 8)),
             dma((3,)),
             dma((8,)),
@@ -895,6 +939,40 @@
     )(*operands)
 
 
+def hand_over_kernel(attn, control, zero, image_out, text_out, control_out, zero_out, sems):
+    copies = [
+        pltpu.make_async_copy(src, dst, sems.at[n])
+        for n, (src, dst) in enumerate(
+            (
+                (attn.at[1], image_out),
+                (attn.at[0], text_out),
+                (control, control_out),
+                (zero, zero_out),
+            )
+        )
+    ]
+    for copy in copies:
+        copy.start()
+    for copy in copies:
+        copy.wait()
+
+
+def hand_over(attn, control, zero):
+    return pl.pallas_call(
+        hand_over_kernel,
+        out_shape=(
+            jax.ShapeDtypeStruct(attn.shape[1:], BF),
+            jax.ShapeDtypeStruct(attn.shape[1:], BF),
+            jax.ShapeDtypeStruct(control.shape, BF),
+            jax.ShapeDtypeStruct(zero.shape, F32),
+        ),
+        in_specs=[HBM] * 3,
+        out_specs=(HBM,) * 4,
+        scratch_shapes=[pltpu.SemaphoreType.DMA((4,))],
+        name="hand_over",
+    )(attn, control, zero)
+
+
 def timestep_activation(timesteps):
     half_freq = FREQ // 2
     frequency = jnp.exp(-math.log(10000.0) * jnp.arange(half_freq, dtype=F32) / half_freq)
@@ -916,7 +994,6 @@
     text_cotangent,
 ):
     activated = timestep_activation(timesteps.reshape(2))
-    activated = jnp.pad(activated, ((0, 14), (0, 0)))
     attn_out, control_grad, zero_t = whole_block(
         text_lengths.reshape(2),
         activated,
@@ -929,13 +1006,12 @@
         text_cotangent.reshape(2, ROWS, HEADS * HD),
         image_cotangent.reshape(2, ROWS, HEADS * HD),
     )
-    norm_factor = 16384 ** (-0.5)
-    zero_grad = jnp.transpose(zero_t).astype(F32) * norm_factor
+    image_attn, text_attn, control_grad, zero_t = hand_over(attn_out, control_grad, zero_t)
     return (
-        attn_out[1].reshape(2, 1, ROWS, HEADS * HD),
-        attn_out[0].reshape(2, 1, ROWS, HEADS * HD),
+        image_attn.reshape(2, 1, ROWS, HEADS * HD),
+        text_attn.reshape(2, 1, ROWS, HEADS * HD),
         control_grad.reshape(8, 1, ROWS, 768),
-        zero_grad,
+        jnp.transpose(zero_t),
     )
 
 

time: 179 us -> 215 us (1.20); the launches traced: 179 us -> 213 us
  Pallas kernels: 172 us -> 210 us
  local copies, waits for them, and re-layouts: 4.24 us -> 0 us
    pallas_call x0 -> x1, Pallas kernels: none -> 46.8 us  [hand_over(): pl.pallas_call(hand_over_kernel, out_shape=(jax.ShapeDtypeStruct(attn.sha...]
    pallas_call x1, Pallas kernels: 172 us -> 164 us  [whole_block(): pl.pallas_call(block_kernel, out_shape=(jax.ShapeDtypeStruct((2, 2, ROWS,...]
    unnamed x2 -> x0, local copies, waits for them, and re-layouts: 3.63 us -> none
where the time goes in v2:
time: 215 us; the launch traced here: 213 us
  Pallas kernels  210 us (98%)
    pallas_call x1, Pallas kernels, whole_block(): pl.pallas_call(block_kernel, out_shape=(jax.ShapeDtypeStruct((2, 2, ROWS,...  164 us
    pallas_call x1, Pallas kernels, hand_over(): pl.pallas_call(hand_over_kernel, out_shape=(jax.ShapeDtypeStruct(attn.sha...  46.8 us

profile of v2, /device:TPU:32, one launch (start us, length us, event | category | flops | bytes accessed | tf_op | source)
XLA Modules:
  0.0 212.6 jit_solution(83275870993922798)
XLA Ops:
  0.6 0.7 convert_bitcast_fusion
  1.3 0.1 multiply_cosine_fusion
  1.4 0.6 fusion.activated
  2.0 163.6 %whole_block.1 = (bf16[2,2,32,2048]{3,2,1,0:T(8,128)(2,1)}, bf16[4,2,32,768]{3,2,1,0:T(8,128)(2,1)}, f32[192,768]{1,0:T(8,128)}) custom-call(s32[2]{0:T(128)} %bitcast.25, bf16[2,256]{1,0:T(2,128)(2,1)} %fusion.activated, bf16[256,6144]{1,0:T(8,128)(2,1)} %mod_weight.1, bf16[256,768]{1,0:T(8,128)(2,1)} %bitcast.21, bf16[768,3072]{1,0:T(8,128)(2,1)} %zero_weight.1, ...), custom_call_target="tpu_custom_call" | custom-call | tf_op jit(solution)/shard_map/whole_block/pallas_call | solution.py:858
  165.6 46.8 %hand_over.1 = (bf16[2,32,2048]{2,1,0:T(8,128)(2,1)}, bf16[2,32,2048]{2,1,0:T(8,128)(2,1)}, bf16[4,2,32,768]{3,2,1,0:T(8,128)(2,1)}, f32[192,768]{1,0:T(8,128)}) custom-call(bf16[2,2,32,2048]{3,2,1,0:T(8,128)(2,1)} %get-tuple-element.11.attn, bf16[4,2,32,768]{3,2,1,0:T(8,128)(2,1)} %get-tuple-element.12.control, f32[192,768]{1,0:T(8,128)} %get-tuple-element.13.zero), custom_call_target="tpu_custom_call" | custom-call | tf_op jit(solution)/shard_map/hand_over/pallas_call | solution.py:961
  (1 shorter events, 0.0 us)

commit v3 on v2

--- a/solution.py
+++ b/solution.py
@@ -21,7 +21,6 @@
 VMEM_LIMIT = 60 * 1024 * 1024
 ANY = pl.BlockSpec(memory_space=pl.ANY)
 VMEM = pl.BlockSpec(memory_space=pltpu.VMEM)
-HBM = pl.BlockSpec(memory_space=pltpu.HBM)
 
 
 class Sends:
@@ -165,6 +164,13 @@
 BLOCK = 256
 
 
+def by_owner(columns, c):
+    runs = columns.shape[1] // 384
+    return jnp.concatenate(
+        [columns[:, n * 384 + c * 192 : n * 384 + c * 192 + 192] for n in range(runs)], axis=1
+    )
+
+
 def block_kernel(
     lengths,
     activated,
@@ -180,7 +186,9 @@
     control_grad,
     zero_out,
     ctl,
+    ctl_in,
     zw,
+    zw_owner,
     base,
     wall,
     offset,
@@ -191,6 +199,7 @@
     rg_right,
     hidden,
     normed,
+    qkv_out,
     joint,
     cots,
     tstage,
@@ -198,10 +207,9 @@
     attn,
     ostage,
     grads,
+    both_grads,
     key_acc,
     value_acc,
-    dn,
-    pair_in,
     pair_sum,
     ry_relay,
     ry_left,
@@ -209,8 +217,8 @@
     cross_out,
     cross_in,
     rows_all,
-    zpart,
-    zpair_in,
+    rows_in,
+    zacc,
     zsum,
     zx_relay,
     zx_left,
@@ -227,19 +235,21 @@
     load_sem,
     send_sem,
     w_sem,
+    share_sem,
     rg_sem,
     ag_sem,
     text_send,
     text_recv,
     stage_recv,
     cross_recv,
-    pair_sem,
+    qkv_sem,
+    grads_sem,
     ry_sem,
     cross_sem,
     gg_sem,
+    rows_sem,
     attn_send,
     attn_recv,
-    zpair_sem,
     zx_sem,
     zy_sem,
     za_sem,
@@ -282,7 +292,7 @@
     load_mod = [
         load(
             mod_weight.at[pl.ds(n % 8 * ROWS, ROWS), pl.ds(n // 8 * D, D)],
-            dn.at[n],
+            pair_sum.at[n // 8, n // 4 % 2, n % 4],
         )
         for n in range(16)
     ]
@@ -293,7 +303,9 @@
         for block in range(3 * h, 3 * h + 3):
             cols = pl.ds(block * 512, 512)
             load_zero[block].wait()
-            product = jnp.dot(ctl[...], zw[:, cols], preferred_element_type=F32)
+            product = jnp.dot(
+                ctl[...].reshape(256, 768), zw[:, cols], preferred_element_type=F32
+            )
             partial[:, :, :, cols] = product.astype(BF).reshape(4, 2, ROWS, 512)
 
     to_group = [
@@ -318,24 +330,20 @@
     to_group[0].start()
     to_group[0].direct()
 
-    row = pl.multiple_of(p.s * ROWS, ROWS)
-    stage_row = pl.multiple_of(q * ROWS, ROWS)
-    plane = pl.ds(pl.multiple_of(p.z * 256, 256), 256)
-    other_plane = pl.ds(pl.multiple_of(p.zo * 256, 256), 256)
+    plane = pl.ds(p.z * 4, 4)
+    other_plane = pl.ds(p.zo * 4, 4)
+    zy = p.z * 4 + p.y
 
     def text_pairs(to):
         near = pl.ds(pl.multiple_of((p.z * 8 + to) * HD, HD), HD)
         far = pl.ds(pl.multiple_of((p.zo * 8 + to) * HD, HD), HD)
-        rows = pl.ds(row, ROWS)
-        image_rows = pl.ds(TXT + row, ROWS)
-        staged = pl.ds(stage_row, ROWS)
         return (
-            (text.at[:, :, :, near], joint.at[:, :, rows], text_recv.at[0]),
-            (text_cot.at[:, :, near], cots.at[:, rows], text_recv.at[1]),
-            (image_cot.at[:, :, near], cots.at[:, image_rows], text_recv.at[2]),
-            (text.at[:, :, :, far], tstage.at[:, :, staged], stage_recv.at[0]),
-            (text_cot.at[:, :, far], cstage.at[0, :, staged], stage_recv.at[1]),
-            (image_cot.at[:, :, far], cstage.at[1, :, staged], stage_recv.at[2]),
+            (text.at[:, :, :, near], joint.at[:, :, 0, zy, p.c], text_recv.at[0]),
+            (text_cot.at[:, :, near], cots.at[:, 0, zy, p.c], text_recv.at[1]),
+            (image_cot.at[:, :, near], cots.at[:, 1, zy, p.c], text_recv.at[2]),
+            (text.at[:, :, :, far], tstage.at[:, :, p.y, p.c], stage_recv.at[0]),
+            (text_cot.at[:, :, far], cstage.at[0, :, p.y, p.c], stage_recv.at[1]),
+            (image_cot.at[:, :, far], cstage.at[1, :, p.y, p.c], stage_recv.at[2]),
         )
 
     def text_copies(k):
@@ -361,23 +369,22 @@
         pltpu.make_async_copy(src, dst, recv).start()
 
     def text_second_hop(i):
-        send(tstage.at[:, i], joint.at[:, i, plane], cross_recv.at[i, 0], **across)
-        send(cstage.at[0, i], cots.at[i, plane], cross_recv.at[i, 1], **across)
-        image_rows = pl.ds(pl.multiple_of(TXT + p.z * 256, 256), 256)
-        send(cstage.at[1, i], cots.at[i, image_rows], cross_recv.at[i, 2], **across)
+        send(tstage.at[:, i], joint.at[:, i, 0, plane], cross_recv.at[i, 0], **across)
+        send(cstage.at[0, i], cots.at[i, 0, plane], cross_recv.at[i, 1], **across)
+        send(cstage.at[1, i], cots.at[i, 1, plane], cross_recv.at[i, 2], **across)
 
     def text_wait(i):
-        arrived(joint.at[:, i, other_plane], cross_recv.at[i, 0])
-        arrived(cots.at[i, other_plane], cross_recv.at[i, 1])
-        image_rows = pl.ds(pl.multiple_of(TXT + p.zo * 256, 256), 256)
-        arrived(cots.at[i, image_rows], cross_recv.at[i, 2])
+        arrived(joint.at[:, i, 0, other_plane], cross_recv.at[i, 0])
+        arrived(cots.at[i, 0, other_plane], cross_recv.at[i, 1])
+        arrived(cots.at[i, 1, other_plane], cross_recv.at[i, 2])
 
     for copy in load_weight:
         copy.wait()
+    mine_cols, pair_cols = pl.ds(0, 384), pl.ds(384, 384)
     weights = Gather4(
         send,
-        lambda d: wall.at[d],
-        lambda d, h: wall.at[d, pl.ds(h * 384, 384)],
+        lambda d: wall.at[d, :, mine_cols],
+        lambda d, h: wall.at[d, pl.ds(h * 384, 384), mine_cols],
         w_sem,
         p.d,
         p.dl,
@@ -387,19 +394,32 @@
     )
     weights.start()
 
+    def share_weight(d, sem):
+        send(wall.at[d, :, mine_cols], wall.at[d, :, pair_cols], share_sem.at[sem], **partner)
+
+    share_weight(p.d, 0)
+    send(ctl, ctl_in, share_sem.at[4], **partner)
+
     for copy in load_mod:
         copy.wait()
     offset[...] = jnp.dot(
-        activated[...], dn[:8].reshape(FREQ, D), preferred_element_type=F32
+        activated[...], pair_sum[0].reshape(FREQ, D), preferred_element_type=F32
     )
     stretch[...] = 1.0 + jnp.dot(
-        activated[...], dn[8:].reshape(FREQ, D), preferred_element_type=F32
+        activated[...], pair_sum[1].reshape(FREQ, D), preferred_element_type=F32
     )
     load_base.wait()
+
+    for block in range(4):
+        columns = zw[:, pl.ds(block * 768, 768)].astype(F32)
+        for c in range(2):
+            zw_owner[c, :, pl.ds(block * 384, 384)] = by_owner(columns, c).astype(BF)
 
     to_group[0].pass_on()
     weights.pass_left()
     weights.pass_right()
+    share_weight(p.dl, 1)
+    share_weight(p.dr, 2)
     to_group[0].sent()
     to_group[1].start()
     to_group[1].direct()
@@ -408,8 +428,8 @@
         [
             Gather4(
                 send,
-                lambda y, i=i, z=z: normed.at[i, z, y, p.c],
-                lambda y, h, i=i, z=z: normed.at[i, z, y, p.c, pl.ds(h * 16, 16)],
+                lambda y, i=i, z=z: normed.at[i, z, y],
+                lambda y, h, i=i, z=z: normed.at[i, z, y, pl.ds(h * 16, 16)],
                 ag_sem.at[i, pl.ds(which * 4, 4)],
                 p.y,
                 p.yl,
@@ -422,10 +442,6 @@
         for i in range(2)
     ]
 
-    def share(i, z, y, sem):
-        slot = normed.at[i, z, y, p.c]
-        send(slot, slot, ag_sem.at[i, sem], **partner)
-
     def standardise(rows):
         values = rows.astype(F32)
         average = jnp.mean(values, axis=-1, keepdims=True)
@@ -443,53 +459,45 @@
             )
             hidden[i, :, cols] = (base[i, :, cols].astype(F32) + residual).astype(BF)
         standard, _ = standardise(hidden[i])
-        normed[i, p.z, p.y, p.c] = (
-            standard * stretch[i : i + 1] + offset[i : i + 1]
-        ).astype(BF)
-        mine = normed.at[i, p.z, p.y, p.c]
+        normed[i, p.z, p.y] = (standard * stretch[i : i + 1] + offset[i : i + 1]).astype(BF)
+        mine = normed.at[i, p.z, p.y]
         send(mine, mine, ag_sem.at[i, 8], **across)
         gathers[i][0].start()
-        send(mine, mine, ag_sem.at[i, 9], **partner)
 
     def gather_second(i):
-        arrived(normed.at[i, p.zo, p.y, p.c], ag_sem.at[i, 8])
+        arrived(normed.at[i, p.zo, p.y], ag_sem.at[i, 8])
         gathers[i][1].start()
-        share(i, p.zo, p.y, 10)
 
     def gather_third(i, which):
-        z = (p.z, p.zo)[which]
         gathers[i][which].pass_left()
         gathers[i][which].pass_right()
-        share(i, z, p.yl, 11 + 3 * which)
-        share(i, z, p.yr, 12 + 3 * which)
 
     def gather_fourth(i, which):
-        z = (p.z, p.zo)[which]
         gathers[i][which].finish()
-        share(i, z, p.yo, 13 + 3 * which)
-
-    def gather_wait(i, which):
-        z = (p.z, p.zo)[which]
-        arrived(normed.at[i, z, p.y, p.co], ag_sem.at[i, 9 + which])
-        for n, y in enumerate((p.yl, p.yr, p.yo)):
-            arrived(normed.at[i, z, y, p.co], ag_sem.at[i, 11 + 3 * which + n])
 
     scaling = HD ** (-0.5)
     position = lax.broadcasted_iota(jnp.int32, (1, TXT + IMG), 1)
 
-    def project(i, z):
+    def project(i):
         product = jnp.dot(
-            normed[i, z].reshape(256, D), wall[...].reshape(D, 384), preferred_element_type=F32
+            normed[i].reshape(256, D), wall[...].reshape(D, 768), preferred_element_type=F32
         ).astype(BF)
-        rows = pl.ds(pl.multiple_of(TXT + z * 256, 256), 256)
         for n in range(3):
-            joint[n, i, rows] = product[:, n * HD : (n + 1) * HD]
+            qkv_out[i, n] = product[:, 384 + n * HD : 384 + (n + 1) * HD].reshape(8, ROWS, HD)
+        send(qkv_out.at[i], joint.at[:, i, 1, :, p.c], qkv_sem.at[i], **partner)
+        for n in range(3):
+            joint[n, i, 1, :, p.c] = product[:, n * HD : (n + 1) * HD].reshape(8, ROWS, HD)
+
+    def project_wait(i):
+        arrived(joint.at[:, i, 1, :, p.co], qkv_sem.at[i])
 
     def attend(i, block):
-        rows = pl.ds(block * BLOCK, BLOCK)
+        slots = pl.ds(block % 2 * 4, 4)
         bias = jnp.where((position >= TXT) | (position < lengths[i]), 0.0, -jnp.inf)
-        query, cot = joint[0, i, rows], cots[i, rows]
-        keys, values = joint[1, i], joint[2, i]
+        query = joint[0, i, block // 2, slots].reshape(BLOCK, HD)
+        cot = cots[i, block // 2, slots].reshape(BLOCK, HD)
+        keys = joint[1, i].reshape(TXT + IMG, HD)
+        values = joint[2, i].reshape(TXT + IMG, HD)
         scores = lax.dot_general(query, keys, NT, preferred_element_type=F32) + bias
         row_max = jnp.max(scores, axis=1, keepdims=True)
         terms = jnp.exp2((scores - row_max) * (scaling * math.log2(math.e)))
@@ -501,9 +509,8 @@
         prob_grad = lax.dot_general(cot, values, NT, preferred_element_type=F32)
         score_grad = (prob * (prob_grad - dots)).astype(BF)
         if block >= 2:
-            grads[pl.ds((block - 2) * BLOCK, BLOCK), :HD] = (
-                jnp.dot(score_grad, keys, preferred_element_type=F32) * scaling
-            ).astype(BF)
+            query_grad = jnp.dot(score_grad, keys, preferred_element_type=F32) * scaling
+            grads[i, slots, :, :, :HD] = query_grad.astype(BF).reshape(4, 2, ROWS, HD)
         key_part = lax.dot_general(score_grad[:, TXT:], query, TN, preferred_element_type=F32)
         value_part = lax.dot_general(low[:, TXT:], cot, TN, preferred_element_type=F32)
         if block == 0:
@@ -513,33 +520,27 @@
             key_acc[...] += key_part
             value_acc[...] += value_part
         else:
-            grads[:, HD : 2 * HD] = ((key_acc[...] + key_part) * scaling).astype(BF)
-            grads[:, 2 * HD :] = (value_acc[...] + value_part).astype(BF)
-
-    pair_sends = [Sends(send_sem.at[pl.ds(176 + 8 * i, 8)]) for i in range(2)]
-
-    def back_project(i, n):
-        if i == 1 and n == 0:
-            pair_sends[0].drain()
-        rows = pl.ds(n * 256, 256)
+            key_grad = ((key_acc[...] + key_part) * scaling).astype(BF)
+            value_grad = (value_acc[...] + value_part).astype(BF)
+            grads[i, :, :, :, HD : 2 * HD] = key_grad.reshape(8, 2, ROWS, HD)
+            grads[i, :, :, :, 2 * HD :] = value_grad.reshape(8, 2, ROWS, HD)
+            send(
+                grads.at[i, :, p.co], both_grads.at[i, :, :, pair_cols], grads_sem.at[i],
+                **partner
+            )
+            both_grads[i, :, :, :384] = grads[i, :, p.c]
+
+    def back_project(i):
+        arrived(both_grads.at[i, :, :, pair_cols], grads_sem.at[i])
         for block in range(4):
             cols = pl.ds(block * 768, 768)
             product = lax.dot_general(
-                grads[rows], wall[block], NT, preferred_element_type=F32
+                both_grads[i].reshape(256, 768), wall[block], NT, preferred_element_type=F32
             ).astype(BF)
-            dn[pl.ds(n * 8, 8), :, cols] = product.reshape(8, ROWS, 768)
-        for y in range(4):
-            pair_sends[i](
-                dn.at[n * 8 + y * 2 + p.co], pair_in.at[i, n, y], pair_sem.at[i, n * 4 + y],
-                **partner
-            )
-
-    def join(i, y):
-        for z in range(2):
-            arrived(pair_in.at[i, z, y], pair_sem.at[i, z * 4 + y])
-            pair_sum[i, z, y] = (
-                dn[z * 8 + y * 2 + p.c].astype(F32) + pair_in[i, z, y].astype(F32)
-            ).astype(BF)
+            pair_sum[i, :, :, :, cols] = product.reshape(2, 4, ROWS, 768)
+            if block % 2:
+                round_y[i, 0].start(block // 2)
+        round_y[i, 0].direct()
 
     half = lambda h: pl.ds(h * HALF, HALF)
     part = lambda r: pl.ds(r * 16, 16)
@@ -563,8 +564,8 @@
     rows_gather = {
         (i, r): Gather4(
             send,
-            lambda g, i=i, r=r: rows_all.at[g, i, part(r)],
-            lambda g, h, i=i, r=r: rows_all.at[g, i, part(r), half(h)],
+            lambda g, i=i, r=r: rows_all.at[:, g, i, part(r)],
+            lambda g, h, i=i, r=r: rows_all.at[h, g, i, part(r)],
             gg_sem.at[i * 2 + r],
             p.g,
             p.gl,
@@ -575,14 +576,6 @@
         for i, r in chunks
     }
 
-    def back_first(i):
-        join(i, p.yo)
-        round_y[i, 0].start()
-        join(i, p.yl)
-        join(i, p.yr)
-        round_y[i, 0].direct()
-        join(i, p.y)
-
     def back_next(i):
         round_y[i, 0].pass_on()
         round_y[i, 1].start()
@@ -607,19 +600,27 @@
         standard, reciprocal = standardise(hidden[i, part(r)])
         arrived(cross_in.at[i, part(r)], cross_sem.at[i * 2 + r])
         scaled = (mine + cross_in[i, part(r)].astype(F32)) * stretch[i : i + 1]
-        rows_all[p.g, i, part(r)] = (
-            reciprocal
-            * (
-                scaled
-                - jnp.mean(scaled, axis=-1, keepdims=True)
-                - standard * jnp.mean(scaled * standard, axis=-1, keepdims=True)
-            )
-        ).astype(BF)
+        residual_grad = reciprocal * (
+            scaled
+            - jnp.mean(scaled, axis=-1, keepdims=True)
+            - standard * jnp.mean(scaled * standard, axis=-1, keepdims=True)
+        )
+        for c in range(2):
+            rows_all[c, p.g, i, part(r)] = by_owner(residual_grad, c).astype(BF)
         rows_gather[i, r].start()
 
     def rows_pass(i, r):
         rows_gather[i, r].pass_left()
         rows_gather[i, r].pass_right()
+
+    def rows_finish(i, r):
+        rows_gather[i, r].finish()
+        send(
+            rows_all.at[p.co, :, i, part(r)],
+            rows_in.at[:, i, part(r)],
+            rows_sem.at[i * 2 + r],
+            **partner
+        )
 
     def attn_pairs(to):
         near = pl.ds(pl.multiple_of((p.z * 8 + to) * ROWS, ROWS), ROWS)
@@ -662,13 +663,28 @@
         send(ostage, attn_out.at[:, :, :, half_cols], attn_recv.at[2], **across)
 
     def control_part(i):
-        control_grad[:, i] = (
-            lax.dot_general(
-                rows_all[:, i].reshape(128, D), zw[...], NT, preferred_element_type=F32
+        total = 0.0
+        for c in range(2):
+            total = total + lax.dot_general(
+                rows_all[c, :, i].reshape(128, HALF),
+                zw_owner[c],
+                NT,
+                preferred_element_type=F32,
             )
-            .astype(BF)
-            .reshape(4, ROWS, 768)
-        )
+        control_grad[:, i] = total.astype(BF).reshape(4, ROWS, 768)
+
+    def zero_part(i, block):
+        cols = pl.ds(block * 384, 384)
+        left = jnp.concatenate(
+            [ref.reshape(128, 384) for ref in (rows_all[p.c, :, i, :, cols], rows_in[:, i, :, cols])]
+        )
+        right = jnp.concatenate([ctl[:, i].reshape(128, 768), ctl_in[:, i].reshape(128, 768)])
+        product = lax.dot_general(left, right, TN, preferred_element_type=F32)
+        if i == 0:
+            zacc[cols] = product
+        else:
+            z, y = block // 2, block % 2 * 2
+            zsum[z, pl.ds(y, 2)] = (zacc[cols] + product).astype(BF).reshape(2, 192, 768)
 
     to_group[0].finish()
     gather_first(0)
@@ -683,36 +699,31 @@
     gather_first(1)
     gather_fourth(0, 0)
     gather_third(0, 1)
-    gather_wait(0, 0)
+    gather_third(1, 0)
     weights.finish()
-    project(0, p.z)
-    gather_third(1, 0)
+    share_weight(p.do, 3)
     gather_fourth(0, 1)
+    for n, d in enumerate((p.d, p.dl, p.dr, p.do)):
+        arrived(wall.at[d, :, pair_cols], share_sem.at[n])
+    project(0)
     gather_second(1)
     text_second_hop(1)
-    gather_wait(0, 1)
-    project(0, p.zo)
     gather_fourth(1, 0)
-    arrived(joint.at[:, :, plane], text_recv.at[0])
-    arrived(cots.at[:, plane], text_recv.at[1])
-    arrived(
-        cots.at[:, pl.ds(pl.multiple_of(TXT + p.z * 256, 256), 256)], text_recv.at[2]
-    )
+    arrived(joint.at[:, :, 0, plane], text_recv.at[0])
+    arrived(cots.at[:, 0, plane], text_recv.at[1])
+    arrived(cots.at[:, 1, plane], text_recv.at[2])
     text_wait(0)
+    project_wait(0)
     attend(0, 0)
     gather_third(1, 1)
     attend(0, 1)
     attend(0, 2)
     gather_fourth(1, 1)
     attend(0, 3)
-    back_project(0, 0)
-    back_project(0, 1)
-    gather_wait(1, 0)
-    project(1, p.z)
-    back_first(0)
-    gather_wait(1, 1)
-    project(1, p.zo)
+    project(1)
+    back_project(0)
     text_wait(1)
+    project_wait(1)
     attend(1, 0)
     attend(1, 1)
     back_next(0)
@@ -722,11 +733,9 @@
     attend(1, 3)
     round_y[0, 1].pass_on()
     back_third(0, 0)
-    back_project(1, 0)
     back_second(0, 1)
-    back_project(1, 1)
+    back_project(1)
     back_third(0, 1)
-    back_first(1)
     rows_pass(0, 0)
     back_next(1)
     rows_pass(0, 1)
@@ -734,27 +743,23 @@
     round_y[1, 1].direct()
     round_y[1, 1].pass_on()
     back_third(1, 0)
+    rows_finish(0, 0)
     back_second(1, 1)
     attn_first_hop()
     back_third(1, 1)
     rows_pass(1, 0)
-    rows_gather[0, 0].finish()
-    rows_gather[0, 1].finish()
+    rows_finish(0, 1)
+    arrived(ctl_in, share_sem.at[4])
     control_part(0)
     rows_pass(1, 1)
-    rows_gather[1, 0].finish()
-    rows_gather[1, 1].finish()
-
-    for z in range(2):
-        for y in range(4):
-            cols = pl.ds((z * 4 + y) * 384, 384)
-            grad_cols = rows_all[:, :, :, cols].reshape(256, 384)
-            product = lax.dot_general(grad_cols, ctl[...], TN, preferred_element_type=F32)
-            zpart[z, y] = product.astype(BF).reshape(2, 192, 768)
-            send(
-                zpart.at[z, y, p.co], zpair_in.at[z, y], zpair_sem.at[z * 4 + y], **partner
-            )
-    attn_second_hop()
+    for r in range(2):
+        arrived(rows_in.at[:, 0, part(r)], rows_sem.at[r])
+    for block in range(4):
+        zero_part(0, block)
+    rows_finish(1, 0)
+    rows_finish(1, 1)
+    for r in range(2):
+        arrived(rows_in.at[:, 1, part(r)], rows_sem.at[2 + r])
 
     cols_a, cols_b = pl.ds(0, 384), pl.ds(384, 384)
     quarter = lambda d: pl.ds(pl.multiple_of(d * 48, 16), 48)
@@ -785,15 +790,13 @@
         to_y,
     )
     for z in range(2):
-        for y in range(4):
-            arrived(zpair_in.at[z, y], zpair_sem.at[z * 4 + y])
-            zsum[z, y] = (
-                zpart[z, y, p.c].astype(F32) + zpair_in[z, y].astype(F32)
-            ).astype(BF)
+        zero_part(1, 2 * z)
+        zero_part(1, 2 * z + 1)
         round_x.start(z)
         zero_y.start(z)
     round_x.direct()
     zero_y.direct()
+    attn_second_hop()
     control_part(1)
     round_x.pass_on()
     zero_y.pass_on()
@@ -842,7 +845,6 @@
     arrived(attn_out.at[:, :, :, half_cols], attn_recv.at[0])
     arrived(attn_out.at[:, :, :, other_cols], attn_recv.at[2])
     send.drain()
-    pair_sends[1].drain()
 
     @pl.loop(1, 8)
     def _(k):
@@ -865,10 +867,12 @@
         in_specs=[pl.BlockSpec(memory_space=pltpu.SMEM), VMEM] + [ANY] * 8,
         out_specs=(ANY, VMEM, VMEM),
         scratch_shapes=[
-            bf(256, 768),
+            bf(4, 2, ROWS, 768),
+            bf(4, 2, ROWS, 768),
             bf(768, D),
+            bf(2, 768, HALF),
             bf(2, ROWS, D),
-            bf(4, 768, 384),
+            bf(4, 768, 768),
             pltpu.VMEM((2, D), F32),
             pltpu.VMEM((2, D), F32),
             bf(4, 2, ROWS, D),
@@ -876,27 +880,27 @@
             bf(2, 2, ROWS, HALF),
             bf(2, 2, ROWS, HALF),
             bf(2, ROWS, D),
-            bf(2, 2, 4, 2, ROWS, D),
-            bf(3, 2, TXT + IMG, HD),
-            bf(2, TXT + IMG, HD),
-            bf(3, 2, 256, HD),
-            bf(2, 2, 256, HD),
+            bf(2, 2, 4, ROWS, D),
+            bf(2, 3, 8, ROWS, HD),
+            bf(3, 2, 2, 8, 2, ROWS, HD),
+            bf(2, 2, 8, 2, ROWS, HD),
+            bf(3, 2, 4, 2, ROWS, HD),
+            bf(2, 2, 4, 2, ROWS, HD),
             bf(2, 2, 512, HD),
             bf(2, 2, ROWS, 1024),
-            bf(IMG, 384),
+            bf(2, 8, 2, ROWS, 384),
+            bf(2, 8, ROWS, 768),
             pltpu.VMEM((IMG, HD), F32),
             pltpu.VMEM((IMG, HD), F32),
-            bf(16, ROWS, D),
-            bf(2, 2, 4, ROWS, D),
             bf(2, 2, 4, ROWS, D),
             bf(2, 2, 2, ROWS, HALF),
             bf(2, 2, 2, ROWS, HALF),
             bf(2, 2, 2, ROWS, HALF),
             bf(2, ROWS, D),
             bf(2, ROWS, D),
-            bf(4, 2, ROWS, D),
-            bf(2, 4, 2, 192, 768),
-            bf(2, 4, 192, 768),
+            bf(2, 4, 2, ROWS, HALF),
+            bf(4, 2, ROWS, HALF),
+            pltpu.VMEM((HALF, 768), F32),
             bf(2, 4, 192, 768),
             bf(2, 4, 48, 384),
             bf(2, 4, 48, 384),
@@ -911,21 +915,23 @@
             bf(48, 768),
             bf(4, 48, 768),
             dma((28,)),
-            dma((192,)),
+            dma((176,)),
             dma((4,)),
+            dma((5,)),
             dma((2, 6)),
-            dma((2, 17)),
+            dma((2, 9)),
             dma((6, 8)),
             dma((3,)),
             dma((3,)),
             dma((2, 3)),
-            dma((2, 8)),
+            dma((2,)),
+            dma((2,)),
             dma((4, 6)),
             dma((4,)),
             dma((4, 4)),
+            dma((4,)),
             dma((2, 8)),
             dma((3,)),
-            dma((8,)),
             dma((6,)),
             dma((6,)),
             dma((7,)),
@@ -966,8 +972,8 @@
             jax.ShapeDtypeStruct(control.shape, BF),
             jax.ShapeDtypeStruct(zero.shape, F32),
         ),
-        in_specs=[HBM] * 3,
-        out_specs=(HBM,) * 4,
+        in_specs=[VMEM] * 3,
+        out_specs=(ANY,) * 4,
         scratch_shapes=[pltpu.SemaphoreType.DMA((4,))],
         name="hand_over",
     )(attn, control, zero)
@@ -998,7 +1004,7 @@
         text_lengths.reshape(2),
         activated,
         mod_weight,
-        control_hidden.reshape(256, 768),
+        control_hidden.reshape(4, 2, ROWS, 768),
         zero_weight,
         image_hidden.reshape(2, ROWS, D),
         jnp.transpose(qkv_weight, (1, 0, 2)),

time: 215 us -> 165 us (0.77)
  Pallas kernels: 210 us -> 162 us
    pallas_call x1, Pallas kernels: 46.8 us -> 2.49 us  [hand_over(): pl.pallas_call(hand_over_kernel, out_shape=(jax.ShapeDtypeStruct(attn.sha...]
    pallas_call x1, Pallas kernels: 164 us -> 159 us  [whole_block(): pl.pallas_call(block_kernel, out_shape=(jax.ShapeDtypeStruct((2, 2, ROWS,...]
where the time goes in v3:
time: 165 us; the launch traced here: 164 us
  Pallas kernels  162 us (98%)
    pallas_call x1, Pallas kernels, whole_block(): pl.pallas_call(block_kernel, out_shape=(jax.ShapeDtypeStruct((2, 2, ROWS,...  159 us

profile of v3, /device:TPU:32, one launch (start us, length us, event | category | flops | bytes accessed | tf_op | source)
XLA Modules:
  0.0 164.0 jit_solution(15661017832214603685)
XLA Ops:
  0.6 0.7 convert_bitcast_fusion
  1.3 0.1 multiply_cosine_fusion
  1.4 0.6 fusion.activated
  2.0 159.3 %whole_block.1 = (bf16[2,2,32,2048]{3,2,1,0:T(8,128)(2,1)}, bf16[4,2,32,768]{3,2,1,0:T(8,128)(2,1)}, f32[192,768]{1,0:T(8,128)}) custom-call(s32[2]{0:T(128)} %bitcast.25, bf16[2,256]{1,0:T(2,128)(2,1)} %fusion.activated, bf16[256,6144]{1,0:T(8,128)(2,1)} %mod_weight.1, bf16[4,2,32,768]{3,2,1,0:T(8,128)(2,1)} %bitcast.21, bf16[768,3072]{1,0:T(8,128)(2,1)} %zero_weight.1, ...), custom_call_target="tpu_custom_call" | custom-call | tf_op jit(solution)/shard_map/whole_block/pallas_call | solution.py:860
  161.3 2.5 %hand_over.1 = (bf16[2,32,2048]{2,1,0:T(8,128)(2,1)}, bf16[2,32,2048]{2,1,0:T(8,128)(2,1)}, bf16[4,2,32,768]{3,2,1,0:T(8,128)(2,1)}, f32[192,768]{1,0:T(8,128)}) custom-call(bf16[2,2,32,2048]{3,2,1,0:T(8,128)(2,1)} %get-tuple-element.11.attn, bf16[4,2,32,768]{3,2,1,0:T(8,128)(2,1)} %get-tuple-element.12.control, f32[192,768]{1,0:T(8,128)} %get-tuple-element.13.zero), custom_call_target="tpu_custom_call" | custom-call | tf_op jit(solution)/shard_map/hand_over/pallas_call | solution.py:967
  (1 shorter events, 0.0 us)

commit v4 on v3

--- a/solution.py
+++ b/solution.py
@@ -232,6 +232,8 @@
     zb_in,
     zown,
     zall,
+    text_mine,
+    cots_mine,
     load_sem,
     send_sem,
     w_sem,
@@ -288,6 +290,11 @@
     load_weight = [
         load(weight.at[n], wall.at[p.d, :, pl.ds(n * HD, HD)]) for n in range(3)
     ]
+    load_text = [
+        load(text, text_mine),
+        load(text_cot, cots_mine.at[0]),
+        load(image_cot, cots_mine.at[1]),
+    ]
     load_base = load(image_hidden, base)
     load_mod = [
         load(
@@ -338,12 +345,10 @@
         near = pl.ds(pl.multiple_of((p.z * 8 + to) * HD, HD), HD)
         far = pl.ds(pl.multiple_of((p.zo * 8 + to) * HD, HD), HD)
         return (
-            (text.at[:, :, :, near], joint.at[:, :, 0, zy, p.c], text_recv.at[0]),
-            (text_cot.at[:, :, near], cots.at[:, 0, zy, p.c], text_recv.at[1]),
-            (image_cot.at[:, :, near], cots.at[:, 1, zy, p.c], text_recv.at[2]),
-            (text.at[:, :, :, far], tstage.at[:, :, p.y, p.c], stage_recv.at[0]),
-            (text_cot.at[:, :, far], cstage.at[0, :, p.y, p.c], stage_recv.at[1]),
-            (image_cot.at[:, :, far], cstage.at[1, :, p.y, p.c], stage_recv.at[2]),
+            (text_mine.at[:, :, :, far], tstage.at[:, :, p.y, p.c], stage_recv.at[0]),
+            (cots_mine.at[:, :, :, far], cstage.at[:, :, p.y, p.c], stage_recv.at[1]),
+            (text_mine.at[:, :, :, near], joint.at[:, :, 0, zy, p.c], text_recv.at[0]),
+            (cots_mine.at[:, :, :, near], cots.at[:, :, zy, p.c], text_recv.at[1]),
         )
 
     def text_copies(k):
@@ -360,6 +365,9 @@
             for n, (src, dst, recv) in enumerate(text_pairs(to))
         ]
 
+    for copy in load_text:
+        copy.wait()
+
     @pl.loop(1, 8)
     def _(k):
         for copy in text_copies(k):
@@ -370,13 +378,11 @@
 
     def text_second_hop(i):
         send(tstage.at[:, i], joint.at[:, i, 0, plane], cross_recv.at[i, 0], **across)
-        send(cstage.at[0, i], cots.at[i, 0, plane], cross_recv.at[i, 1], **across)
-        send(cstage.at[1, i], cots.at[i, 1, plane], cross_recv.at[i, 2], **across)
+        send(cstage.at[:, i], cots.at[:, i, plane], cross_recv.at[i, 1], **across)
 
     def text_wait(i):
         arrived(joint.at[:, i, 0, other_plane], cross_recv.at[i, 0])
-        arrived(cots.at[i, 0, other_plane], cross_recv.at[i, 1])
-        arrived(cots.at[i, 1, other_plane], cross_recv.at[i, 2])
+        arrived(cots.at[:, i, other_plane], cross_recv.at[i, 1])
 
     for copy in load_weight:
         copy.wait()
@@ -495,7 +501,7 @@
         slots = pl.ds(block % 2 * 4, 4)
         bias = jnp.where((position >= TXT) | (position < lengths[i]), 0.0, -jnp.inf)
         query = joint[0, i, block // 2, slots].reshape(BLOCK, HD)
-        cot = cots[i, block // 2, slots].reshape(BLOCK, HD)
+        cot = cots[block // 2, i, slots].reshape(BLOCK, HD)
         keys = joint[1, i].reshape(TXT + IMG, HD)
         values = joint[2, i].reshape(TXT + IMG, HD)
         scores = lax.dot_general(query, keys, NT, preferred_element_type=F32) + bias
@@ -691,35 +697,33 @@
     to_group[1].pass_on()
     gather_third(0, 0)
     gather_second(0)
-    to_group[1].finish()
-    arrived(tstage, stage_recv.at[0])
-    arrived(cstage.at[0], stage_recv.at[1])
-    arrived(cstage.at[1], stage_recv.at[2])
-    text_second_hop(0)
-    gather_first(1)
     gather_fourth(0, 0)
     gather_third(0, 1)
-    gather_third(1, 0)
+    arrived(tstage, stage_recv.at[0])
+    arrived(cstage, stage_recv.at[1])
+    text_second_hop(0)
+    to_group[1].finish()
+    gather_first(1)
     weights.finish()
     share_weight(p.do, 3)
     gather_fourth(0, 1)
     for n, d in enumerate((p.d, p.dl, p.dr, p.do)):
         arrived(wall.at[d, :, pair_cols], share_sem.at[n])
     project(0)
+    gather_third(1, 0)
     gather_second(1)
     text_second_hop(1)
-    gather_fourth(1, 0)
     arrived(joint.at[:, :, 0, plane], text_recv.at[0])
-    arrived(cots.at[:, 0, plane], text_recv.at[1])
-    arrived(cots.at[:, 1, plane], text_recv.at[2])
+    arrived(cots.at[:, :, plane], text_recv.at[1])
     text_wait(0)
     project_wait(0)
     attend(0, 0)
+    gather_fourth(1, 0)
+    attend(0, 1)
     gather_third(1, 1)
-    attend(0, 1)
     attend(0, 2)
+    attend(0, 3)
     gather_fourth(1, 1)
-    attend(0, 3)
     project(1)
     back_project(0)
     text_wait(1)
@@ -733,10 +737,10 @@
     attend(1, 3)
     round_y[0, 1].pass_on()
     back_third(0, 0)
+    back_project(1)
     back_second(0, 1)
-    back_project(1)
+    rows_pass(0, 0)
     back_third(0, 1)
-    rows_pass(0, 0)
     back_next(1)
     rows_pass(0, 1)
     back_second(1, 0)
@@ -865,7 +869,7 @@
             jax.ShapeDtypeStruct((192, 768), F32),
         ),
         in_specs=[pl.BlockSpec(memory_space=pltpu.SMEM), VMEM] + [ANY] * 8,
-        out_specs=(ANY, VMEM, VMEM),
+        out_specs=(VMEM, VMEM, VMEM),
         scratch_shapes=[
             bf(4, 2, ROWS, 768),
             bf(4, 2, ROWS, 768),
@@ -914,16 +918,18 @@
             bf(7, 48, 384),
             bf(48, 768),
             bf(4, 48, 768),
-            dma((28,)),
+            bf(3, 2, ROWS, HEADS * HD),
+            bf(2, 2, ROWS, HEADS * HD),
+            dma((32,)),
             dma((176,)),
             dma((4,)),
             dma((5,)),
             dma((2, 6)),
             dma((2, 9)),
-            dma((6, 8)),
-            dma((3,)),
-            dma((3,)),
-            dma((2, 3)),
+            dma((4, 8)),
+            dma((2,)),
+            dma((2,)),
+            dma((2, 2)),
             dma((2,)),
             dma((2,)),
             dma((4, 6)),

time: 165 us -> 168 us (1.018)
  Pallas kernels: 162 us -> 166 us
    pallas_call x1, Pallas kernels: 159 us -> 163 us  [whole_block(): pl.pallas_call(block_kernel, out_shape=(jax.ShapeDtypeStruct((2, 2, ROWS,...]
where the time goes in v4:
time: 168 us
  Pallas kernels  166 us (99%)
    pallas_call x1, Pallas kernels, whole_block(): pl.pallas_call(block_kernel, out_shape=(jax.ShapeDtypeStruct((2, 2, ROWS,...  163 us

profile of v4, /device:TPU:32, one launch (start us, length us, event | category | flops | bytes accessed | tf_op | source)
XLA Modules:
  0.0 167.9 jit_solution(1741033115505151294)
XLA Ops:
  0.6 0.7 convert_bitcast_fusion
  1.3 0.1 multiply_cosine_fusion
  1.4 0.6 fusion.activated
  2.0 163.2 %whole_block.1 = (bf16[2,2,32,2048]{3,2,1,0:T(8,128)(2,1)}, bf16[4,2,32,768]{3,2,1,0:T(8,128)(2,1)}, f32[192,768]{1,0:T(8,128)}) custom-call(s32[2]{0:T(128)} %bitcast.25, bf16[2,256]{1,0:T(2,128)(2,1)} %fusion.activated, bf16[256,6144]{1,0:T(8,128)(2,1)} %mod_weight.1, bf16[4,2,32,768]{3,2,1,0:T(8,128)(2,1)} %bitcast.21, bf16[768,3072]{1,0:T(8,128)(2,1)} %zero_weight.1, ...), custom_call_target="tpu_custom_call" | custom-call | tf_op jit(solution)/shard_map/whole_block/pallas_call | solution.py:864
  165.2 2.5 %hand_over.1 = (bf16[2,32,2048]{2,1,0:T(8,128)(2,1)}, bf16[2,32,2048]{2,1,0:T(8,128)(2,1)}, bf16[4,2,32,768]{3,2,1,0:T(8,128)(2,1)}, f32[192,768]{1,0:T(8,128)}) custom-call(bf16[2,2,32,2048]{3,2,1,0:T(8,128)(2,1)} %get-tuple-element.11.attn, bf16[4,2,32,768]{3,2,1,0:T(8,128)(2,1)} %get-tuple-element.12.control, f32[192,768]{1,0:T(8,128)} %get-tuple-element.13.zero), custom_call_target="tpu_custom_call" | custom-call | tf_op jit(solution)/shard_map/hand_over/pallas_call | solution.py:973
  (1 shorter events, 0.0 us)

commit v5 on v4

--- a/solution.py
+++ b/solution.py
@@ -41,10 +41,16 @@
         copy.start()
         self.started += 1
         self.copies.append(copy)
+        return copy
+
+    def sent(self, copies):
+        for copy in copies:
+            copy.wait_send()
+        waited = [id(copy) for copy in copies]
+        self.copies = [copy for copy in self.copies if id(copy) not in waited]
 
     def drain(self):
-        for copy in self.copies:
-            copy.wait_send()
+        self.sent(list(self.copies))
 
 
 def arrived(dst, recv):
@@ -94,38 +100,27 @@
         self.send, self.src, self.relay = send, src, relay
         self.from_left, self.from_right, self.sems = from_left, from_right, sems
         self.me, self.left, self.right, self.far, self.to = me, left, right, far, to
-
-    def start(self, *halves):
-        for h in halves or (0, 1):
-            to = (self.left, self.right)[h]
-            self.send(self.src(self.far, h), self.relay(h), self.sems.at[h], **self.to(to))
-
-    def direct(self):
-        self.send(
-            self.src(self.left, 1), self.from_right(1), self.sems.at[2], **self.to(self.left)
-        )
-        self.send(
-            self.src(self.right, 0), self.from_left(0), self.sems.at[3], **self.to(self.right)
-        )
-
-    def pass_on(self):
-        arrived(self.relay(0), self.sems.at[0])
-        add_into(self.src(self.left, 0), self.relay(0))
-        self.send(
-            self.src(self.left, 0), self.from_right(0), self.sems.at[4], **self.to(self.left)
-        )
-        arrived(self.relay(1), self.sems.at[1])
-        add_into(self.src(self.right, 1), self.relay(1))
-        self.send(
-            self.src(self.right, 1), self.from_left(1), self.sems.at[5], **self.to(self.right)
-        )
-        self.passed = self.send.copies[-2:]
-
-    def sent(self):
-        for copy in self.passed:
-            copy.wait_send()
-        waited = [id(copy) for copy in self.passed]
-        self.send.copies = [copy for copy in self.send.copies if id(copy) not in waited]
+        self.passed = []
+
+    def start(self, h):
+        to = (self.left, self.right)[h]
+        self.send(self.src(self.far, h), self.relay(h), self.sems.at[h], **self.to(to))
+
+    def direct(self, h):
+        if h:
+            dst, to = self.from_right(1), self.left
+        else:
+            dst, to = self.from_left(0), self.right
+        self.send(self.src(to, h), dst, self.sems.at[3 - h], **self.to(to))
+
+    def pass_on(self, h):
+        arrived(self.relay(h), self.sems.at[h])
+        if h:
+            dst, to = self.from_left(1), self.right
+        else:
+            dst, to = self.from_right(0), self.left
+        add_into(self.src(to, h), self.relay(h))
+        self.passed.append(self.send(self.src(to, h), dst, self.sems.at[4 + h], **self.to(to)))
 
     def finish(self):
         arrived(self.from_right(1), self.sems.at[2])
@@ -141,8 +136,10 @@
 
     def start(self, own=None):
         own = self.slot(self.me) if own is None else own
-        self.send(own, self.slot(self.me), self.sems.at[0], **self.to(self.right))
-        self.send(own, self.slot(self.me), self.sems.at[1], **self.to(self.left))
+        self.begun = [
+            self.send(own, self.slot(self.me), self.sems.at[0], **self.to(self.right)),
+            self.send(own, self.slot(self.me), self.sems.at[1], **self.to(self.left)),
+        ]
 
     def pass_left(self):
         arrived(self.slot(self.left), self.sems.at[0])
@@ -159,6 +156,19 @@
         arrived(self.half(self.far, 1), self.sems.at[3])
 
 
+ORDER = (
+    "res0", "res1", "Rs00", "T10", "Ws", "mod", "zwo", "Rp000", "Rp100", "Rs01", "LN00", "GL000",
+    "GR000", "Rp001", "Rp101", "WL", "WR_", "Gz00", "Rs10", "LN01", "T20", "T11", "GR001",
+    "GL001", "Wf", "Rp010", "Rp110", "Gz01", "Rs11", "LN10", "GL010", "GR010", "GR011", "GL011",
+    "GL100", "GR100", "Rp011", "Rp111", "proj0", "Gz10", "LN11", "att00", "att01", "GL101",
+    "Gz11", "att02", "att03", "T21", "GL110", "GR101", "GR110", "GR111", "bpa0", "GL111", "bpb0",
+    "Bs00", "Bd00", "proj1", "Bp100", "Bp000", "att10", "Bs01", "att11", "att12", "Bd01", "att13",
+    "BX00", "Bp101", "Bp001", "bpa1", "bpb1", "Bs10", "Bd10", "BL00", "BX01", "Bp110", "Bp010",
+    "Bs11", "Bd11", "AL00", "AR00", "BL01", "Af00", "Bp111", "BX10", "Bp011", "AL01", "AR01",
+    "BX11", "O1", "BL10", "Af01", "ctl0", "BL11", "AS10", "zp0", "AS11", "AL10", "AR10", "Af10",
+    "AL11", "AR11", "zp1a", "Af11", "ctl1", "zp1b", "Zp0y", "Zp0x", "O2", "Zp1x", "Zp1y", "ZA",
+    "ZB", "ZS", "zgL_", "zgR_",
+)
 NT = (((1,), (1,)), ((), ()))
 TN = (((0,), (0,)), ((), ()))
 BLOCK = 256
@@ -230,7 +240,6 @@
     zb_out,
     za_in,
     zb_in,
-    zown,
     zall,
     text_mine,
     cots_mine,
@@ -304,9 +313,21 @@
         for n in range(16)
     ]
 
-    load_control.wait()
+    half = lambda h: pl.ds(h * HALF, HALF)
+    part = lambda r: pl.ds(r * 16, 16)
+    chunks = [(i, r) for i in range(2) for r in range(2)]
+    steps = {}
+
+    def step(name, *args):
+        def add(f):
+            steps[name] = lambda: f(*args)
+            return f
+
+        return add
 
     def residual_part(h):
+        if h == 0:
+            load_control.wait()
         for block in range(3 * h, 3 * h + 3):
             cols = pl.ds(block * 512, 512)
             load_zero[block].wait()
@@ -314,78 +335,100 @@
                 ctl[...].reshape(256, 768), zw[:, cols], preferred_element_type=F32
             )
             partial[:, :, :, cols] = product.astype(BF).reshape(4, 2, ROWS, 512)
-
-    to_group = [
-        Scatter4(
+        if h == 1:
+            all_here()
+
+    step("res0", 0)(residual_part)
+    step("res1", 1)(residual_part)
+
+    to_group = {
+        (i, r): Scatter4(
             send,
-            lambda g, h, i=i: partial.at[g, i, :, pl.ds(h * HALF, HALF)],
-            lambda h, i=i: rg_relay.at[i, h],
-            lambda h, i=i: rg_left.at[i, h],
-            lambda h, i=i: rg_right.at[i, h],
-            rg_sem.at[i],
+            lambda g, h, i=i, r=r: partial.at[g, i, part(r), half(h)],
+            lambda h, i=i, r=r: rg_relay.at[i, h, part(r)],
+            lambda h, i=i, r=r: rg_left.at[i, h, part(r)],
+            lambda h, i=i, r=r: rg_right.at[i, h, part(r)],
+            rg_sem.at[i * 2 + r],
             p.g,
             p.gl,
             p.gr,
             p.go,
             to_g,
         )
-        for i in range(2)
-    ]
-    residual_part(0)
-    residual_part(1)
-    all_here()
-    to_group[0].start()
-    to_group[0].direct()
+        for i, r in chunks
+    }
+
+    def group_start(n):
+        if n:
+            send.sent(to_group[chunks[n - 1]].passed)
+        scatter = to_group[chunks[n]]
+        for h in range(2):
+            scatter.start(h)
+        scatter.direct(1)
+        scatter.direct(0)
+
+    for n, (i, r) in enumerate(chunks):
+        step(f"Rs{i}{r}", n)(group_start)
+        for h in range(2):
+            step(f"Rp{h}{i}{r}", h)(to_group[i, r].pass_on)
 
     plane = pl.ds(p.z * 4, 4)
     other_plane = pl.ds(p.zo * 4, 4)
     zy = p.z * 4 + p.y
 
-    def text_pairs(to):
+    def text_pairs(i, to):
         near = pl.ds(pl.multiple_of((p.z * 8 + to) * HD, HD), HD)
         far = pl.ds(pl.multiple_of((p.zo * 8 + to) * HD, HD), HD)
         return (
-            (text_mine.at[:, :, :, far], tstage.at[:, :, p.y, p.c], stage_recv.at[0]),
-            (cots_mine.at[:, :, :, far], cstage.at[:, :, p.y, p.c], stage_recv.at[1]),
-            (text_mine.at[:, :, :, near], joint.at[:, :, 0, zy, p.c], text_recv.at[0]),
-            (cots_mine.at[:, :, :, near], cots.at[:, :, zy, p.c], text_recv.at[1]),
-        )
-
-    def text_copies(k):
+            (text_mine.at[:, i, :, far], tstage.at[:, i, p.y, p.c], stage_recv.at[0, i]),
+            (cots_mine.at[:, i, :, far], cstage.at[:, i, p.y, p.c], stage_recv.at[1, i]),
+            (text_mine.at[:, i, :, near], joint.at[:, i, 0, zy, p.c], text_recv.at[0, i]),
+            (cots_mine.at[:, i, :, near], cots.at[:, i, zy, p.c], text_recv.at[1, i]),
+        )
+
+    def text_copies(i, k):
         to = (q + k) % 8
         return [
             pltpu.make_async_remote_copy(
                 src_ref=src,
                 dst_ref=dst,
-                send_sem=text_send.at[n, k],
+                send_sem=text_send.at[n, i, k],
                 recv_sem=recv,
                 device_id={"seq": p.z * 8 + to},
                 device_id_type=MESH,
             )
-            for n, (src, dst, recv) in enumerate(text_pairs(to))
+            for n, (src, dst, recv) in enumerate(text_pairs(i, to))
         ]
 
-    for copy in load_text:
-        copy.wait()
-
-    @pl.loop(1, 8)
-    def _(k):
-        for copy in text_copies(k):
-            copy.start()
-
-    for src, dst, recv in text_pairs(q):
-        pltpu.make_async_copy(src, dst, recv).start()
+    def text_first_hop(i):
+        if i == 0:
+            for copy in load_text:
+                copy.wait()
+
+        @pl.loop(1, 8)
+        def _(k):
+            for copy in text_copies(i, k):
+                copy.start()
+
+        for src, dst, recv in text_pairs(i, q):
+            pltpu.make_async_copy(src, dst, recv).start()
 
     def text_second_hop(i):
+        arrived(tstage.at[:, i], stage_recv.at[0, i])
+        arrived(cstage.at[:, i], stage_recv.at[1, i])
         send(tstage.at[:, i], joint.at[:, i, 0, plane], cross_recv.at[i, 0], **across)
         send(cstage.at[:, i], cots.at[:, i, plane], cross_recv.at[i, 1], **across)
 
     def text_wait(i):
+        arrived(joint.at[:, i, 0, plane], text_recv.at[0, i])
+        arrived(cots.at[:, i, plane], text_recv.at[1, i])
         arrived(joint.at[:, i, 0, other_plane], cross_recv.at[i, 0])
         arrived(cots.at[:, i, other_plane], cross_recv.at[i, 1])
 
-    for copy in load_weight:
-        copy.wait()
+    for i in range(2):
+        step(f"T1{i}", i)(text_first_hop)
+        step(f"T2{i}", i)(text_second_hop)
+
     mine_cols, pair_cols = pl.ds(0, 384), pl.ds(384, 384)
     weights = Gather4(
         send,
@@ -398,55 +441,67 @@
         p.do,
         to_d,
     )
-    weights.start()
 
     def share_weight(d, sem):
         send(wall.at[d, :, mine_cols], wall.at[d, :, pair_cols], share_sem.at[sem], **partner)
 
-    share_weight(p.d, 0)
-    send(ctl, ctl_in, share_sem.at[4], **partner)
-
-    for copy in load_mod:
-        copy.wait()
-    offset[...] = jnp.dot(
-        activated[...], pair_sum[0].reshape(FREQ, D), preferred_element_type=F32
-    )
-    stretch[...] = 1.0 + jnp.dot(
-        activated[...], pair_sum[1].reshape(FREQ, D), preferred_element_type=F32
-    )
-    load_base.wait()
-
-    for block in range(4):
-        columns = zw[:, pl.ds(block * 768, 768)].astype(F32)
-        for c in range(2):
-            zw_owner[c, :, pl.ds(block * 384, 384)] = by_owner(columns, c).astype(BF)
-
-    to_group[0].pass_on()
-    weights.pass_left()
-    weights.pass_right()
-    share_weight(p.dl, 1)
-    share_weight(p.dr, 2)
-    to_group[0].sent()
-    to_group[1].start()
-    to_group[1].direct()
-
-    gathers = [
-        [
-            Gather4(
-                send,
-                lambda y, i=i, z=z: normed.at[i, z, y],
-                lambda y, h, i=i, z=z: normed.at[i, z, y, pl.ds(h * 16, 16)],
-                ag_sem.at[i, pl.ds(which * 4, 4)],
-                p.y,
-                p.yl,
-                p.yr,
-                p.yo,
-                to_y,
-            )
-            for which, z in enumerate((p.z, p.zo))
-        ]
-        for i in range(2)
-    ]
+    @step("Ws")
+    def _():
+        for copy in load_weight:
+            copy.wait()
+        weights.start()
+        share_weight(p.d, 0)
+        send(ctl, ctl_in, share_sem.at[4], **partner)
+
+    @step("WL")
+    def _():
+        weights.pass_left()
+        share_weight(p.dl, 1)
+
+    @step("WR_")
+    def _():
+        weights.pass_right()
+        share_weight(p.dr, 2)
+
+    @step("Wf")
+    def _():
+        weights.finish()
+        share_weight(p.do, 3)
+
+    @step("mod")
+    def _():
+        for copy in load_mod:
+            copy.wait()
+        offset[...] = jnp.dot(
+            activated[...], pair_sum[0].reshape(FREQ, D), preferred_element_type=F32
+        )
+        stretch[...] = 1.0 + jnp.dot(
+            activated[...], pair_sum[1].reshape(FREQ, D), preferred_element_type=F32
+        )
+        load_base.wait()
+
+    @step("zwo")
+    def _():
+        for block in range(4):
+            columns = zw[:, pl.ds(block * 768, 768)].astype(F32)
+            for c in range(2):
+                zw_owner[c, :, pl.ds(block * 384, 384)] = by_owner(columns, c).astype(BF)
+
+    gathers = {
+        (i, r, which): Gather4(
+            send,
+            lambda y, i=i, r=r, z=z: normed.at[i, z, y, part(r)],
+            lambda y, h, i=i, r=r, z=z: normed.at[i, z, y, part(r), half(h)],
+            ag_sem.at[i * 2 + r, pl.ds(which * 4, 4)],
+            p.y,
+            p.yl,
+            p.yr,
+            p.yo,
+            to_y,
+        )
+        for i, r in chunks
+        for which, z in enumerate((p.z, p.zo))
+    }
 
     def standardise(rows):
         values = rows.astype(F32)
@@ -455,36 +510,45 @@
         reciprocal = lax.rsqrt(jnp.mean(centred * centred, axis=-1, keepdims=True) + 1e-06)
         return centred * reciprocal, reciprocal
 
-    def gather_first(i):
+    def gather_first(i, r):
+        to_group[i, r].finish()
+        rows = part(r)
         for h in range(2):
-            cols = pl.ds(h * HALF, HALF)
             residual = (
-                partial[p.g, i, :, cols].astype(F32)
-                + rg_left[i, h].astype(F32)
-                + rg_right[i, h].astype(F32)
+                partial[p.g, i, rows, half(h)].astype(F32)
+                + rg_left[i, h, rows].astype(F32)
+                + rg_right[i, h, rows].astype(F32)
             )
-            hidden[i, :, cols] = (base[i, :, cols].astype(F32) + residual).astype(BF)
-        standard, _ = standardise(hidden[i])
-        normed[i, p.z, p.y] = (standard * stretch[i : i + 1] + offset[i : i + 1]).astype(BF)
-        mine = normed.at[i, p.z, p.y]
-        send(mine, mine, ag_sem.at[i, 8], **across)
-        gathers[i][0].start()
-
-    def gather_second(i):
-        arrived(normed.at[i, p.zo, p.y], ag_sem.at[i, 8])
-        gathers[i][1].start()
-
-    def gather_third(i, which):
-        gathers[i][which].pass_left()
-        gathers[i][which].pass_right()
-
-    def gather_fourth(i, which):
-        gathers[i][which].finish()
+            hidden[i, rows, half(h)] = (base[i, rows, half(h)].astype(F32) + residual).astype(BF)
+        standard, _ = standardise(hidden[i, rows])
+        normed[i, p.z, p.y, rows] = (
+            standard * stretch[i : i + 1] + offset[i : i + 1]
+        ).astype(BF)
+        mine = normed.at[i, p.z, p.y, rows]
+        send(mine, mine, ag_sem.at[i * 2 + r, 8], **across)
+        gathers[i, r, 0].start()
+
+    def gather_second(i, r):
+        arrived(normed.at[i, p.zo, p.y, part(r)], ag_sem.at[i * 2 + r, 8])
+        gathers[i, r, 1].start()
+
+    for i, r in chunks:
+        step(f"LN{i}{r}", i, r)(gather_first)
+        step(f"Gz{i}{r}", i, r)(gather_second)
+        for which in range(2):
+            step(f"GL{i}{r}{which}")(gathers[i, r, which].pass_left)
+            step(f"GR{i}{r}{which}")(gathers[i, r, which].pass_right)
 
     scaling = HD ** (-0.5)
     position = lax.broadcasted_iota(jnp.int32, (1, TXT + IMG), 1)
 
     def project(i):
+        for r in range(2):
+            for which in range(2):
+                gathers[i, r, which].finish()
+        if i == 0:
+            for n, d in enumerate((p.d, p.dl, p.dr, p.do)):
+                arrived(wall.at[d, :, pair_cols], share_sem.at[n])
         product = jnp.dot(
             normed[i].reshape(256, D), wall[...].reshape(D, 768), preferred_element_type=F32
         ).astype(BF)
@@ -494,10 +558,10 @@
         for n in range(3):
             joint[n, i, 1, :, p.c] = product[:, n * HD : (n + 1) * HD].reshape(8, ROWS, HD)
 
-    def project_wait(i):
-        arrived(joint.at[:, i, 1, :, p.co], qkv_sem.at[i])
-
     def attend(i, block):
+        if block == 0:
+            text_wait(i)
+            arrived(joint.at[:, i, 1, :, p.co], qkv_sem.at[i])
         slots = pl.ds(block % 2 * 4, 4)
         bias = jnp.where((position >= TXT) | (position < lengths[i]), 0.0, -jnp.inf)
         query = joint[0, i, block // 2, slots].reshape(BLOCK, HD)
@@ -536,21 +600,21 @@
             )
             both_grads[i, :, :, :384] = grads[i, :, p.c]
 
-    def back_project(i):
-        arrived(both_grads.at[i, :, :, pair_cols], grads_sem.at[i])
+    for i in range(2):
+        step(f"proj{i}", i)(project)
         for block in range(4):
+            step(f"att{i}{block}", i, block)(attend)
+
+    def back_project(i, h):
+        if h == 0:
+            arrived(both_grads.at[i, :, :, pair_cols], grads_sem.at[i])
+        for block in range(2 * h, 2 * h + 2):
             cols = pl.ds(block * 768, 768)
             product = lax.dot_general(
                 both_grads[i].reshape(256, 768), wall[block], NT, preferred_element_type=F32
             ).astype(BF)
             pair_sum[i, :, :, :, cols] = product.reshape(2, 4, ROWS, 768)
-            if block % 2:
-                round_y[i, 0].start(block // 2)
-        round_y[i, 0].direct()
-
-    half = lambda h: pl.ds(h * HALF, HALF)
-    part = lambda r: pl.ds(r * 16, 16)
-    chunks = [(i, r) for i in range(2) for r in range(2)]
+
     round_y = {
         (i, r): Scatter4(
             send,
@@ -567,24 +631,14 @@
         )
         for i, r in chunks
     }
-    rows_gather = {
-        (i, r): Gather4(
-            send,
-            lambda g, i=i, r=r: rows_all.at[:, g, i, part(r)],
-            lambda g, h, i=i, r=r: rows_all.at[h, g, i, part(r)],
-            gg_sem.at[i * 2 + r],
-            p.g,
-            p.gl,
-            p.gr,
-            p.go,
-            to_g,
-        )
-        for i, r in chunks
-    }
-
-    def back_next(i):
-        round_y[i, 0].pass_on()
-        round_y[i, 1].start()
+
+    def scatter_start(i, r):
+        round_y[i, r].start(0)
+        round_y[i, r].start(1)
+
+    def scatter_direct(i, r):
+        round_y[i, r].direct(1)
+        round_y[i, r].direct(0)
 
     def y_sum(i, r, z, h):
         return (
@@ -593,7 +647,7 @@
             + ry_right[i, h, z, part(r)].astype(F32)
         )
 
-    def back_second(i, r):
+    def scatter_cross(i, r):
         round_y[i, r].finish()
         for h in range(2):
             cross_out[i, part(r), half(h)] = y_sum(i, r, p.zo, h).astype(BF)
@@ -601,7 +655,7 @@
             cross_out.at[i, part(r)], cross_in.at[i, part(r)], cross_sem.at[i * 2 + r], **across
         )
 
-    def back_third(i, r):
+    def norm_back(i, r):
         mine = jnp.concatenate([y_sum(i, r, p.z, h) for h in range(2)], axis=1)
         standard, reciprocal = standardise(hidden[i, part(r)])
         arrived(cross_in.at[i, part(r)], cross_sem.at[i * 2 + r])
@@ -613,20 +667,58 @@
         )
         for c in range(2):
             rows_all[c, p.g, i, part(r)] = by_owner(residual_grad, c).astype(BF)
-        rows_gather[i, r].start()
-
-    def rows_pass(i, r):
-        rows_gather[i, r].pass_left()
-        rows_gather[i, r].pass_right()
-
-    def rows_finish(i, r):
-        rows_gather[i, r].finish()
-        send(
-            rows_all.at[p.co, :, i, part(r)],
-            rows_in.at[:, i, part(r)],
-            rows_sem.at[i * 2 + r],
-            **partner
-        )
+        if i == 0:
+            rows_gather[0, r].start()
+
+    def rows_at(c, g, i, n):
+        if i:
+            return rows_all.at[c, g, 1, :, pl.ds(n * 768, 768)]
+        return rows_all.at[c, g, 0, part(n)]
+
+    def rows_in_at(i, n):
+        if i:
+            return rows_in.at[:, 1, :, pl.ds(n * 768, 768)]
+        return rows_in.at[:, 0, part(n)]
+
+    every = slice(None)
+    rows_gather = {
+        (i, n): Gather4(
+            send,
+            lambda g, i=i, n=n: rows_at(every, g, i, n),
+            lambda g, h, i=i, n=n: rows_at(h, g, i, n),
+            gg_sem.at[i * 2 + n],
+            p.g,
+            p.gl,
+            p.gr,
+            p.go,
+            to_g,
+        )
+        for i, n in chunks
+    }
+
+    def rows_start(n):
+        if n:
+            send.sent(rows_gather[1, 0].begun)
+        rows_gather[1, n].start()
+
+    def rows_finish(i, n):
+        rows_gather[i, n].finish()
+        send(rows_at(p.co, every, i, n), rows_in_at(i, n), rows_sem.at[i * 2 + n], **partner)
+
+    for i in range(2):
+        step(f"bpa{i}", i, 0)(back_project)
+        step(f"bpb{i}", i, 1)(back_project)
+        step(f"AS1{i}", i)(rows_start)
+    for i, r in chunks:
+        step(f"Bs{i}{r}", i, r)(scatter_start)
+        step(f"Bd{i}{r}", i, r)(scatter_direct)
+        for h in range(2):
+            step(f"Bp{h}{i}{r}", h)(round_y[i, r].pass_on)
+        step(f"BX{i}{r}", i, r)(scatter_cross)
+        step(f"BL{i}{r}", i, r)(norm_back)
+        step(f"AL{i}{r}")(rows_gather[i, r].pass_left)
+        step(f"AR{i}{r}")(rows_gather[i, r].pass_right)
+        step(f"Af{i}{r}", i, r)(rows_finish)
 
     def attn_pairs(to):
         near = pl.ds(pl.multiple_of((p.z * 8 + to) * ROWS, ROWS), ROWS)
@@ -652,7 +744,8 @@
             for n, (src, dst, recv) in enumerate(attn_pairs(to))
         ]
 
-    def attn_first_hop():
+    @step("O1")
+    def _():
         @pl.loop(1, 8)
         def _(k):
             for copy in attn_copies(k):
@@ -664,7 +757,8 @@
     half_cols = pl.ds(pl.multiple_of(p.z * 1024, 1024), 1024)
     other_cols = pl.ds(pl.multiple_of(p.zo * 1024, 1024), 1024)
 
-    def attn_second_hop():
+    @step("O2")
+    def _():
         arrived(ostage, attn_recv.at[1])
         send(ostage, attn_out.at[:, :, :, half_cols], attn_recv.at[2], **across)
 
@@ -692,78 +786,16 @@
             z, y = block // 2, block % 2 * 2
             zsum[z, pl.ds(y, 2)] = (zacc[cols] + product).astype(BF).reshape(2, 192, 768)
 
-    to_group[0].finish()
-    gather_first(0)
-    to_group[1].pass_on()
-    gather_third(0, 0)
-    gather_second(0)
-    gather_fourth(0, 0)
-    gather_third(0, 1)
-    arrived(tstage, stage_recv.at[0])
-    arrived(cstage, stage_recv.at[1])
-    text_second_hop(0)
-    to_group[1].finish()
-    gather_first(1)
-    weights.finish()
-    share_weight(p.do, 3)
-    gather_fourth(0, 1)
-    for n, d in enumerate((p.d, p.dl, p.dr, p.do)):
-        arrived(wall.at[d, :, pair_cols], share_sem.at[n])
-    project(0)
-    gather_third(1, 0)
-    gather_second(1)
-    text_second_hop(1)
-    arrived(joint.at[:, :, 0, plane], text_recv.at[0])
-    arrived(cots.at[:, :, plane], text_recv.at[1])
-    text_wait(0)
-    project_wait(0)
-    attend(0, 0)
-    gather_fourth(1, 0)
-    attend(0, 1)
-    gather_third(1, 1)
-    attend(0, 2)
-    attend(0, 3)
-    gather_fourth(1, 1)
-    project(1)
-    back_project(0)
-    text_wait(1)
-    project_wait(1)
-    attend(1, 0)
-    attend(1, 1)
-    back_next(0)
-    attend(1, 2)
-    back_second(0, 0)
-    round_y[0, 1].direct()
-    attend(1, 3)
-    round_y[0, 1].pass_on()
-    back_third(0, 0)
-    back_project(1)
-    back_second(0, 1)
-    rows_pass(0, 0)
-    back_third(0, 1)
-    back_next(1)
-    rows_pass(0, 1)
-    back_second(1, 0)
-    round_y[1, 1].direct()
-    round_y[1, 1].pass_on()
-    back_third(1, 0)
-    rows_finish(0, 0)
-    back_second(1, 1)
-    attn_first_hop()
-    back_third(1, 1)
-    rows_pass(1, 0)
-    rows_finish(0, 1)
-    arrived(ctl_in, share_sem.at[4])
-    control_part(0)
-    rows_pass(1, 1)
-    for r in range(2):
-        arrived(rows_in.at[:, 0, part(r)], rows_sem.at[r])
-    for block in range(4):
-        zero_part(0, block)
-    rows_finish(1, 0)
-    rows_finish(1, 1)
-    for r in range(2):
-        arrived(rows_in.at[:, 1, part(r)], rows_sem.at[2 + r])
+    step("ctl0", 0)(control_part)
+    step("ctl1", 1)(control_part)
+
+    @step("zp0")
+    def _():
+        arrived(ctl_in, share_sem.at[4])
+        for n in range(2):
+            arrived(rows_in_at(0, n), rows_sem.at[n])
+        for block in range(4):
+            zero_part(0, block)
 
     cols_a, cols_b = pl.ds(0, 384), pl.ds(384, 384)
     quarter = lambda d: pl.ds(pl.multiple_of(d * 48, 16), 48)
@@ -793,57 +825,86 @@
         p.yo,
         to_y,
     )
-    for z in range(2):
+    def zero_send(z):
+        arrived(rows_in_at(1, z), rows_sem.at[2 + z])
         zero_part(1, 2 * z)
         zero_part(1, 2 * z + 1)
         round_x.start(z)
         zero_y.start(z)
-    round_x.direct()
-    zero_y.direct()
-    attn_second_hop()
-    control_part(1)
-    round_x.pass_on()
-    zero_y.pass_on()
-    round_x.finish()
-    for z in range(2):
-        za_out[z] = (
-            zsum[z, :, quarter(p.d), cols_a].astype(F32)
-            + zx_left[z].astype(F32)
-            + zx_right[z].astype(F32)
-        ).astype(BF)
-    others_a = [(dz, dy) for dz in range(2) for dy in range(4) if dz or dy]
-    for n, (dz, dy) in enumerate(others_a):
-        z, y = (p.z + dz) % 2, (p.y + dy) % 4
-        send(za_out.at[z, y], za_in.at[n], za_sem.at[n], seq=p.seq(z, y, p.c))
-    zero_y.finish()
-    for z in range(2):
-        zb_out[z] = (
-            (
-                zsum[z, p.y, :, cols_b].astype(F32)
-                + zy_left[z].astype(F32)
-                + zy_right[z].astype(F32)
+        round_x.direct(z)
+        zero_y.direct(z)
+
+    step("zp1a", 0)(zero_send)
+    step("zp1b", 1)(zero_send)
+    for h in range(2):
+        step(f"Zp{h}x", h)(round_x.pass_on)
+        step(f"Zp{h}y", h)(zero_y.pass_on)
+    others = [(dz, dy) for dz in range(2) for dy in range(4) if dz or dy]
+
+    @step("ZA")
+    def _():
+        round_x.finish()
+        for z in range(2):
+            za_out[z] = (
+                zsum[z, :, quarter(p.d), cols_a].astype(F32)
+                + zx_left[z].astype(F32)
+                + zx_right[z].astype(F32)
+            ).astype(BF)
+        for n, (dz, dy) in enumerate(others):
+            z, y = (p.z + dz) % 2, (p.y + dy) % 4
+            send(za_out.at[z, y], za_in.at[n], za_sem.at[n], seq=p.seq(z, y, p.c))
+
+    @step("ZB")
+    def _():
+        zero_y.finish()
+        for z in range(2):
+            zb_out[z] = (
+                (
+                    zsum[z, p.y, :, cols_b].astype(F32)
+                    + zy_left[z].astype(F32)
+                    + zy_right[z].astype(F32)
+                )
+                .astype(BF)
+                .reshape(4, 48, 384)
             )
-            .astype(BF)
-            .reshape(4, 48, 384)
-        )
-    for n, (dz, dd) in enumerate(others_a):
-        z, d = (p.z + dz) % 2, (p.d + dd) % 4
-        send(zb_out.at[z, d], zb_in.at[n], zb_sem.at[n], seq=p.seq(z, p.y, p.c), dp=d)
-    total = za_out[p.z, p.y].astype(F32)
-    for n in range(7):
-        arrived(za_in.at[n], za_sem.at[n])
-        total = total + za_in[n].astype(F32)
-    zown[:, cols_a] = total.astype(BF)
-    total = zb_out[p.z, p.d].astype(F32)
-    for n in range(7):
-        arrived(zb_in.at[n], zb_sem.at[n])
-        total = total + zb_in[n].astype(F32)
-    zown[:, cols_b] = total.astype(BF)
-    for k in range(1, 4):
-        send(zown, zall.at[p.d], zg_sem.at[k - 1], dp=(p.d + k) % 4)
-    zall[p.d] = zown[...]
-    for k in range(1, 4):
-        arrived(zall.at[(p.d + 4 - k) % 4], zg_sem.at[k - 1])
+        for n, (dz, dd) in enumerate(others):
+            z, d = (p.z + dz) % 2, (p.d + dd) % 4
+            send(zb_out.at[z, d], zb_in.at[n], zb_sem.at[n], seq=p.seq(z, p.y, p.c), dp=d)
+
+    zero_gather = Gather4(
+        send,
+        lambda d: zall.at[d],
+        lambda d, h: zall.at[d, :, pl.ds(h * 384, 384)],
+        zg_sem,
+        p.d,
+        p.dl,
+        p.dr,
+        p.do,
+        to_d,
+    )
+
+    @step("ZS")
+    def _():
+        total = za_out[p.z, p.y].astype(F32)
+        for n in range(7):
+            arrived(za_in.at[n], za_sem.at[n])
+            total = total + za_in[n].astype(F32)
+        zall[p.d, :, cols_a] = total.astype(BF)
+        total = zb_out[p.z, p.d].astype(F32)
+        for n in range(7):
+            arrived(zb_in.at[n], zb_sem.at[n])
+            total = total + zb_in[n].astype(F32)
+        zall[p.d, :, cols_b] = total.astype(BF)
+        zero_gather.start()
+
+    step("zgL_")(zero_gather.pass_left)
+    step("zgR_")(zero_gather.pass_right)
+
+    for name in ORDER:
+        steps.pop(name)()
+    assert not steps
+
+    zero_gather.finish()
     zero_out[...] = zall[...].reshape(192, 768).astype(F32) * (16384 ** (-0.5))
 
     arrived(attn_out.at[:, :, :, half_cols], attn_recv.at[0])
@@ -852,8 +913,9 @@
 
     @pl.loop(1, 8)
     def _(k):
-        for copy in text_copies(k):
-            copy.wait_send()
+        for i in range(2):
+            for copy in text_copies(i, k):
+                copy.wait_send()
         for copy in attn_copies(k):
             copy.wait_send()
 
@@ -916,19 +978,18 @@
             bf(2, 4, 48, 384),
             bf(7, 48, 384),
             bf(7, 48, 384),
-            bf(48, 768),
             bf(4, 48, 768),
             bf(3, 2, ROWS, HEADS * HD),
             bf(2, 2, ROWS, HEADS * HD),
             dma((32,)),
-            dma((176,)),
+            dma((224,)),
             dma((4,)),
             dma((5,)),
-            dma((2, 6)),
-            dma((2, 9)),
-            dma((4, 8)),
-            dma((2,)),
-            dma((2,)),
+            dma((4, 6)),
+            dma((4, 9)),
+            dma((4, 2, 8)),
+            dma((2, 2)),
+            dma((2, 2)),
             dma((2, 2)),
             dma((2,)),
             dma((2,)),
@@ -942,7 +1003,7 @@
             dma((6,)),
             dma((7,)),
             dma((7,)),
-            dma((3,)),
+            dma((4,)),
         ],
         compiler_params=pltpu.CompilerParams(
             collective_id=1, has_side_effects=True, vmem_limit_bytes=VMEM_LIMIT

time: 168 us -> 160 us (0.952)
  Pallas kernels: 166 us -> 156 us
    pallas_call x1, Pallas kernels: 163 us -> 154 us  [whole_block(): pl.pallas_call(block_kernel, out_shape=(jax.ShapeDtypeStruct((2, 2, ROWS,...]
where the time goes in v5:
time: 160 us; the launch traced here: 158 us
  Pallas kernels  156 us (98%)
    pallas_call x1, Pallas kernels, whole_block(): pl.pallas_call(block_kernel, out_shape=(jax.ShapeDtypeStruct((2, 2, ROWS,...  154 us

profile of v5, /device:TPU:32, one launch (start us, length us, event | category | flops | bytes accessed | tf_op | source)
XLA Modules:
  0.0 158.3 jit_solution(15659566919690881866)
XLA Ops:
  0.6 0.7 convert_bitcast_fusion
  1.3 0.1 multiply_cosine_fusion
  1.4 0.6 fusion.activated
  2.0 153.6 %whole_block.1 = (bf16[2,2,32,2048]{3,2,1,0:T(8,128)(2,1)}, bf16[4,2,32,768]{3,2,1,0:T(8,128)(2,1)}, f32[192,768]{1,0:T(8,128)}) custom-call(s32[2]{0:T(128)} %bitcast.25, bf16[2,256]{1,0:T(2,128)(2,1)} %fusion.activated, bf16[256,6144]{1,0:T(8,128)(2,1)} %mod_weight.1, bf16[4,2,32,768]{3,2,1,0:T(8,128)(2,1)} %bitcast.21, bf16[768,3072]{1,0:T(8,128)(2,1)} %zero_weight.1, ...), custom_call_target="tpu_custom_call" | custom-call | tf_op jit(solution)/shard_map/whole_block/pallas_call | solution.py:926
  155.7 2.5 %hand_over.1 = (bf16[2,32,2048]{2,1,0:T(8,128)(2,1)}, bf16[2,32,2048]{2,1,0:T(8,128)(2,1)}, bf16[4,2,32,768]{3,2,1,0:T(8,128)(2,1)}, f32[192,768]{1,0:T(8,128)}) custom-call(bf16[2,2,32,2048]{3,2,1,0:T(8,128)(2,1)} %get-tuple-element.11.attn, bf16[4,2,32,768]{3,2,1,0:T(8,128)(2,1)} %get-tuple-element.12.control, f32[192,768]{1,0:T(8,128)} %get-tuple-element.13.zero), custom_call_target="tpu_custom_call" | custom-call | tf_op jit(solution)/shard_map/hand_over/pallas_call | solution.py:1034
  (1 shorter events, 0.0 us)

commit v6 on v5

--- a/solution.py
+++ b/solution.py
@@ -157,17 +157,17 @@
 
 
 ORDER = (
-    "res0", "res1", "Rs00", "T10", "Ws", "mod", "zwo", "Rp000", "Rp100", "Rs01", "LN00", "GL000",
-    "GR000", "Rp001", "Rp101", "WL", "WR_", "Gz00", "Rs10", "LN01", "T20", "T11", "GR001",
-    "GL001", "Wf", "Rp010", "Rp110", "Gz01", "Rs11", "LN10", "GL010", "GR010", "GR011", "GL011",
-    "GL100", "GR100", "Rp011", "Rp111", "proj0", "Gz10", "LN11", "att00", "att01", "GL101",
-    "Gz11", "att02", "att03", "T21", "GL110", "GR101", "GR110", "GR111", "bpa0", "GL111", "bpb0",
-    "Bs00", "Bd00", "proj1", "Bp100", "Bp000", "att10", "Bs01", "att11", "att12", "Bd01", "att13",
-    "BX00", "Bp101", "Bp001", "bpa1", "bpb1", "Bs10", "Bd10", "BL00", "BX01", "Bp110", "Bp010",
-    "Bs11", "Bd11", "AL00", "AR00", "BL01", "Af00", "Bp111", "BX10", "Bp011", "AL01", "AR01",
-    "BX11", "O1", "BL10", "Af01", "ctl0", "BL11", "AS10", "zp0", "AS11", "AL10", "AR10", "Af10",
-    "AL11", "AR11", "zp1a", "Af11", "ctl1", "zp1b", "Zp0y", "Zp0x", "O2", "Zp1x", "Zp1y", "ZA",
-    "ZB", "ZS", "zgL_", "zgR_",
+    "res0", "res1", "Rs00", "T10", "Ws", "Rp000", "Rp100", "Rs01", "mod", "LN00", "Rp101",
+    "Rp001", "T11", "WL", "Rs10", "GR000", "WR_", "LN01", "zwo", "T20", "Gz00", "GL000", "Rp110",
+    "Rp010", "GR001", "Gz01", "Rs11", "Wf", "LN10", "GL010", "GL001", "GR011", "GR100", "GR010",
+    "GL011", "Rp111", "Rp011", "GL100", "proj0", "Gz10", "LN11", "att00", "att01", "Gz11",
+    "att02", "att03", "GR101", "GL101", "T21", "GR111", "GL111", "GL110", "GR110", "bpa0", "bpb0",
+    "Bs00", "proj1", "Bd00", "Bp100", "Bp000", "att10", "att11", "att12", "Bs01", "att13", "BX00",
+    "Bd01", "bpa1", "Bp001", "Bp101", "BL00", "bpb1", "Bs10", "BX01", "Bd10", "Bp010", "Bp110",
+    "Bs11", "AR00", "AL00", "BL01", "Bd11", "Bp011", "BX10", "Bp111", "AL01", "AR01", "BX11",
+    "Af00", "Af01", "BL10", "BL11", "AS10", "O1", "AS11", "AL10", "AR10", "zp0", "Af10", "AL11",
+    "AR11", "zp1a", "Af11", "zp1b", "Zp0y", "Zp0x", "Zp1x", "ctl1", "Zp1y", "ctl0", "ZA", "ZB",
+    "ZS", "zgL_", "zgR_", "O2",
 )
 NT = (((1,), (1,)), ((), ()))
 TN = (((0,), (0,)), ((), ()))
@@ -183,7 +183,7 @@
 
 def block_kernel(
     lengths,
-    activated,
+    timesteps,
     mod_weight,
     control,
     zero_weight,
@@ -335,8 +335,10 @@
                 ctl[...].reshape(256, 768), zw[:, cols], preferred_element_type=F32
             )
             partial[:, :, :, cols] = product.astype(BF).reshape(4, 2, ROWS, 512)
-        if h == 1:
+        if h == 0:
             all_here()
+            to_group[0, 0].start(0)
+            to_group[0, 0].direct(0)
 
     step("res0", 0)(residual_part)
     step("res1", 1)(residual_part)
@@ -362,10 +364,11 @@
         if n:
             send.sent(to_group[chunks[n - 1]].passed)
         scatter = to_group[chunks[n]]
-        for h in range(2):
+        for h in range(0 if n else 1, 2):
             scatter.start(h)
         scatter.direct(1)
-        scatter.direct(0)
+        if n:
+            scatter.direct(0)
 
     for n, (i, r) in enumerate(chunks):
         step(f"Rs{i}{r}", n)(group_start)
@@ -472,11 +475,16 @@
     def _():
         for copy in load_mod:
             copy.wait()
+        lane = lax.broadcasted_iota(jnp.int32, (1, FREQ // 2), 1).astype(F32)
+        frequency = jnp.exp(lane * (-math.log(10000.0) / (FREQ // 2)))
+        angles = jnp.concatenate([timesteps[i].astype(F32) * frequency for i in range(2)])
+        embedding = jnp.concatenate([jnp.cos(angles), jnp.sin(angles)], axis=1)
+        activated = (embedding / (1.0 + jnp.exp(-embedding))).astype(BF)
         offset[...] = jnp.dot(
-            activated[...], pair_sum[0].reshape(FREQ, D), preferred_element_type=F32
+            activated, pair_sum[0].reshape(FREQ, D), preferred_element_type=F32
         )
         stretch[...] = 1.0 + jnp.dot(
-            activated[...], pair_sum[1].reshape(FREQ, D), preferred_element_type=F32
+            activated, pair_sum[1].reshape(FREQ, D), preferred_element_type=F32
         )
         load_base.wait()
 
@@ -540,7 +548,6 @@
             step(f"GR{i}{r}{which}")(gathers[i, r, which].pass_right)
 
     scaling = HD ** (-0.5)
-    position = lax.broadcasted_iota(jnp.int32, (1, TXT + IMG), 1)
 
     def project(i):
         for r in range(2):
@@ -563,26 +570,43 @@
             text_wait(i)
             arrived(joint.at[:, i, 1, :, p.co], qkv_sem.at[i])
         slots = pl.ds(block % 2 * 4, 4)
-        bias = jnp.where((position >= TXT) | (position < lengths[i]), 0.0, -jnp.inf)
         query = joint[0, i, block // 2, slots].reshape(BLOCK, HD)
         cot = cots[block // 2, i, slots].reshape(BLOCK, HD)
         keys = joint[1, i].reshape(TXT + IMG, HD)
         values = joint[2, i].reshape(TXT + IMG, HD)
-        scores = lax.dot_general(query, keys, NT, preferred_element_type=F32) + bias
-        row_max = jnp.max(scores, axis=1, keepdims=True)
-        terms = jnp.exp2((scores - row_max) * (scaling * math.log2(math.e)))
-        prob = terms * (1.0 / jnp.sum(terms, axis=1, keepdims=True))
-        low = prob.astype(BF)
-        attended = jnp.dot(low, values, preferred_element_type=F32).astype(BF)
-        attn[block // 2, i, pl.ds(block % 2 * BLOCK, BLOCK)] = attended
-        dots = jnp.sum(cot.astype(F32) * attended.astype(F32), axis=1, keepdims=True)
-        prob_grad = lax.dot_general(cot, values, NT, preferred_element_type=F32)
-        score_grad = (prob * (prob_grad - dots)).astype(BF)
+        scores = lax.dot_general(keys, query, NT, preferred_element_type=F32)
+        text_live = lax.broadcasted_iota(jnp.int32, (TXT, 1), 0) < lengths[i]
+        text_scores = jnp.where(text_live, scores[:TXT], -jnp.inf)
+        image_scores = scores[TXT:]
+        col_max = jnp.maximum(
+            jnp.max(text_scores, axis=0, keepdims=True),
+            jnp.max(image_scores, axis=0, keepdims=True),
+        )
+        rate = scaling * math.log2(math.e)
+        text_terms = jnp.exp2((text_scores - col_max) * rate)
+        image_terms = jnp.exp2((image_scores - col_max) * rate)
+        share = 1.0 / (
+            jnp.sum(text_terms, axis=0, keepdims=True) + jnp.sum(image_terms, axis=0, keepdims=True)
+        )
+        text_prob, image_prob = text_terms * share, image_terms * share
+        image_low = image_prob.astype(BF)
+        attended = lax.dot_general(
+            values[:TXT], text_prob.astype(BF), TN, preferred_element_type=F32
+        ) + lax.dot_general(values[TXT:], image_low, TN, preferred_element_type=F32)
+        low_attended = attended.astype(BF).astype(F32)
+        attn[block // 2, i, pl.ds(block % 2 * BLOCK, BLOCK)] = low_attended.T.astype(BF)
+        dots = jnp.sum(cot.astype(F32).T * low_attended, axis=0, keepdims=True)
+        prob_grad = lax.dot_general(values, cot, NT, preferred_element_type=F32)
+        image_grad = (image_prob * (prob_grad[TXT:] - dots)).astype(BF)
         if block >= 2:
-            query_grad = jnp.dot(score_grad, keys, preferred_element_type=F32) * scaling
-            grads[i, slots, :, :, :HD] = query_grad.astype(BF).reshape(4, 2, ROWS, HD)
-        key_part = lax.dot_general(score_grad[:, TXT:], query, TN, preferred_element_type=F32)
-        value_part = lax.dot_general(low[:, TXT:], cot, TN, preferred_element_type=F32)
+            text_grad = (text_prob * (prob_grad[:TXT] - dots)).astype(BF)
+            query_grad = lax.dot_general(
+                keys[:TXT], text_grad, TN, preferred_element_type=F32
+            ) + lax.dot_general(keys[TXT:], image_grad, TN, preferred_element_type=F32)
+            query_grad = (query_grad * scaling).T.astype(BF)
+            grads[i, slots, :, :, :HD] = query_grad.reshape(4, 2, ROWS, HD)
+        key_part = jnp.dot(image_grad, query, preferred_element_type=F32)
+        value_part = jnp.dot(image_low, cot, preferred_element_type=F32)
         if block == 0:
             key_acc[...] = key_part
             value_acc[...] = value_part
@@ -930,7 +954,7 @@
             jax.ShapeDtypeStruct((4, 2, ROWS, 768), BF),
             jax.ShapeDtypeStruct((192, 768), F32),
         ),
-        in_specs=[pl.BlockSpec(memory_space=pltpu.SMEM), VMEM] + [ANY] * 8,
+        in_specs=[pl.BlockSpec(memory_space=pltpu.SMEM)] * 2 + [ANY] * 8,
         out_specs=(VMEM, VMEM, VMEM),
         scratch_shapes=[
             bf(4, 2, ROWS, 768),
@@ -1046,14 +1070,6 @@
     )(attn, control, zero)
 
 
-def timestep_activation(timesteps):
-    half_freq = FREQ // 2
-    frequency = jnp.exp(-math.log(10000.0) * jnp.arange(half_freq, dtype=F32) / half_freq)
-    angles = timesteps.astype(F32)[..., None] * frequency
-    embedding = jnp.concatenate([jnp.cos(angles), jnp.sin(angles)], axis=-1)
-    return jax.nn.silu(embedding).astype(BF)
-
-
 def body(
     image_hidden,
     control_hidden,
@@ -1066,10 +1082,9 @@
     image_cotangent,
     text_cotangent,
 ):
-    activated = timestep_activation(timesteps.reshape(2))
     attn_out, control_grad, zero_t = whole_block(
         text_lengths.reshape(2),
-        activated,
+        timesteps.reshape(2),
         mod_weight,
         control_hidden.reshape(4, 2, ROWS, 768),
         zero_weight,

time: 160 us -> 163 us (1.019)
  Pallas kernels: 156 us -> 162 us
    pallas_call x1, Pallas kernels: 154 us -> 159 us  [whole_block(): pl.pallas_call(block_kernel, out_shape=(jax.ShapeDtypeStruct((2, 2, ROWS,...]
where the time goes in v6:
time: 163 us
  Pallas kernels  162 us (99%)
    pallas_call x1, Pallas kernels, whole_block(): pl.pallas_call(block_kernel, out_shape=(jax.ShapeDtypeStruct((2, 2, ROWS,...  159 us

profile of v6, /device:TPU:32, one launch (start us, length us, event | category | flops | bytes accessed | tf_op | source)
XLA Modules:
  0.0 162.5 jit_solution(3966562636648416005)
XLA Ops:
  0.6 159.2 %whole_block.1 = (bf16[2,2,32,2048]{3,2,1,0:T(8,128)(2,1)}, bf16[4,2,32,768]{3,2,1,0:T(8,128)(2,1)}, f32[192,768]{1,0:T(8,128)}) custom-call(s32[2]{0:T(128)} %bitcast.24, s32[2]{0:T(128)} %bitcast.25, bf16[256,6144]{1,0:T(8,128)(2,1)} %mod_weight.1, bf16[4,2,32,768]{3,2,1,0:T(8,128)(2,1)} %bitcast.20, bf16[768,3072]{1,0:T(8,128)(2,1)} %zero_weight.1, ...), custom_call_target="tpu_custom_call" | custom-call | tf_op jit(solution)/shard_map/whole_block/pallas_call | solution.py:950
  159.9 2.5 %hand_over.1 = (bf16[2,32,2048]{2,1,0:T(8,128)(2,1)}, bf16[2,32,2048]{2,1,0:T(8,128)(2,1)}, bf16[4,2,32,768]{3,2,1,0:T(8,128)(2,1)}, f32[192,768]{1,0:T(8,128)}) custom-call(bf16[2,2,32,2048]{3,2,1,0:T(8,128)(2,1)} %get-tuple-element.11.attn, bf16[4,2,32,768]{3,2,1,0:T(8,128)(2,1)} %get-tuple-element.12.control, f32[192,768]{1,0:T(8,128)} %get-tuple-element.13.zero), custom_call_target="tpu_custom_call" | custom-call | tf_op jit(solution)/shard_map/hand_over/pallas_call | solution.py:1058

commit v7 on v5

--- a/solution.py
+++ b/solution.py
@@ -157,17 +157,17 @@
 
 
 ORDER = (
-    "res0", "res1", "Rs00", "T10", "Ws", "mod", "zwo", "Rp000", "Rp100", "Rs01", "LN00", "GL000",
+    "res0", "res1", "Rs00", "T10", "Ws", "mod", "Rp000", "Rp100", "Rs01", "LN00", "GL000",
     "GR000", "Rp001", "Rp101", "WL", "WR_", "Gz00", "Rs10", "LN01", "T20", "T11", "GR001",
     "GL001", "Wf", "Rp010", "Rp110", "Gz01", "Rs11", "LN10", "GL010", "GR010", "GR011", "GL011",
     "GL100", "GR100", "Rp011", "Rp111", "proj0", "Gz10", "LN11", "att00", "att01", "GL101",
     "Gz11", "att02", "att03", "T21", "GL110", "GR101", "GR110", "GR111", "bpa0", "GL111", "bpb0",
     "Bs00", "Bd00", "proj1", "Bp100", "Bp000", "att10", "Bs01", "att11", "att12", "Bd01", "att13",
     "BX00", "Bp101", "Bp001", "bpa1", "bpb1", "Bs10", "Bd10", "BL00", "BX01", "Bp110", "Bp010",
-    "Bs11", "Bd11", "AL00", "AR00", "BL01", "Af00", "Bp111", "BX10", "Bp011", "AL01", "AR01",
-    "BX11", "O1", "BL10", "Af01", "ctl0", "BL11", "AS10", "zp0", "AS11", "AL10", "AR10", "Af10",
-    "AL11", "AR11", "zp1a", "Af11", "ctl1", "zp1b", "Zp0y", "Zp0x", "O2", "Zp1x", "Zp1y", "ZA",
-    "ZB", "ZS", "zgL_", "zgR_",
+    "Bs11", "Bd11", "AL00", "AR00", "BL01", "zwo", "Af00", "Bp111", "BX10", "Bp011", "AL01",
+    "AR01", "BX11", "O1", "BL10", "Af01", "ctl0", "BL11", "AS10", "zp0", "AS11", "AL10", "AR10",
+    "Af10", "AL11", "AR11", "zp1a", "Af11", "ctl1", "zp1b", "Zp0y", "Zp0x", "O2", "Zp1x", "Zp1y",
+    "ZA", "ZB", "ZS", "zgL_", "zgR_",
 )
 NT = (((1,), (1,)), ((), ()))
 TN = (((0,), (0,)), ((), ()))
@@ -183,7 +183,7 @@
 
 def block_kernel(
     lengths,
-    activated,
+    timesteps,
     mod_weight,
     control,
     zero_weight,
@@ -335,8 +335,10 @@
                 ctl[...].reshape(256, 768), zw[:, cols], preferred_element_type=F32
             )
             partial[:, :, :, cols] = product.astype(BF).reshape(4, 2, ROWS, 512)
-        if h == 1:
+        if h == 0:
             all_here()
+            to_group[0, 0].start(0)
+            to_group[0, 0].direct(0)
 
     step("res0", 0)(residual_part)
     step("res1", 1)(residual_part)
@@ -362,10 +364,11 @@
         if n:
             send.sent(to_group[chunks[n - 1]].passed)
         scatter = to_group[chunks[n]]
-        for h in range(2):
+        for h in range(0 if n else 1, 2):
             scatter.start(h)
         scatter.direct(1)
-        scatter.direct(0)
+        if n:
+            scatter.direct(0)
 
     for n, (i, r) in enumerate(chunks):
         step(f"Rs{i}{r}", n)(group_start)
@@ -472,11 +475,16 @@
     def _():
         for copy in load_mod:
             copy.wait()
+        lane = lax.broadcasted_iota(jnp.int32, (1, FREQ // 2), 1).astype(F32)
+        frequency = jnp.exp(lane * (-math.log(10000.0) / (FREQ // 2)))
+        angles = jnp.concatenate([timesteps[i].astype(F32) * frequency for i in range(2)])
+        embedding = jnp.concatenate([jnp.cos(angles), jnp.sin(angles)], axis=1)
+        activated = (embedding / (1.0 + jnp.exp(-embedding))).astype(BF)
         offset[...] = jnp.dot(
-            activated[...], pair_sum[0].reshape(FREQ, D), preferred_element_type=F32
+            activated, pair_sum[0].reshape(FREQ, D), preferred_element_type=F32
         )
         stretch[...] = 1.0 + jnp.dot(
-            activated[...], pair_sum[1].reshape(FREQ, D), preferred_element_type=F32
+            activated, pair_sum[1].reshape(FREQ, D), preferred_element_type=F32
         )
         load_base.wait()
 
@@ -930,7 +938,7 @@
             jax.ShapeDtypeStruct((4, 2, ROWS, 768), BF),
             jax.ShapeDtypeStruct((192, 768), F32),
         ),
-        in_specs=[pl.BlockSpec(memory_space=pltpu.SMEM), VMEM] + [ANY] * 8,
+        in_specs=[pl.BlockSpec(memory_space=pltpu.SMEM)] * 2 + [ANY] * 8,
         out_specs=(VMEM, VMEM, VMEM),
         scratch_shapes=[
             bf(4, 2, ROWS, 768),
@@ -1046,14 +1054,6 @@
     )(attn, control, zero)
 
 
-def timestep_activation(timesteps):
-    half_freq = FREQ // 2
-    frequency = jnp.exp(-math.log(10000.0) * jnp.arange(half_freq, dtype=F32) / half_freq)
-    angles = timesteps.astype(F32)[..., None] * frequency
-    embedding = jnp.concatenate([jnp.cos(angles), jnp.sin(angles)], axis=-1)
-    return jax.nn.silu(embedding).astype(BF)
-
-
 def body(
     image_hidden,
     control_hidden,
@@ -1066,10 +1066,9 @@
     image_cotangent,
     text_cotangent,
 ):
-    activated = timestep_activation(timesteps.reshape(2))
     attn_out, control_grad, zero_t = whole_block(
         text_lengths.reshape(2),
-        activated,
+        timesteps.reshape(2),
         mod_weight,
         control_hidden.reshape(4, 2, ROWS, 768),
         zero_weight,

time: 160 us -> 161 us (level)
  Pallas kernels: 156 us -> 159 us
    pallas_call x1, Pallas kernels: 154 us -> 156 us  [whole_block(): pl.pallas_call(block_kernel, out_shape=(jax.ShapeDtypeStruct((2, 2, ROWS,...]
where the time goes in v7:
time: 161 us; the launch traced here: 159 us
  Pallas kernels  159 us (99%)
    pallas_call x1, Pallas kernels, whole_block(): pl.pallas_call(block_kernel, out_shape=(jax.ShapeDtypeStruct((2, 2, ROWS,...  156 us

profile of v7, /device:TPU:32, one launch (start us, length us, event | category | flops | bytes accessed | tf_op | source)
XLA Modules:
  0.0 159.4 jit_solution(4984449787740776405)
XLA Ops:
  0.6 156.1 %whole_block.1 = (bf16[2,2,32,2048]{3,2,1,0:T(8,128)(2,1)}, bf16[4,2,32,768]{3,2,1,0:T(8,128)(2,1)}, f32[192,768]{1,0:T(8,128)}) custom-call(s32[2]{0:T(128)} %bitcast.24, s32[2]{0:T(128)} %bitcast.25, bf16[256,6144]{1,0:T(8,128)(2,1)} %mod_weight.1, bf16[4,2,32,768]{3,2,1,0:T(8,128)(2,1)} %bitcast.20, bf16[768,3072]{1,0:T(8,128)(2,1)} %zero_weight.1, ...), custom_call_target="tpu_custom_call" | custom-call | tf_op jit(solution)/shard_map/whole_block/pallas_call | solution.py:934
  156.7 2.5 %hand_over.1 = (bf16[2,32,2048]{2,1,0:T(8,128)(2,1)}, bf16[2,32,2048]{2,1,0:T(8,128)(2,1)}, bf16[4,2,32,768]{3,2,1,0:T(8,128)(2,1)}, f32[192,768]{1,0:T(8,128)}) custom-call(bf16[2,2,32,2048]{3,2,1,0:T(8,128)(2,1)} %get-tuple-element.11.attn, bf16[4,2,32,768]{3,2,1,0:T(8,128)(2,1)} %get-tuple-element.12.control, f32[192,768]{1,0:T(8,128)} %get-tuple-element.13.zero), custom_call_target="tpu_custom_call" | custom-call | tf_op jit(solution)/shard_map/hand_over/pallas_call | solution.py:1042

commit v8 on v7

--- a/solution.py
+++ b/solution.py
@@ -157,17 +157,17 @@
 
 
 ORDER = (
-    "res0", "res1", "Rs00", "T10", "Ws", "mod", "Rp000", "Rp100", "Rs01", "LN00", "GL000",
-    "GR000", "Rp001", "Rp101", "WL", "WR_", "Gz00", "Rs10", "LN01", "T20", "T11", "GR001",
-    "GL001", "Wf", "Rp010", "Rp110", "Gz01", "Rs11", "LN10", "GL010", "GR010", "GR011", "GL011",
-    "GL100", "GR100", "Rp011", "Rp111", "proj0", "Gz10", "LN11", "att00", "att01", "GL101",
-    "Gz11", "att02", "att03", "T21", "GL110", "GR101", "GR110", "GR111", "bpa0", "GL111", "bpb0",
-    "Bs00", "Bd00", "proj1", "Bp100", "Bp000", "att10", "Bs01", "att11", "att12", "Bd01", "att13",
-    "BX00", "Bp101", "Bp001", "bpa1", "bpb1", "Bs10", "Bd10", "BL00", "BX01", "Bp110", "Bp010",
-    "Bs11", "Bd11", "AL00", "AR00", "BL01", "zwo", "Af00", "Bp111", "BX10", "Bp011", "AL01",
-    "AR01", "BX11", "O1", "BL10", "Af01", "ctl0", "BL11", "AS10", "zp0", "AS11", "AL10", "AR10",
-    "Af10", "AL11", "AR11", "zp1a", "Af11", "ctl1", "zp1b", "Zp0y", "Zp0x", "O2", "Zp1x", "Zp1y",
-    "ZA", "ZB", "ZS", "zgL_", "zgR_",
+    "res0", "res1", "Rs00", "T10", "Ws", "Rp000", "Rp100", "Rs01", "mod", "LN00", "Rp101",
+    "Rp001", "T11", "WL", "Rs10", "GR000", "WR_", "LN01", "T20", "Gz00", "GL000", "Rp110",
+    "Rp010", "GR001", "Gz01", "Rs11", "Wf", "LN10", "GL010", "GL001", "GR011", "GR100", "GR010",
+    "GL011", "Rp111", "Rp011", "GL100", "proj0", "Gz10", "LN11", "att00", "att01", "Gz11",
+    "att02", "att03", "GR101", "GL101", "T21", "GR111", "GL111", "GL110", "GR110", "bpa0", "bpb0",
+    "Bs00", "proj1", "Bd00", "Bp100", "Bp000", "att10", "att11", "att12", "Bs01", "att13", "BX00",
+    "Bd01", "bpa1", "Bp001", "Bp101", "BL00", "bpb1", "Bs10", "BX01", "Bd10", "Bp010", "Bp110",
+    "Bs11", "AR00", "AL00", "BL01", "zwo", "Bd11", "Bp011", "BX10", "Bp111", "AL01", "AR01",
+    "BX11", "Af00", "Af01", "BL10", "BL11", "AS10", "O1", "AS11", "AL10", "AR10", "zp0", "Af10",
+    "AL11", "AR11", "zp1a", "Af11", "zp1b", "Zp0y", "Zp0x", "Zp1x", "ctl1", "Zp1y", "ctl0", "ZA",
+    "ZB", "ZS", "zgL_", "zgR_", "O2",
 )
 NT = (((1,), (1,)), ((), ()))
 TN = (((0,), (0,)), ((), ()))

time: 161 us -> 164 us (1.019)
  Pallas kernels: 159 us -> 163 us
    pallas_call x1, Pallas kernels: 156 us -> 160 us  [whole_block(): pl.pallas_call(block_kernel, out_shape=(jax.ShapeDtypeStruct((2, 2, ROWS,...]
where the time goes in v8:
time: 164 us
  Pallas kernels  163 us (99%)
    pallas_call x1, Pallas kernels, whole_block(): pl.pallas_call(block_kernel, out_shape=(jax.ShapeDtypeStruct((2, 2, ROWS,...  160 us

profile of v8, /device:TPU:32, one launch (start us, length us, event | category | flops | bytes accessed | tf_op | source)
XLA Modules:
  0.0 163.7 jit_solution(913784530650084477)
XLA Ops:
  0.6 160.4 %whole_block.1 = (bf16[2,2,32,2048]{3,2,1,0:T(8,128)(2,1)}, bf16[4,2,32,768]{3,2,1,0:T(8,128)(2,1)}, f32[192,768]{1,0:T(8,128)}) custom-call(s32[2]{0:T(128)} %bitcast.24, s32[2]{0:T(128)} %bitcast.25, bf16[256,6144]{1,0:T(8,128)(2,1)} %mod_weight.1, bf16[4,2,32,768]{3,2,1,0:T(8,128)(2,1)} %bitcast.20, bf16[768,3072]{1,0:T(8,128)(2,1)} %zero_weight.1, ...), custom_call_target="tpu_custom_call" | custom-call | tf_op jit(solution)/shard_map/whole_block/pallas_call | solution.py:934
  161.0 2.5 %hand_over.1 = (bf16[2,32,2048]{2,1,0:T(8,128)(2,1)}, bf16[2,32,2048]{2,1,0:T(8,128)(2,1)}, bf16[4,2,32,768]{3,2,1,0:T(8,128)(2,1)}, f32[192,768]{1,0:T(8,128)}) custom-call(bf16[2,2,32,2048]{3,2,1,0:T(8,128)(2,1)} %get-tuple-element.11.attn, bf16[4,2,32,768]{3,2,1,0:T(8,128)(2,1)} %get-tuple-element.12.control, f32[192,768]{1,0:T(8,128)} %get-tuple-element.13.zero), custom_call_target="tpu_custom_call" | custom-call | tf_op jit(solution)/shard_map/hand_over/pallas_call | solution.py:1042

commit v9 on v6

--- a/solution.py
+++ b/solution.py
@@ -157,17 +157,17 @@
 
 
 ORDER = (
-    "res0", "res1", "Rs00", "T10", "Ws", "Rp000", "Rp100", "Rs01", "mod", "LN00", "Rp101",
-    "Rp001", "T11", "WL", "Rs10", "GR000", "WR_", "LN01", "zwo", "T20", "Gz00", "GL000", "Rp110",
-    "Rp010", "GR001", "Gz01", "Rs11", "Wf", "LN10", "GL010", "GL001", "GR011", "GR100", "GR010",
-    "GL011", "Rp111", "Rp011", "GL100", "proj0", "Gz10", "LN11", "att00", "att01", "Gz11",
-    "att02", "att03", "GR101", "GL101", "T21", "GR111", "GL111", "GL110", "GR110", "bpa0", "bpb0",
-    "Bs00", "proj1", "Bd00", "Bp100", "Bp000", "att10", "att11", "att12", "Bs01", "att13", "BX00",
-    "Bd01", "bpa1", "Bp001", "Bp101", "BL00", "bpb1", "Bs10", "BX01", "Bd10", "Bp010", "Bp110",
-    "Bs11", "AR00", "AL00", "BL01", "Bd11", "Bp011", "BX10", "Bp111", "AL01", "AR01", "BX11",
-    "Af00", "Af01", "BL10", "BL11", "AS10", "O1", "AS11", "AL10", "AR10", "zp0", "Af10", "AL11",
-    "AR11", "zp1a", "Af11", "zp1b", "Zp0y", "Zp0x", "Zp1x", "ctl1", "Zp1y", "ctl0", "ZA", "ZB",
-    "ZS", "zgL_", "zgR_", "O2",
+    "res0", "res1", "Rs00", "T11", "Rp100", "Rp000", "T10", "Rs01", "mod", "Ws", "LN00", "Rp001",
+    "Rp101", "Rs10", "zwo", "LN01", "Rp110", "Rp010", "WR_", "Gz00", "GR000", "Gz01", "Rs11",
+    "WL", "LN10", "T20", "GR010", "GL010", "GL001", "GL011", "GR011", "GR001", "Rp011", "Rp111",
+    "Wf", "GL000", "Gz10", "GR100", "proj0", "GL100", "GL101", "LN11", "GR101", "att00", "att01",
+    "Gz11", "att02", "GR110", "att03", "T21", "GL111", "GR111", "GL110", "bpa0", "bpb0", "Bs00",
+    "proj1", "Bd00", "Bp100", "Bp000", "att10", "att11", "Bs01", "att12", "BX00", "att13", "Bd01",
+    "Bp001", "Bp101", "BL00", "bpa1", "bpb1", "Bs10", "BX01", "Bd10", "Bp010", "Bp110", "AL00",
+    "AR00", "Bs11", "BL01", "Af00", "Bd11", "BX10", "Bp011", "Bp111", "AR01", "AL01", "BX11",
+    "Af01", "BL10", "BL11", "AS10", "zp0", "AS11", "AR10", "AL10", "ctl0", "O1", "Af10", "AL11",
+    "AR11", "zp1a", "Af11", "zp1b", "O2", "Zp0y", "Zp1y", "Zp0x", "Zp1x", "ZB", "ZA", "ZS",
+    "zgL_", "zgR_", "ctl1",
 )
 NT = (((1,), (1,)), ((), ()))
 TN = (((0,), (0,)), ((), ()))
@@ -404,9 +404,8 @@
         ]
 
     def text_first_hop(i):
-        if i == 0:
-            for copy in load_text:
-                copy.wait()
+        while load_text:
+            load_text.pop().wait()
 
         @pl.loop(1, 8)
         def _(k):

time: 163 us -> 155 us (0.951)
  Pallas kernels: 162 us -> 152 us
    pallas_call x1, Pallas kernels: 159 us -> 150 us  [whole_block(): pl.pallas_call(block_kernel, out_shape=(jax.ShapeDtypeStruct((2, 2, ROWS,...]
where the time goes in v9:
time: 155 us; the launch traced here: 153 us
  Pallas kernels  152 us (98%)
    pallas_call x1, Pallas kernels, whole_block(): pl.pallas_call(block_kernel, out_shape=(jax.ShapeDtypeStruct((2, 2, ROWS,...  150 us

profile of v9, /device:TPU:32, one launch (start us, length us, event | category | flops | bytes accessed | tf_op | source)
XLA Modules:
  0.0 153.2 jit_solution(3320679718333189375)
XLA Ops:
  0.6 149.9 %whole_block.1 = (bf16[2,2,32,2048]{3,2,1,0:T(8,128)(2,1)}, bf16[4,2,32,768]{3,2,1,0:T(8,128)(2,1)}, f32[192,768]{1,0:T(8,128)}) custom-call(s32[2]{0:T(128)} %bitcast.24, s32[2]{0:T(128)} %bitcast.25, bf16[256,6144]{1,0:T(8,128)(2,1)} %mod_weight.1, bf16[4,2,32,768]{3,2,1,0:T(8,128)(2,1)} %bitcast.20, bf16[768,3072]{1,0:T(8,128)(2,1)} %zero_weight.1, ...), custom_call_target="tpu_custom_call" | custom-call | tf_op jit(solution)/shard_map/whole_block/pallas_call | solution.py:949
  150.6 2.5 %hand_over.1 = (bf16[2,32,2048]{2,1,0:T(8,128)(2,1)}, bf16[2,32,2048]{2,1,0:T(8,128)(2,1)}, bf16[4,2,32,768]{3,2,1,0:T(8,128)(2,1)}, f32[192,768]{1,0:T(8,128)}) custom-call(bf16[2,2,32,2048]{3,2,1,0:T(8,128)(2,1)} %get-tuple-element.11.attn, bf16[4,2,32,768]{3,2,1,0:T(8,128)(2,1)} %get-tuple-element.12.control, f32[192,768]{1,0:T(8,128)} %get-tuple-element.13.zero), custom_call_target="tpu_custom_call" | custom-call | tf_op jit(solution)/shard_map/hand_over/pallas_call | solution.py:1057

commit v10 on v9

--- a/solution.py
+++ b/solution.py
@@ -166,8 +166,8 @@
     "Bp001", "Bp101", "BL00", "bpa1", "bpb1", "Bs10", "BX01", "Bd10", "Bp010", "Bp110", "AL00",
     "AR00", "Bs11", "BL01", "Af00", "Bd11", "BX10", "Bp011", "Bp111", "AR01", "AL01", "BX11",
     "Af01", "BL10", "BL11", "AS10", "zp0", "AS11", "AR10", "AL10", "ctl0", "O1", "Af10", "AL11",
-    "AR11", "zp1a", "Af11", "zp1b", "O2", "Zp0y", "Zp1y", "Zp0x", "Zp1x", "ZB", "ZA", "ZS",
-    "zgL_", "zgR_", "ctl1",
+    "AR11", "zp1a", "Af11", "zp1b", "O2", "Zp0y0", "Zp1y0", "Zp0x0", "Zp1x0", "Zp0y1", "Zp1y1",
+    "Zp0x1", "Zp1x1", "ZB", "ZA", "ZS", "zgL_", "zgR_", "ctl1",
 )
 NT = (((1,), (1,)), ((), ()))
 TN = (((0,), (0,)), ((), ()))
@@ -822,51 +822,62 @@
 
     cols_a, cols_b = pl.ds(0, 384), pl.ds(384, 384)
     quarter = lambda d: pl.ds(pl.multiple_of(d * 48, 16), 48)
-    round_x = Scatter4(
-        send,
-        lambda d, h: zsum.at[h, :, quarter(d), cols_a],
-        lambda h: zx_relay.at[h],
-        lambda h: zx_left.at[h],
-        lambda h: zx_right.at[h],
-        zx_sem,
-        p.d,
-        p.dl,
-        p.dr,
-        p.do,
-        to_d,
-    )
-    zero_y = Scatter4(
-        send,
-        lambda y, h: zsum.at[h, y, :, cols_b],
-        lambda h: zy_relay.at[h],
-        lambda h: zy_left.at[h],
-        lambda h: zy_right.at[h],
-        zy_sem,
-        p.y,
-        p.yl,
-        p.yr,
-        p.yo,
-        to_y,
-    )
+    round_x = [
+        Scatter4(
+            send,
+            lambda d, h, z=z: zsum.at[z, pl.ds(2 * h, 2), quarter(d), cols_a],
+            lambda h, z=z: zx_relay.at[z, pl.ds(2 * h, 2)],
+            lambda h, z=z: zx_left.at[z, pl.ds(2 * h, 2)],
+            lambda h, z=z: zx_right.at[z, pl.ds(2 * h, 2)],
+            zx_sem.at[z],
+            p.d,
+            p.dl,
+            p.dr,
+            p.do,
+            to_d,
+        )
+        for z in range(2)
+    ]
+    zero_y = [
+        Scatter4(
+            send,
+            lambda y, h, z=z: zsum.at[z, y, pl.ds(96 * h, 96), cols_b],
+            lambda h, z=z: zy_relay.at[z, pl.ds(96 * h, 96)],
+            lambda h, z=z: zy_left.at[z, pl.ds(96 * h, 96)],
+            lambda h, z=z: zy_right.at[z, pl.ds(96 * h, 96)],
+            zy_sem.at[z],
+            p.y,
+            p.yl,
+            p.yr,
+            p.yo,
+            to_y,
+        )
+        for z in range(2)
+    ]
+
     def zero_send(z):
         arrived(rows_in_at(1, z), rows_sem.at[2 + z])
         zero_part(1, 2 * z)
         zero_part(1, 2 * z + 1)
-        round_x.start(z)
-        zero_y.start(z)
-        round_x.direct(z)
-        zero_y.direct(z)
+        for h in range(2):
+            round_x[z].start(h)
+            zero_y[z].start(h)
+        for h in range(2):
+            round_x[z].direct(h)
+            zero_y[z].direct(h)
 
     step("zp1a", 0)(zero_send)
     step("zp1b", 1)(zero_send)
-    for h in range(2):
-        step(f"Zp{h}x", h)(round_x.pass_on)
-        step(f"Zp{h}y", h)(zero_y.pass_on)
+    for z in range(2):
+        for h in range(2):
+            step(f"Zp{h}x{z}", h)(round_x[z].pass_on)
+            step(f"Zp{h}y{z}", h)(zero_y[z].pass_on)
     others = [(dz, dy) for dz in range(2) for dy in range(4) if dz or dy]
 
     @step("ZA")
     def _():
-        round_x.finish()
+        for z in range(2):
+            round_x[z].finish()
         for z in range(2):
             za_out[z] = (
                 zsum[z, :, quarter(p.d), cols_a].astype(F32)
@@ -879,7 +890,8 @@
 
     @step("ZB")
     def _():
-        zero_y.finish()
+        for z in range(2):
+            zero_y[z].finish()
         for z in range(2):
             zb_out[z] = (
                 (
@@ -1022,8 +1034,8 @@
             dma((4,)),
             dma((2, 8)),
             dma((3,)),
-            dma((6,)),
-            dma((6,)),
+            dma((2, 6)),
+            dma((2, 6)),
             dma((7,)),
             dma((7,)),
             dma((4,)),

time: 155 us -> 152 us (0.981)
  Pallas kernels: 152 us -> 150 us
    pallas_call x1, Pallas kernels: 150 us -> 148 us  [whole_block(): pl.pallas_call(block_kernel, out_shape=(jax.ShapeDtypeStruct((2, 2, ROWS,...]
where the time goes in v10:
time: 152 us; the launch traced here: 151 us
  Pallas kernels  150 us (99%)
    pallas_call x1, Pallas kernels, whole_block(): pl.pallas_call(block_kernel, out_shape=(jax.ShapeDtypeStruct((2, 2, ROWS,...  148 us

profile of v10, /device:TPU:32, one launch (start us, length us, event | category | flops | bytes accessed | tf_op | source)
XLA Modules:
  0.0 150.9 jit_solution(3393570167877773504)
XLA Ops:
  0.6 147.6 %whole_block.1 = (bf16[2,2,32,2048]{3,2,1,0:T(8,128)(2,1)}, bf16[4,2,32,768]{3,2,1,0:T(8,128)(2,1)}, f32[192,768]{1,0:T(8,128)}) custom-call(s32[2]{0:T(128)} %bitcast.24, s32[2]{0:T(128)} %bitcast.25, bf16[256,6144]{1,0:T(8,128)(2,1)} %mod_weight.1, bf16[4,2,32,768]{3,2,1,0:T(8,128)(2,1)} %bitcast.20, bf16[768,3072]{1,0:T(8,128)(2,1)} %zero_weight.1, ...), custom_call_target="tpu_custom_call" | custom-call | tf_op jit(solution)/shard_map/whole_block/pallas_call | solution.py:961
  148.3 2.5 %hand_over.1 = (bf16[2,32,2048]{2,1,0:T(8,128)(2,1)}, bf16[2,32,2048]{2,1,0:T(8,128)(2,1)}, bf16[4,2,32,768]{3,2,1,0:T(8,128)(2,1)}, f32[192,768]{1,0:T(8,128)}) custom-call(bf16[2,2,32,2048]{3,2,1,0:T(8,128)(2,1)} %get-tuple-element.11.attn, bf16[4,2,32,768]{3,2,1,0:T(8,128)(2,1)} %get-tuple-element.12.control, f32[192,768]{1,0:T(8,128)} %get-tuple-element.13.zero), custom_call_target="tpu_custom_call" | custom-call | tf_op jit(solution)/shard_map/hand_over/pallas_call | solution.py:1069
